TPU v7x, 32 devices: a whole 2x2x4 slice. The times are simulated.
32 devices in a mesh: wide: 8 (over z, y), narrow: 4 (over x, core).
Axes of the slice: x: 2, y: 2, z: 4, core: 2. Of those that a mesh axis runs over, the one named last changes fastest.
Arguments:
- section_input: bfloat16 [16384, 256], P(('wide', 'narrow')), may hold values from -40 to 40
- mid_features: bfloat16 [16384, 256], P(('wide', 'narrow')), may hold values from -40 to 40
- out_grad: bfloat16 [16384, 256], P(('wide', 'narrow')), may hold values from -6 to 6
- to_hilbert: int32 [16384], P(('wide', 'narrow')), may hold values from 0 to 16383, as said below
- to_zorder: int32 [16384], P(('wide', 'narrow')), may hold values from 0 to 16383, as said below
- qkv_weight: bfloat16 [2, 256, 768], replicated, may hold values from -0.6 to 0.6
- out_weight: bfloat16 [2, 256, 256], replicated, may hold values from -0.75 to 0.75
Outputs:
- input_grad: bfloat16 [16384, 256], P(('wide', 'narrow'))
- qkv_weight_grad: float32 [2, 256, 768], replicated
- out_weight_grad: float32 [2, 256, 256], replicated
Inputs may be any that keep to these rules, and one draw needn't show every extreme that they name: to_hilbert is a permutation of the 16384 points. The devices form 8 aligned groups of 4 consecutive devices (octants of the scan); the points of one group in z-order are exactly the points of one group in Hilbert order, the pairing of groups drawn from the seed. Between a z-order device and a Hilbert-order device of paired groups at least 64 and at most 192 points move, the most reached in every draw; between unpaired groups none. to_zorder is the inverse permutation of to_hilbert.
All inputs are finite; a program needn't handle non-finite values.
Results may differ from a plain program's by a relative error of at most 0.011.
The roundings to bfloat16 on the way count: a program that leaves them out, or rounds other values in their place, can miss the bound.
Values may be sent and summed in bfloat16 or wider, within the bound.
No kernel may reach another device: no remote copies, remote signals or barrier semaphores. Data moves between devices by JAX's collectives and lax.ppermute only.
A program may use at most 64 MiB of HBM per device.

v0:
```python
from functools import partial

import jax
import jax.numpy as jnp
from jax import lax
from jax.sharding import PartitionSpec as P

HEADS = 16
PATCH = 512


def head_backward(inputs, score_scale):
    queries, key_rows, values, delta_out = inputs
    scores = jnp.dot(queries, key_rows.T, preferred_element_type=jnp.float32) * score_scale
    row_peak = jnp.max(scores, axis=-1, keepdims=True)
    powers = jnp.exp(scores - row_peak)
    weights = powers / jnp.sum(powers, axis=-1, keepdims=True)
    weights_half = weights.astype(jnp.bfloat16)
    attended = jnp.dot(weights_half, values, preferred_element_type=jnp.float32).astype(
        jnp.bfloat16
    )
    weight_grad = jnp.dot(delta_out, values.T, preferred_element_type=jnp.float32)
    centre = jnp.sum(weights * weight_grad, axis=-1, keepdims=True)
    score_grad = (weights * (weight_grad - centre) * score_scale).astype(jnp.bfloat16)
    query_grad = jnp.dot(score_grad, key_rows, preferred_element_type=jnp.float32)
    key_grad = jnp.dot(score_grad.T, queries, preferred_element_type=jnp.float32)
    value_grad = jnp.dot(weights_half.T, delta_out, preferred_element_type=jnp.float32)
    return (attended, jnp.stack([query_grad, key_grad, value_grad]).astype(jnp.bfloat16))


def patch_backward(features, gradients, qkv_w, out_w):
    rows_count, channels = features.shape
    head_size = channels // HEADS
    score_scale = head_size ** (-0.5)
    projected = jnp.dot(features, qkv_w, preferred_element_type=jnp.float32).astype(jnp.bfloat16)
    split_heads = projected.reshape(rows_count, 3, HEADS, head_size).transpose(1, 2, 0, 3)
    out_delta = jnp.dot(gradients, out_w.T, preferred_element_type=jnp.float32).astype(jnp.bfloat16)
    out_delta = out_delta.reshape(rows_count, HEADS, head_size).transpose(1, 0, 2)
    attended, qkv_delta = lax.map(
        partial(head_backward, score_scale=score_scale),
        (split_heads[0], split_heads[1], split_heads[2], out_delta),
    )
    mixed_heads = attended.transpose(1, 0, 2).reshape(rows_count, channels)
    qkv_flat = qkv_delta.transpose(2, 1, 0, 3).reshape(rows_count, 3 * channels)
    out_w_grad = jnp.dot(mixed_heads.T, gradients, preferred_element_type=jnp.float32)
    qkv_w_grad = jnp.dot(features.T, qkv_flat, preferred_element_type=jnp.float32)
    feature_grad = jnp.dot(qkv_flat, qkv_w.T, preferred_element_type=jnp.float32)
    return (feature_grad, qkv_w_grad, out_w_grad)


def layer_backward(features, gradients, qkv_w, out_w):
    rows_total, channels = features.shape
    feat_blocks = features.reshape(-1, PATCH, channels)
    grad_blocks = gradients.reshape(-1, PATCH, channels)

    def step_fn(running, inputs_pair):
        feature_grad, qkv_w_grad, out_w_grad = patch_backward(
            inputs_pair[0], inputs_pair[1], qkv_w, out_w
        )
        return ((running[0] + qkv_w_grad, running[1] + out_w_grad), feature_grad)

    zero_sums = (
        jnp.zeros((channels, 3 * channels), jnp.float32),
        jnp.zeros((channels, channels), jnp.float32),
    )
    totals, feature_grads = lax.scan(step_fn, zero_sums, (feat_blocks, grad_blocks))
    return (feature_grads.reshape(rows_total, channels), totals[0], totals[1])


def plan_route(targets, local_rows, devices_total, capacity):
    owners = targets // local_rows
    positions = targets % local_rows
    order = jnp.argsort(owners, stable=True)
    sorted_owner = owners[order]
    device_ids = jnp.arange(devices_total, dtype=jnp.int32)
    counts = jnp.sum((owners[:, None] == device_ids[None, :]).astype(jnp.int32), axis=0)
    before = jnp.sum(
        jnp.where(device_ids[None, :] < sorted_owner[:, None], counts[None, :], 0), axis=1
    )
    ranks = jnp.arange(local_rows, dtype=jnp.int32) - before
    slot_ids = sorted_owner * capacity + ranks
    index_buffer = (
        jnp.full((devices_total * capacity,), local_rows, jnp.int32)
        .at[slot_ids]
        .set(positions[order])
    )
    return (order, slot_ids, index_buffer)


def reorder(rows, route, wide_count, narrow_count, capacity):
    order, slot_ids, index_buffer = route
    local_rows, channels = rows.shape
    devices_total = wide_count * narrow_count
    packed = (
        jnp.zeros((devices_total * capacity, channels), rows.dtype).at[slot_ids].set(rows[order])
    )
    recv_rows, recv_index = (
        lax.all_to_all(
            packed.reshape(devices_total, capacity, channels),
            ("wide", "narrow"),
            split_axis=0,
            concat_axis=0,
            tiled=True,
        ),
        lax.all_to_all(
            index_buffer.reshape(devices_total, capacity),
            ("wide", "narrow"),
            split_axis=0,
            concat_axis=0,
            tiled=True,
        ),
    )
    placed = jnp.zeros((local_rows, channels), rows.dtype)
    return placed.at[recv_index.reshape(-1)].set(recv_rows.reshape(-1, channels), mode="drop")


def on_device(section_input, mid_features, out_grad, to_hilbert, to_zorder, qkv_weight, out_weight):
    wide_count = lax.axis_size("wide")
    narrow_count = lax.axis_size("narrow")
    devices_total = wide_count * narrow_count
    local_rows, channels = section_input.shape
    octant_devices = devices_total // 8
    base_share = local_rows // octant_devices
    capacity = base_share + 2 * (base_share // 4)
    forward_route = plan_route(to_zorder, local_rows, devices_total, capacity)
    backward_route = plan_route(to_hilbert, local_rows, devices_total, capacity)
    feats_hilbert = reorder(section_input, forward_route, wide_count, narrow_count, capacity)
    late_grad, late_qkv, late_out = layer_backward(
        mid_features, out_grad, qkv_weight[1], out_weight[1]
    )
    mid_grad = (out_grad.astype(jnp.float32) + late_grad).astype(jnp.bfloat16)
    grads_hilbert = reorder(mid_grad, forward_route, wide_count, narrow_count, capacity)
    early_grad, early_qkv, early_out = layer_backward(
        feats_hilbert, grads_hilbert, qkv_weight[0], out_weight[0]
    )
    returned = reorder(
        early_grad.astype(jnp.bfloat16), backward_route, wide_count, narrow_count, capacity
    )
    input_grad = (mid_grad.astype(jnp.float32) + returned.astype(jnp.float32)).astype(jnp.bfloat16)
    grad_scale = (local_rows * devices_total) ** (-0.5)
    qkv_sum, out_sum = lax.psum(
        (jnp.stack([early_qkv, late_qkv]), jnp.stack([early_out, late_out])), ("wide", "narrow")
    )
    return (input_grad, qkv_sum * grad_scale, out_sum * grad_scale)


def solution(mesh):
    placed = (
        P(("wide", "narrow"), None),
        P(("wide", "narrow"), None),
        P(("wide", "narrow"), None),
        P(("wide", "narrow")),
        P(("wide", "narrow")),
        P(),
        P(),
    )
    return jax.shard_map(
        on_device,
        mesh=mesh,
        in_specs=placed,
        out_specs=(P(("wide", "narrow"), None), P(), P()),
        check_vma=False,
    )
```

profile of v0, /device:TPU:0, one launch (start us, length us, event | category | flops | bytes accessed | tf_op | source)
XLA Modules:
  0.0 541.0 jit_solution(14376891628767215111)
XLA Ops:
  8.1 3.8 sort.32
  11.9 3.5 gather_fusion.2
  15.5 3.5 gather_fusion.3
  22.2 7.3 %all-to-all-start.1 = ((s32[32,1,192]{2,1,0:T(1,128)}), s32[32,1,192]{2,1,0:T(1,128)S(1)}, u32[]{:S(2)}, u32[]{:S(2)}) async-start(s32[32,1,192]{2,1,0:T(1,128)} %all_to_all.24), calls=%async_computation.1 | async-start | bytes 65536 | tf_op jit(solution)/shard_map/all_to_all | solution.py:105
  31.4 58.8 %while.44 = (s32[]{:T(128)}, bf16[16,512,16]{1,2,0:T(8,128)(2,1)S(1)}, bf16[16,3,512,16]{2,3,0,1:T(8,128)(2,1)S(1)}, bf16[16,512,16]{1,2,0:T(8,128)(2,1)S(1)}, b...) while((s32[]{:T(128)}, ...), condition=%wide.region_4.5_spmd, body=%wide.region_0.4_spmd.sunk | while | flops 55753216 | bytes 10286181 | solution.py:39
  90.6 6.1 %scatter_custom_fusion.4 = bf16[6144,256]{1,0:T(8,128)(2,1)} fusion(s32[512]{0:T(512)S(1)} %bitcast.260, bf16[]{:T(256)} %constant.110.clone.1, bf16[512,256]{1,0:T(8,128)(2,1)S(1)} %fusion.76, s32[1024]{0:T(1024)S(1)} %pad_clamp_fusion), kind=kCustom, calls=%fused_computation.102 | custom fusion | bytes 3145730 | tf_op jit(solution)/shard_map/scatter | solution.py:95
  96.7 6.0 %all-to-all-start.3 = ((bf16[32,192,256]{2,1,0:T(8,128)(2,1)}), bf16[32,192,256]{2,1,0:T(8,128)(2,1)S(1)}, u32[]{:S(2)}, u32[]{:S(2)}) async-start(bf16[32,192,256]{2,1,0:T(8,128)(2,1)} %bitcast.45), calls=%async_computation.3 | async-start | bytes 6291456 | tf_op jit(solution)/shard_map/all_to_all | solution.py:98
  102.8 6.0 %scatter_custom_fusion.2 = bf16[6144,256]{1,0:T(8,128)(2,1)} fusion(s32[512]{0:T(512)S(1)} %bitcast.261, bf16[]{:T(256)} %constant.110.clone.1, bf16[512,256]{1,0:T(8,128)(2,1)S(1)} %copy-done, s32[1024]{0:T(1024)S(1)} %pad_clamp_fusion), kind=kCustom, calls=%fused_computation.104 | custom fusion | bytes 3145730 | tf_op jit(solution)/shard_map/scatter | solution.py:95
  108.8 65.3 %all-to-all-done.3 = bf16[32,192,256]{2,1,0:T(8,128)(2,1)S(1)} async-done(((bf16[32,192,256]{2,1,0:T(8,128)(2,1)}), bf16[32,192,256]{2,1,0:T(8,128)(2,1)S(1)}, u32[]{:S(2)}, u32[]{:S(2)}) %all-to-all-start.3) | async-done | bytes 3145760 | tf_op jit(solution)/shard_map/all_to_all | solution.py:98
  174.1 4.0 all-to-all-start.2
  178.1 3.8 sort.31
  181.9 3.5 gather_fusion
  185.4 3.5 gather_fusion.1
  192.5 27.0 %scatter_custom_fusion.5 = bf16[512,256]{1,0:T(8,128)(2,1)} fusion(s32[6144]{0:T(1024)S(1)} %bitcast.251, bf16[6144,256]{1,0:T(8,128)(2,1)S(1)} %bitcast.239, bf16[]{:T(256)} %constant.110.clone.1), kind=kCustom, calls=%fused_computation.145 | custom fusion | bytes 262146 | tf_op jit(solution)/shard_map/scatter | solution.py:114
  220.8 28.8 %all-to-all-done.2 = bf16[32,192,256]{2,1,0:T(8,128)(2,1)} async-done(((bf16[32,192,256]{2,1,0:T(8,128)(2,1)}), bf16[32,192,256]{2,1,0:T(8,128)(2,1)}, u32[]{:S(2)}, u32[]{:S(2)}) %all-to-all-start.2) | async-done | bytes 3145760 | tf_op jit(solution)/shard_map/all_to_all | solution.py:98
  249.5 4.2 all-to-all-start
  253.7 26.6 %scatter_custom_fusion.3 = bf16[512,256]{1,0:T(8,128)(2,1)S(1)} fusion(s32[6144]{0:T(1024)S(1)} %bitcast.252, bf16[6144,256]{1,0:T(8,128)(2,1)} %bitcast.37, bf16[]{:T(256)} %constant.110.clone.1), kind=kCustom, calls=%fused_computation.147 | custom fusion | bytes 262656 | tf_op jit(solution)/shard_map/scatter | solution.py:114
  282.9 35.9 %while.45 = (s32[]{:T(128)}, bf16[16,512,16]{1,2,0:T(8,128)(2,1)S(1)}, bf16[16,3,512,16]{2,3,0,1:T(8,128)(2,1)S(1)}, bf16[16,512,16]{1,2,0:T(8,128)(2,1)S(1)}, b...) while((s32[]{:T(128)}, ...), condition=%wide.region_21.22_spmd, body=%wide.region_17.21_spmd.sunk | while | flops 55753216 | bytes 10286181 | solution.py:39
  319.2 6.0 %scatter_custom_fusion.6 = bf16[6144,256]{1,0:T(8,128)(2,1)} fusion(s32[512]{0:T(512)S(1)} %bitcast.258, bf16[]{:T(256)} %constant.110.clone.1, bf16[512,256]{1,0:T(8,128)(2,1)S(1)} %convolution_convert_fusion.10, s32[1024]{0:T(1024)S(1)} %pad_clamp_fusion.1), kind=kCustom, calls=%fused_computation.100 | custom fusion | bytes 3145730 | tf_op jit(solution)/shard_map/scatter | solution.py:95
  325.2 5.6 %all-to-all-start.4 = ((bf16[32,192,256]{2,1,0:T(8,128)(2,1)}), bf16[32,192,256]{2,1,0:T(8,128)(2,1)S(1)}, u32[]{:S(2)}, u32[]{:S(2)}) async-start(bf16[32,192,256]{2,1,0:T(8,128)(2,1)} %bitcast.52), calls=%async_computation.4 | async-start | bytes 6291456 | tf_op jit(solution)/shard_map/all_to_all | solution.py:98
  333.2 2.5 convolution_bitcast_fusion
  341.9 158.9 %all-reduce.3.cloned.1.call-done = (f32[2,256,768]{2,1,0:T(8,128)}, f32[2,256,256]{2,1,0:T(8,128)}) async-done(((f32[2,256,768]{2,1,0:T(8,128)}, f32[2,256,256]{2,1,0:T(8,128)}), (f32[2,256,768]{2,1,0:T(8,128)}, f32[2,256,256]{2,1,0:T(8,128)})) %all-reduce.3.cloned.1.call-update) | async-done | bytes 2097168 | tf_op jit(solution)/shard_map/psum | solution.py:141
  502.7 2.7 broadcast_multiply_fusion
  505.3 27.0 %scatter_custom_fusion.7 = bf16[512,256]{1,0:T(8,128)(2,1)} fusion(s32[6144]{0:T(1024)S(1)} %bitcast.250, bf16[6144,256]{1,0:T(8,128)(2,1)S(1)} %bitcast.238, bf16[]{:T(256)} %constant.110.clone.1), kind=kCustom, calls=%fused_computation.143 | custom fusion | bytes 262146 | tf_op jit(solution)/shard_map/scatter | solution.py:114
  (368 shorter events, 120.3 us)
Async XLA Ops:
  7.2 95.6 %copy-start = (bf16[512,256]{1,0:T(8,128)(2,1)S(1)}, bf16[512,256]{1,0:T(8,128)(2,1)}, u32[]{:S(2)}) copy-start(bf16[512,256]{1,0:T(8,128)(2,1)} %param.11) | copy-start | bytes 786436
  7.2 22.3 %copy-start.8 = (bf16[512,256]{1,0:T(8,128)(2,1)S(1)}, bf16[512,256]{1,0:T(8,128)(2,1)}, u32[]{:S(2)}) copy-start(bf16[512,256]{1,0:T(8,128)(2,1)} %param.12) | copy-start | bytes 786436
  7.2 22.3 %copy-start.9 = (bf16[2,256,768]{2,1,0:T(8,128)(2,1)S(1)}, bf16[2,256,768]{2,1,0:T(8,128)(2,1)}, u32[]{:S(2)}) copy-start(bf16[2,256,768]{2,1,0:T(8,128)(2,1)} %param.16) | copy-start | bytes 2359300
  15.5 15.5 %copy-start.5 = (bf16[512,256]{1,0:T(8,128)(2,1)S(1)}, bf16[512,256]{1,0:T(8,128)(2,1)}, u32[]{:S(2)}) copy-start(bf16[512,256]{1,0:T(8,128)(2,1)} %param.13) | copy-start | bytes 786436
  15.5 15.5 %copy-start.11 = (bf16[2,256,256]{2,1,0:T(8,128)(2,1)S(1)}, bf16[2,256,256]{2,1,0:T(8,128)(2,1)}, u32[]{:S(2)}) copy-start(bf16[2,256,256]{2,1,0:T(8,128)(2,1)} %param.17) | copy-start | bytes 786436
  22.2 74.5 %all-to-all-start.1 = ((s32[32,1,192]{2,1,0:T(1,128)}), s32[32,1,192]{2,1,0:T(1,128)S(1)}, u32[]{:S(2)}, u32[]{:S(2)}) async-start(s32[32,1,192]{2,1,0:T(1,128)} %all_to_all.24), calls=%async_computation.1 | async-start | bytes 65536 | tf_op jit(solution)/shard_map/all_to_all | solution.py:105
  90.2 6.5 %copy-start.2 = (bf16[16,3,512,16]{2,3,0,1:T(8,128)(2,1)}, bf16[16,3,512,16]{2,3,0,1:T(8,128)(2,1)S(1)}, u32[]{:S(2)}) copy-start(bf16[16,3,512,16]{2,3,0,1:T(8,128)(2,1)S(1)} %get-tuple-element.129) | copy-start | bytes 2359300
  90.2 6.5 %copy-start.6 = (bf16[16,512,16]{1,2,0:T(8,128)(2,1)}, bf16[16,512,16]{1,2,0:T(8,128)(2,1)S(1)}, u32[]{:S(2)}) copy-start(bf16[16,512,16]{1,2,0:T(8,128)(2,1)S(1)} %get-tuple-element.134) | copy-start | bytes 786436
  90.6 6.1 %copy-start.12 = (bf16[512,256]{1,0:T(8,128)(2,1)}, bf16[512,256]{1,0:T(8,128)(2,1)S(1)}, u32[]{:S(2)}) copy-start(bf16[512,256]{1,0:T(8,128)(2,1)S(1)} %fusion.76) | copy-start | bytes 786436
  96.7 77.4 %all-to-all-start.3 = ((bf16[32,192,256]{2,1,0:T(8,128)(2,1)}), bf16[32,192,256]{2,1,0:T(8,128)(2,1)S(1)}, u32[]{:S(2)}, u32[]{:S(2)}) async-start(bf16[32,192,256]{2,1,0:T(8,128)(2,1)} %bitcast.45), calls=%async_computation.3 | async-start | bytes 6291456 | tf_op jit(solution)/shard_map/all_to_all | solution.py:98
  174.1 4.0 copy-start.13
  174.1 75.4 %all-to-all-start.2 = ((bf16[32,192,256]{2,1,0:T(8,128)(2,1)}), bf16[32,192,256]{2,1,0:T(8,128)(2,1)}, u32[]{:S(2)}, u32[]{:S(2)}) async-start(bf16[32,192,256]{2,1,0:T(8,128)(2,1)} %bitcast.36), calls=%async_computation.2 | async-start | bytes 6291456 | tf_op jit(solution)/shard_map/all_to_all | solution.py:98
  249.5 75.7 %all-to-all-start = ((s32[32,1,192]{2,1,0:T(1,128)}), s32[32,1,192]{2,1,0:T(1,128)S(1)}, u32[]{:S(2)}, u32[]{:S(2)}) async-start(s32[32,1,192]{2,1,0:T(1,128)} %all_to_all.22), calls=%async_computation | async-start | bytes 65536 | tf_op jit(solution)/shard_map/all_to_all | solution.py:105
  280.3 0.7 copy-start.4
  282.9 35.9 %copy-start.10 = (bf16[2,256,768]{2,1,0:T(8,128)(2,1)S(1)}, bf16[2,256,768]{2,1,0:T(8,128)(2,1)}, u32[]{:S(2)}) copy-start(bf16[2,256,768]{2,1,0:T(8,128)(2,1)} %param.16) | copy-start | bytes 2359300
  318.8 6.5 %copy-start.3 = (bf16[16,3,512,16]{2,3,0,1:T(8,128)(2,1)}, bf16[16,3,512,16]{2,3,0,1:T(8,128)(2,1)S(1)}, u32[]{:S(2)}) copy-start(bf16[16,3,512,16]{2,3,0,1:T(8,128)(2,1)S(1)} %get-tuple-element.132) | copy-start | bytes 2359300
  318.8 6.5 %copy-start.7 = (bf16[16,512,16]{1,2,0:T(8,128)(2,1)}, bf16[16,512,16]{1,2,0:T(8,128)(2,1)S(1)}, u32[]{:S(2)}) copy-start(bf16[16,512,16]{1,2,0:T(8,128)(2,1)S(1)} %get-tuple-element.133) | copy-start | bytes 786436
  325.2 180.1 %all-to-all-start.4 = ((bf16[32,192,256]{2,1,0:T(8,128)(2,1)}), bf16[32,192,256]{2,1,0:T(8,128)(2,1)S(1)}, u32[]{:S(2)}, u32[]{:S(2)}) async-start(bf16[32,192,256]{2,1,0:T(8,128)(2,1)} %bitcast.52), calls=%async_computation.4 | async-start | bytes 6291456 | tf_op jit(solution)/shard_map/all_to_all | solution.py:98
  330.9 169.9 %all-reduce.3.cloned.1.call-start = ((), (), s32[]{:S(2)}) async-start(), calls=%async_computation.5 | async-start | bytes 4194304 | tf_op jit(solution)/shard_map/psum | solution.py:141
  335.8 4.8 copy-start.1
Sparse Core Ops, SparseCore 0:
  342.0 158.7 all-reduce.2
where the time goes:
time: 544 us; the launch traced here: 541 us
  waiting for transfers between devices  253 us (47%)
  local copies, waits for them, and re-layouts  122 us (22%)
  matrix products  89.5 us (16%)
  other arithmetic  34.3 us (6%)
  starting transfers between devices  27.4 us (5%)
  between operations  14.4 us (3%)
    psum x1, waiting for transfers between devices, on_device(): lax.psum((jnp.stack([early_qkv, late_qkv]), jnp.stack([early_out, late_ou...  159 us
    all_to_all x3, waiting for transfers between devices, reorder(): lax.all_to_all(packed.reshape(devices_total, capacity, channels), ('wide'...  94.1 us
    scatter x3, local copies, waits for them, and re-layouts, reorder(): placed.at[recv_index.reshape(-1)]  80.6 us
    dot_general x32, matrix products, head_backward(): jnp.dot(delta_out, values.T, preferred_element_type=jnp.float32)  23.4 us
    dot_general x32, matrix products, head_backward(): jnp.dot(weights_half, values, preferred_element_type=jnp.float32)  20.5 us
    scatter x3, local copies, waits for them, and re-layouts, reorder(): jnp.zeros((devices_total * capacity, channels), rows.dtype).at[slot_ids]  18.1 us
    all_to_all x3, starting transfers between devices, reorder(): lax.all_to_all(packed.reshape(devices_total, capacity, channels), ('wide'...  15.6 us
    all_to_all x2, starting transfers between devices, reorder(): lax.all_to_all(index_buffer.reshape(devices_total, capacity), ('wide', 'n...  11.5 us
  transfers between devices with their start and end apart: 6, of which 3 were waited for; matrix products, arithmetic and copies ran while one was open for 37% of the time, Pallas kernels for 0%

commit v1 on v0

v1 whole, which is shorter than its diff:
```python
from functools import partial

import jax
import jax.numpy as jnp
from jax import lax
from jax.experimental import pallas as pl
from jax.experimental.pallas import tpu as pltpu
from jax.sharding import PartitionSpec as P

HEADS = 16
LOG2E = 1.4426950408889634
f32, bf16 = jnp.float32, jnp.bfloat16
AXES = ("wide", "narrow")
VMEM_LIMIT = 48 * 2**20


def dg(a, b, contract_a, contract_b):
    return lax.dot_general(
        a, b, (((contract_a,), (contract_b,)), ((), ())), preferred_element_type=f32
    )


def whole(*_):
    return pl.BlockSpec(memory_space=pltpu.VMEM)


def scalar_spec():
    return pl.BlockSpec(memory_space=pltpu.SMEM)


def call(body, out_shape, n_in, scratch=(), flops=0):
    n_out = len(out_shape)
    return pl.pallas_call(
        body,
        out_shape=tuple(out_shape),
        in_specs=[scalar_spec()] + [whole()] * (n_in - 1),
        out_specs=tuple([whole()] * n_out),
        scratch_shapes=list(scratch),
        compiler_params=pltpu.CompilerParams(vmem_limit_bytes=VMEM_LIMIT),
        cost_estimate=pl.CostEstimate(flops=flops, bytes_accessed=2**20, transcendentals=0),
    )


def slot_matrix(slots, first, count):
    rows = slots.shape[1]
    at = lax.broadcasted_iota(jnp.int32, (count, rows), 0) + first
    return (at == slots).astype(f32).astype(bf16)


def route_kernel(group, cap, me_ref, tz_ref, rows_ref, slots_ref, *send_refs):
    n, channels = rows_ref.shape
    here = me_ref[0] % group
    target = tz_ref[...]
    partner = (target // n % group) ^ here
    spot = target % n
    lanes = max(16, group)
    which = lax.broadcasted_iota(jnp.int32, (lanes, n), 0)
    mine = (which == partner).astype(f32)
    earlier = (
        lax.broadcasted_iota(jnp.int32, (n, n), 0) < lax.broadcasted_iota(jnp.int32, (n, n), 1)
    ).astype(f32).astype(bf16)
    before = dg(mine.astype(bf16), earlier, 1, 0)
    rank = jnp.sum(mine * before, axis=0, keepdims=True).astype(jnp.int32)
    slots = partner * cap + rank
    slots_ref[...] = slots
    row_at = lax.broadcasted_iota(jnp.int32, (16, n), 0)
    info = jnp.where(
        row_at == 0, spot % 256, jnp.where(row_at == 1, spot // 256, (row_at == 2).astype(jnp.int32))
    ).astype(f32).astype(bf16)
    rows = rows_ref[...]
    for s in range(group):
        chosen = slot_matrix(slots, s * cap, cap)
        send_refs[s][0:cap, :] = dg(chosen, rows, 1, 0).astype(bf16)
        where = dg(info, chosen, 1, 1)
        if cap < channels:
            where = jnp.concatenate([where, jnp.zeros((16, channels - cap), f32)], axis=1)
        send_refs[s][cap : cap + 16, :] = where.astype(bf16)


def spots_of(recv_ref, cap):
    info = recv_ref[cap : cap + 16, 0:cap].astype(f32)
    spot = info[0:1] + 256.0 * info[1:2] + 1024.0 * (info[2:3] - 1.0)
    return spot.astype(jnp.int32)


def place_matrix(spot, n):
    at = lax.broadcasted_iota(jnp.int32, (n, spot.shape[1]), 0)
    return (at == spot).astype(f32).astype(bf16)


def one_head(proj, delta, head, n, channels, size):
    at = pl.multiple_of(head * size, size)
    q = proj[pl.ds(at, size), :]
    k = proj[pl.ds(channels + at, size), :]
    v = proj[pl.ds(2 * channels + at, size), :]
    o = proj[pl.ds(3 * channels + at, size), :]
    score_scale = size**-0.5
    scores = dg(k, q, 0, 0)
    peak = jnp.max(scores, axis=0, keepdims=True)
    powers = jnp.exp2((scores - peak) * (score_scale * LOG2E))
    weights = powers * (1.0 / jnp.sum(powers, axis=0, keepdims=True))
    half = weights.astype(bf16)
    weight_grad = dg(v, o, 0, 0)
    centre = jnp.sum(weights * weight_grad, axis=0, keepdims=True)
    score_grad = (weights * (weight_grad - centre)).astype(bf16)
    delta[pl.ds(at, size), :] = (dg(k, score_grad, 1, 0) * score_scale).astype(bf16)
    delta[pl.ds(channels + at, size), :] = (dg(q, score_grad, 1, 1) * score_scale).astype(bf16)
    delta[pl.ds(2 * channels + at, size), :] = dg(o, half, 1, 1).astype(bf16)
    delta[pl.ds(3 * channels + at, size), :] = dg(v, half, 1, 0).astype(bf16)


def layer(me, h, g, qkv_w, out_w, proj, delta, sums_ref):
    n, channels = h.shape
    size = channels // HEADS
    proj[0 : 3 * channels, :] = dg(qkv_w, h, 0, 1).astype(bf16)
    proj[3 * channels : 4 * channels, :] = dg(out_w, g, 1, 1).astype(bf16)

    def step(head, carry):
        one_head(proj, delta, head, n, channels, size)
        return carry

    lax.fori_loop(0, HEADS, step, 0)
    qkv_delta = delta[0 : 3 * channels, :]
    qkv_grad = dg(h.T, qkv_delta, 1, 1)
    out_grad = dg(delta[3 * channels : 4 * channels, :], g, 1, 0)
    chunks, rows, _ = sums_ref.shape
    per = channels // rows
    for c in range(chunks):
        part, start = c // per, (c % per) * rows
        if part < 3:
            piece = qkv_grad[start : start + rows, part * channels : (part + 1) * channels]
        else:
            piece = out_grad[start : start + rows, :]
        sums_ref[c ^ me] = piece.astype(bf16)
    return dg(qkv_w, qkv_delta, 1, 0).T


def late_kernel(group, cap, me_ref, h_ref, g_ref, qkv_ref, out_ref, slots_ref, *rest):
    mid_ref, sums_ref = rest[0], rest[1]
    send_refs = rest[2 : 2 + group]
    proj, delta = rest[2 + group :]
    g = g_ref[...]
    row_grad = layer(me_ref[0], h_ref[...], g, qkv_ref[1], out_ref[1], proj, delta, sums_ref)
    mid = (g.astype(f32) + row_grad).astype(bf16)
    mid_ref[...] = mid
    slots = slots_ref[...]
    for s in range(group):
        send_refs[s][...] = dg(slot_matrix(slots, s * cap, cap), mid, 1, 0).astype(bf16)


def early_kernel(group, cap, me_ref, qkv_ref, out_ref, *rest):
    feats_refs = rest[0:group]
    grads_refs = rest[group : 2 * group]
    sums_ref = rest[2 * group]
    send_refs = rest[2 * group + 1 : 3 * group + 1]
    proj, delta = rest[3 * group + 1 :]
    n, channels = proj.shape[1], feats_refs[0].shape[1]
    h = jnp.zeros((n, channels), f32)
    g = jnp.zeros((n, channels), f32)
    spots = []
    for s in range(group):
        spot = spots_of(feats_refs[s], cap)
        spots.append(spot)
        place = place_matrix(spot, n)
        h = h + dg(place, feats_refs[s][0:cap, :], 1, 0)
        g = g + dg(place, grads_refs[s][...], 1, 0)
    h, g = h.astype(bf16), g.astype(bf16)
    row_grad = layer(me_ref[0], h, g, qkv_ref[0], out_ref[0], proj, delta, sums_ref)
    early = row_grad.astype(bf16)
    for s in range(group):
        send_refs[s][...] = dg(place_matrix(spots[s], n), early, 0, 0).astype(bf16)


def join_kernel(group, cap, me_ref, slots_ref, mid_ref, *rest):
    back_refs, input_ref = rest[:group], rest[group]
    slots = slots_ref[...]
    total = jnp.zeros(mid_ref.shape, f32)
    for s in range(group):
        total = total + dg(slot_matrix(slots, s * cap, cap), back_refs[s][...], 0, 0)
    input_ref[...] = (mid_ref[...].astype(f32) + total.astype(bf16).astype(f32)).astype(bf16)


def finish_kernel(scale, me_ref, early_ref, late_ref, qkv_ref, out_ref):
    me = me_ref[0]
    chunks, rows, channels = early_ref.shape
    per = channels // rows
    for l, ref in enumerate((early_ref, late_ref)):
        for c in range(chunks):
            part, start = c // per, (c % per) * rows
            piece = ref[c ^ me].astype(f32) * scale
            if part < 3:
                qkv_ref[l, start : start + rows, part * channels : (part + 1) * channels] = piece
            else:
                out_ref[l, start : start + rows, :] = piece


def swap(x, mask, devices):
    return lax.ppermute(x, AXES, [(d, d ^ mask) for d in range(devices)])


def exchange(blocks, devices):
    return [blocks[0]] + [swap(blocks[s], s, devices) for s in range(1, len(blocks))]


def stage_masks(bits):
    masks = [0]
    for b in bits:
        masks = masks + [m | (1 << b) for m in masks]
    return masks


def sum_everywhere(x, stages, devices):
    tail = x.shape[1:]
    live = list(range(len(stages)))
    for bits in stages:
        masks = stage_masks(bits)
        parts = x.reshape((len(masks), -1) + tail)
        got = [parts[0]] + [swap(parts[i], masks[i], devices) for i in range(1, len(masks))]
        x = sum(p.astype(f32) for p in got).astype(bf16)
    for bits in reversed(stages):
        masks = stage_masks(bits)
        got = [x] + [swap(x, m, devices) for m in masks[1:]]
        x = jnp.concatenate(got, axis=0)
    return x


def plan_stages(mesh_shape, core_first):
    return core_first


def on_device(stages, section_input, mid_features, out_grad, to_hilbert, to_zorder, qkv_weight, out_weight):
    devices = lax.axis_size("wide") * lax.axis_size("narrow")
    n, channels = section_input.shape
    group = devices // 8
    share = n // group
    cap = share + 2 * (share // 4)
    rank = lax.axis_index("wide") * lax.axis_size("narrow") + lax.axis_index("narrow")
    me = rank.astype(jnp.int32).reshape(1)
    order = [b for bits in stages for b in reversed(bits)]
    total_bits = len(order)
    place = jnp.int32(0)
    for i, b in enumerate(order):
        place = place | (((rank >> b) & 1) << (total_bits - 1 - i))
    place = place.astype(jnp.int32).reshape(1)

    rows_s = jax.ShapeDtypeStruct((n, channels), bf16)
    send_s = jax.ShapeDtypeStruct((cap, channels), bf16)
    chunk_rows = 4 * channels // devices
    sums_s = jax.ShapeDtypeStruct((devices, chunk_rows, channels), bf16)
    scratch = [pltpu.VMEM((4 * channels, n), bf16), pltpu.VMEM((4 * channels, n), bf16)]

    slots, *feats = call(
        partial(route_kernel, group, cap),
        [jax.ShapeDtypeStruct((1, n), jnp.int32)]
        + [jax.ShapeDtypeStruct((cap + 16, channels), bf16)] * group,
        3,
        flops=10**9,
    )(me, to_zorder.reshape(1, n), section_input)
    feats = exchange(feats, devices)
    mid, late_sums, *grads = call(
        partial(late_kernel, group, cap),
        [rows_s, sums_s] + [send_s] * group,
        6,
        scratch,
        flops=2 * 10**10,
    )(place, mid_features, out_grad, qkv_weight, out_weight, slots)
    grads = exchange(grads, devices)
    early_sums, *backs = call(
        partial(early_kernel, group, cap),
        [sums_s] + [send_s] * group,
        3 + 2 * group,
        scratch,
        flops=2 * 10**10,
    )(place, qkv_weight, out_weight, *feats, *grads)
    backs = exchange(backs, devices)
    late_total = sum_everywhere(late_sums, stages, devices)
    early_total = sum_everywhere(early_sums, stages, devices)
    (input_grad,) = call(partial(join_kernel, group, cap), [rows_s], 3 + group, flops=10**9)(
        me, slots, mid, *backs
    )
    qkv_grad, out_w_grad = call(
        partial(finish_kernel, float((n * devices) ** -0.5)),
        [jax.ShapeDtypeStruct(qkv_weight.shape, f32), jax.ShapeDtypeStruct(out_weight.shape, f32)],
        3,
        flops=10**8,
    )(place, early_total, late_total)
    return (input_grad, qkv_grad, out_w_grad)


def solution(mesh):
    devices = mesh.size
    bits = devices.bit_length() - 1
    stages = [(0,)] + [tuple(range(b, min(b + 2, bits))) for b in range(1, bits, 2)]
    placed = (
        P(AXES, None),
        P(AXES, None),
        P(AXES, None),
        P(AXES),
        P(AXES),
        P(),
        P(),
    )
    return jax.shard_map(
        partial(on_device, stages),
        mesh=mesh,
        in_specs=placed,
        out_specs=(P(AXES, None), P(), P()),
        check_vma=False,
    )
```

time: 544 us -> 124 us (0.23)
  waiting for transfers between devices: 253 us -> 31.9 us
  local copies, waits for them, and re-layouts: 122 us -> 2.4 us
  matrix products: 89.5 us -> 0 us
  Pallas kernels: 0 us -> 49.7 us
  other arithmetic: 34.3 us -> 0.3 us
  between operations: 14.4 us -> 0.93 us
  starting transfers between devices: 27.4 us -> 39 us
    psum x1 -> x0, waiting for transfers between devices: 159 us -> none  [on_device(): lax.psum((jnp.stack([early_qkv, late_qkv]), jnp.stack([early_out, late_ou...]
    scatter x8 -> x0, local copies, waits for them, and re-layouts: 104 us -> none  [the longest x3 80.6 us: reorder(): placed.at[recv_index.reshape(-1)]]
    all_to_all x5 -> x0, waiting for transfers between devices: 94.1 us -> none  [the longest x3 94.1 us: reorder(): lax.all_to_all(packed.reshape(devices_total, capacity, channels), ('wide'...]
    dot_general x202 -> x0, matrix products: 89.5 us -> none  [the longest x32 23.4 us: head_backward(): jnp.dot(delta_out, values.T, preferred_element_type=jnp.float32)]
    pallas_call x0 -> x5, Pallas kernels: none -> 49.7 us  [the longest x1 23.4 us: on_device(): call(partial(early_kernel, group, cap), [sums_s] + [send_s] * group, 3 +...]
    ppermute x0 -> x37, starting transfers between devices: none -> 39 us  [swap(): return lax.ppermute(x, AXES, [(d, d ^ mask) for d in range(devices)])]
    ppermute x0 -> x37, waiting for transfers between devices: none -> 31.9 us  [swap(): return lax.ppermute(x, AXES, [(d, d ^ mask) for d in range(devices)])]
    all_to_all x5 -> x0, starting transfers between devices: 27.1 us -> none  [the longest x3 15.6 us: reorder(): lax.all_to_all(packed.reshape(devices_total, capacity, channels), ('wide'...]
  transfers between devices with their start and end apart: 6 -> 37, of which waited for: 3 -> 18; matrix products, arithmetic and copies ran while one was open for 37% -> 0% of each run, Pallas kernels for 0% -> 20%
where the time goes in v1:
time: 124 us
  Pallas kernels  49.7 us (40%)
  starting transfers between devices  39 us (31%)
  waiting for transfers between devices  31.9 us (26%)
  local copies, waits for them, and re-layouts  2.4 us (2%)
    ppermute x37, starting transfers between devices, swap(): return lax.ppermute(x, AXES, [(d, d ^ mask) for d in range(devices)])  39 us
    ppermute x37, waiting for transfers between devices, swap(): return lax.ppermute(x, AXES, [(d, d ^ mask) for d in range(devices)])  31.9 us
    pallas_call x1, Pallas kernels, on_device(): call(partial(early_kernel, group, cap), [sums_s] + [send_s] * group, 3 +...  23.4 us
    pallas_call x1, Pallas kernels, on_device(): call(partial(late_kernel, group, cap), [rows_s, sums_s] + [send_s] * grou...  22.8 us
  transfers between devices with their start and end apart: 37, of which 18 were waited for; matrix products, arithmetic and copies ran while one was open for 0% of the time, Pallas kernels for 20%

profile of v1, /device:TPU:0, one launch (start us, length us, event | category | flops | bytes accessed | tf_op | source)
XLA Modules:
  0.0 124.2 jit_solution(1329072173974846517)
XLA Ops:
  3.6 22.8 %shard_map.86 = (bf16[512,256]{1,0:T(8,128)(2,1)S(1)}, bf16[32,32,256]{2,1,0:T(8,128)(2,1)S(1)}, bf16[192,256]{1,0:T(8,128)(2,1)S(1)}, bf16[192,256]{1,0:T(8,128...) custom-call(s32[1]{0:T(128)} %bitcast.2.me_ref, bf16[512,256]{1,0:T(8,128)(2,1)S(1)} %copy-done.2, ...), custom_call_target="tpu_custom_call" | custom-call | flops 20000000000 | bytes 1048576 | tf_op jit(solution)/shard_map/pallas_call | solution.py:260
  28.3 2.9 %collective-permute-start.24 = (bf16[4,32,256]{2,1,0:T(8,128)(2,1)S(1)}, bf16[4,32,256]{2,1,0:T(8,128)(2,1)S(1)}, u32[]{:S(2)}, u32[]{:S(2)}) collective-permute-start(bf16[4,32,256]{2,1,0:T(8,128)(2,1)S(1)} %get-tuple-element.43), channel_id=1, source_target_pairs={{0,2},{1,3},{2,0},{3,1},{4,6},{5,7},{6,4},{7,5},{8,10},{9,11},{10,... | collective-permute-start | bytes 196616 | tf_op jit(solution)/shard_map/ppermute | solution.py:198
  31.2 1.5 %collective-permute-start.26 = (bf16[4,32,256]{2,1,0:T(8,128)(2,1)S(1)}, bf16[4,32,256]{2,1,0:T(8,128)(2,1)S(1)}, u32[]{:S(2)}, u32[]{:S(2)}) collective-permute-start(bf16[4,32,256]{2,1,0:T(8,128)(2,1)S(1)} %get-tuple-element.44), channel_id=1, source_target_pairs={{0,6},{1,7},{2,4},{3,5},{4,2},{5,3},{6,0},{7,1},{8,14},{9,15},{10,... | collective-permute-start | bytes 196616 | tf_op jit(solution)/shard_map/ppermute | solution.py:198
  32.8 1.9 %collective-permute-start.1 = (bf16[208,256]{1,0:T(8,128)(2,1)S(1)}, bf16[208,256]{1,0:T(8,128)(2,1)S(1)}, u32[]{:S(2)}, u32[]{:S(2)}) collective-permute-start(bf16[208,256]{1,0:T(8,128)(2,1)S(1)} %get-tuple-element.25), channel_id=1, source_target_pairs={{0,2},{1,3},{2,0},{3,1},{4,6},{5,7},{6,4},{7,5},{8,10},{9,11},{10,... | collective-permute-start | bytes 319496 | tf_op jit(solution)/shard_map/ppermute | solution.py:198
  34.9 1.6 %collective-permute-done.26 = bf16[4,32,256]{2,1,0:T(8,128)(2,1)S(1)} collective-permute-done((bf16[4,32,256]{2,1,0:T(8,128)(2,1)S(1)}, bf16[4,32,256]{2,1,0:T(8,128)(2,1)S(1)}, u32[]{:S(2)}, u32[]{:S(2)}) %collective-permute-start.26) | collective-permute-done | bytes 65568 | tf_op jit(solution)/shard_map/ppermute | solution.py:198
  38.9 4.6 %collective-permute-done.4.rest_6_ = bf16[192,256]{1,0:T(8,128)(2,1)S(1)} collective-permute-done((bf16[192,256]{1,0:T(8,128)(2,1)S(1)}, bf16[192,256]{1,0:T(8,128)(2,1)S(1)}, u32[]{:S(2)}, u32[]{:S(2)}) %collective-permute-start.4) | collective-permute-done | bytes 98336 | tf_op jit(solution)/shard_map/ppermute | solution.py:198
  43.5 1.6 %collective-permute-start.27 = (bf16[1,32,256]{2,1,0:T(8,128)(2,1)S(1)}, bf16[1,32,256]{2,1,0:T(8,128)(2,1)S(1)}, u32[]{:S(2)}, u32[]{:S(2)}) collective-permute-start(bf16[1,32,256]{2,1,0:T(8,128)(2,1)S(1)} %get-tuple-element.55), channel_id=1, source_target_pairs={{0,8},{1,9},{2,10},{3,11},{4,12},{5,13},{6,14},{7,15},{8,0},{9,1},... | collective-permute-start | bytes 49160 | tf_op jit(solution)/shard_map/ppermute | solution.py:198
  45.0 3.5 %collective-permute-start.29 = (bf16[1,32,256]{2,1,0:T(8,128)(2,1)S(1)}, bf16[1,32,256]{2,1,0:T(8,128)(2,1)S(1)}, u32[]{:S(2)}, u32[]{:S(2)}) collective-permute-start(bf16[1,32,256]{2,1,0:T(8,128)(2,1)S(1)} %get-tuple-element.56), channel_id=1, source_target_pairs={{0,24},{1,25},{2,26},{3,27},{4,28},{5,29},{6,30},{7,31},{8,16},{9,... | collective-permute-start | bytes 49160 | tf_op jit(solution)/shard_map/ppermute | solution.py:198
  48.6 23.4 %shard_map.87 = (bf16[32,32,256]{2,1,0:T(8,128)(2,1)S(1)}, bf16[192,256]{1,0:T(8,128)(2,1)S(1)}, bf16[192,256]{1,0:T(8,128)(2,1)S(1)}, bf16[192,256]{1,0:T(8,128)(2,1)S(1)}, bf16[192,256]{1,0:T(8,128)(2,1)S(1)}) custom-call(s32[1]{0:T(128)} %bitcast.2.me_ref, bf16[2,256,768]{2,1,0:T(8,128)(2,1)S(1)} %copy-done, bf16[2,256,256]{2,1,0:T(8,128)(2,1)S(1)} %copy-done.4, ...), custom_call_target="tpu_custom_call" | custom-call | flops 20000000000 | bytes 1048576 | tf_op jit(solution)/shard_map/pallas_call | solution.py:268
  73.5 2.2 %collective-permute-start.32 = (bf16[1,32,256]{2,1,0:T(8,128)(2,1)S(1)}, bf16[1,32,256]{2,1,0:T(8,128)(2,1)S(1)}, u32[]{:S(2)}, u32[]{:S(2)}) collective-permute-start(bf16[1,32,256]{2,1,0:T(8,128)(2,1)S(1)} %get-tuple-element.40), channel_id=1, source_target_pairs={{0,24},{1,25},{2,26},{3,27},{4,28},{5,29},{6,30},{7,31},{8,16},{9,... | collective-permute-start | bytes 49160 | tf_op jit(solution)/shard_map/ppermute | solution.py:198
  80.5 1.6 %collective-permute-start.34 = (bf16[4,32,256]{2,1,0:T(8,128)(2,1)S(1)}, bf16[4,32,256]{2,1,0:T(8,128)(2,1)S(1)}, u32[]{:S(2)}, u32[]{:S(2)}) collective-permute-start(bf16[4,32,256]{2,1,0:T(8,128)(2,1)S(1)} %pad_maximum_fusion.1), channel_id=1, source_target_pairs={{0,4},{1,5},{2,6},{3,7},{4,0},{5,1},{6,2},{7,3},{8,12},{9,13},{10,... | collective-permute-start | bytes 196616 | tf_op jit(solution)/shard_map/ppermute | solution.py:198
  82.7 1.6 %collective-permute-start.10 = (bf16[4,32,256]{2,1,0:T(8,128)(2,1)S(1)}, bf16[4,32,256]{2,1,0:T(8,128)(2,1)S(1)}, u32[]{:S(2)}, u32[]{:S(2)}) collective-permute-start(bf16[4,32,256]{2,1,0:T(8,128)(2,1)S(1)} %get-tuple-element.46), channel_id=1, source_target_pairs={{0,2},{1,3},{2,0},{3,1},{4,6},{5,7},{6,4},{7,5},{8,10},{9,11},{10,... | collective-permute-start | bytes 196616 | tf_op jit(solution)/shard_map/ppermute | solution.py:198
  84.3 2.0 %collective-permute-done.33 = bf16[4,32,256]{2,1,0:T(8,128)(2,1)S(1)} collective-permute-done((bf16[4,32,256]{2,1,0:T(8,128)(2,1)S(1)}, bf16[4,32,256]{2,1,0:T(8,128)(2,1)S(1)}, u32[]{:S(2)}, u32[]{:S(2)}) %collective-permute-start.33) | collective-permute-done | bytes 65568 | tf_op jit(solution)/shard_map/ppermute | solution.py:198
  87.0 1.5 %collective-permute-start.11 = (bf16[4,32,256]{2,1,0:T(8,128)(2,1)S(1)}, bf16[4,32,256]{2,1,0:T(8,128)(2,1)S(1)}, u32[]{:S(2)}, u32[]{:S(2)}) collective-permute-start(bf16[4,32,256]{2,1,0:T(8,128)(2,1)S(1)} %get-tuple-element.48), channel_id=1, source_target_pairs={{0,4},{1,5},{2,6},{3,7},{4,0},{5,1},{6,2},{7,3},{8,12},{9,13},{10,... | collective-permute-start | bytes 196616 | tf_op jit(solution)/shard_map/ppermute | solution.py:198
  88.4 1.5 %collective-permute-start.35 = (bf16[4,32,256]{2,1,0:T(8,128)(2,1)S(1)}, bf16[4,32,256]{2,1,0:T(8,128)(2,1)S(1)}, u32[]{:S(2)}, u32[]{:S(2)}) collective-permute-start(bf16[4,32,256]{2,1,0:T(8,128)(2,1)S(1)} %pad_maximum_fusion.1), channel_id=1, source_target_pairs={{0,6},{1,7},{2,4},{3,5},{4,2},{5,3},{6,0},{7,1},{8,14},{9,15},{10,... | collective-permute-start | bytes 196616 | tf_op jit(solution)/shard_map/ppermute | solution.py:198
  89.9 1.7 %collective-permute-done.12 = bf16[4,32,256]{2,1,0:T(8,128)(2,1)S(1)} collective-permute-done((bf16[4,32,256]{2,1,0:T(8,128)(2,1)S(1)}, bf16[4,32,256]{2,1,0:T(8,128)(2,1)S(1)}, u32[]{:S(2)}, u32[]{:S(2)}) %collective-permute-start.12) | collective-permute-done | bytes 65568 | tf_op jit(solution)/shard_map/ppermute | solution.py:198
  93.4 1.9 %collective-permute-start.15 = (bf16[1,32,256]{2,1,0:T(8,128)(2,1)S(1)}, bf16[1,32,256]{2,1,0:T(8,128)(2,1)S(1)}, u32[]{:S(2)}, u32[]{:S(2)}) collective-permute-start(bf16[1,32,256]{2,1,0:T(8,128)(2,1)S(1)} %get-tuple-element.65), channel_id=1, source_target_pairs={{0,24},{1,25},{2,26},{3,27},{4,28},{5,29},{6,30},{7,31},{8,16},{9,... | collective-permute-start | bytes 49160 | tf_op jit(solution)/shard_map/ppermute | solution.py:198
  95.9 3.2 %collective-permute-done.15 = bf16[1,32,256]{2,1,0:T(8,128)(2,1)S(1)} collective-permute-done((bf16[1,32,256]{2,1,0:T(8,128)(2,1)S(1)}, bf16[1,32,256]{2,1,0:T(8,128)(2,1)S(1)}, u32[]{:S(2)}, u32[]{:S(2)}) %collective-permute-start.15) | collective-permute-done | bytes 16416 | tf_op jit(solution)/shard_map/ppermute | solution.py:198
  100.2 1.8 %collective-permute-start.18 = (bf16[1,32,256]{2,1,0:T(8,128)(2,1)S(1)}, bf16[1,32,256]{2,1,0:T(8,128)(2,1)S(1)}, u32[]{:S(2)}, u32[]{:S(2)}) collective-permute-start(bf16[1,32,256]{2,1,0:T(8,128)(2,1)S(1)} %get-tuple-element.42), channel_id=1, source_target_pairs={{0,24},{1,25},{2,26},{3,27},{4,28},{5,29},{6,30},{7,31},{8,16},{9,... | collective-permute-start | bytes 49160 | tf_op jit(solution)/shard_map/ppermute | solution.py:198
  102.3 2.4 %collective-permute-start.16 = (bf16[1,32,256]{2,1,0:T(8,128)(2,1)S(1)}, bf16[1,32,256]{2,1,0:T(8,128)(2,1)S(1)}, u32[]{:S(2)}, u32[]{:S(2)}) collective-permute-start(bf16[1,32,256]{2,1,0:T(8,128)(2,1)S(1)} %get-tuple-element.42), channel_id=1, source_target_pairs={{0,8},{1,9},{2,10},{3,11},{4,12},{5,13},{6,14},{7,15},{8,0},{9,1},... | collective-permute-start | bytes 49160 | tf_op jit(solution)/shard_map/ppermute | solution.py:198
  108.1 3.6 %collective-permute-done.19 = bf16[4,32,256]{2,1,0:T(8,128)(2,1)S(1)} collective-permute-done((bf16[4,32,256]{2,1,0:T(8,128)(2,1)S(1)}, bf16[4,32,256]{2,1,0:T(8,128)(2,1)S(1)}, u32[]{:S(2)}, u32[]{:S(2)}) %collective-permute-start.19) | collective-permute-done | bytes 65568 | tf_op jit(solution)/shard_map/ppermute | solution.py:198
  113.1 2.8 %collective-permute-done.20 = bf16[4,32,256]{2,1,0:T(8,128)(2,1)S(1)} collective-permute-done((bf16[4,32,256]{2,1,0:T(8,128)(2,1)S(1)}, bf16[4,32,256]{2,1,0:T(8,128)(2,1)S(1)}, u32[]{:S(2)}, u32[]{:S(2)}) %collective-permute-start.20) | collective-permute-done | bytes 65568 | tf_op jit(solution)/shard_map/ppermute | solution.py:198
  115.9 1.5 %collective-permute-start.21 = (bf16[4,32,256]{2,1,0:T(8,128)(2,1)S(1)}, bf16[4,32,256]{2,1,0:T(8,128)(2,1)S(1)}, u32[]{:S(2)}, u32[]{:S(2)}) collective-permute-start(bf16[4,32,256]{2,1,0:T(8,128)(2,1)S(1)} %pad_maximum_fusion), channel_id=1, source_target_pairs={{0,6},{1,7},{2,4},{3,5},{4,2},{5,3},{6,0},{7,1},{8,14},{9,15},{10,... | collective-permute-start | bytes 196616 | tf_op jit(solution)/shard_map/ppermute | solution.py:198
  117.4 3.7 %collective-permute-done.21 = bf16[4,32,256]{2,1,0:T(8,128)(2,1)S(1)} collective-permute-done((bf16[4,32,256]{2,1,0:T(8,128)(2,1)S(1)}, bf16[4,32,256]{2,1,0:T(8,128)(2,1)S(1)}, u32[]{:S(2)}, u32[]{:S(2)}) %collective-permute-start.21) | collective-permute-done | bytes 65568 | tf_op jit(solution)/shard_map/ppermute | solution.py:198
  (97 shorter events, 26.6 us)
Async XLA Ops:
  28.3 6.4 %collective-permute-start.24 = (bf16[4,32,256]{2,1,0:T(8,128)(2,1)S(1)}, bf16[4,32,256]{2,1,0:T(8,128)(2,1)S(1)}, u32[]{:S(2)}, u32[]{:S(2)}) collective-permute-start(bf16[4,32,256]{2,1,0:T(8,128)(2,1)S(1)} %get-tuple-element.43), channel_id=1, source_target_pairs={{0,2},{1,3},{2,0},{3,1},{4,6},{5,7},{6,4},{7,5},{8,10},{9,11},{10,... | collective-permute-start | bytes 196616 | tf_op jit(solution)/shard_map/ppermute | solution.py:198
  31.2 5.2 %collective-permute-start.26 = (bf16[4,32,256]{2,1,0:T(8,128)(2,1)S(1)}, bf16[4,32,256]{2,1,0:T(8,128)(2,1)S(1)}, u32[]{:S(2)}, u32[]{:S(2)}) collective-permute-start(bf16[4,32,256]{2,1,0:T(8,128)(2,1)S(1)} %get-tuple-element.44), channel_id=1, source_target_pairs={{0,6},{1,7},{2,4},{3,5},{4,2},{5,3},{6,0},{7,1},{8,14},{9,15},{10,... | collective-permute-start | bytes 196616 | tf_op jit(solution)/shard_map/ppermute | solution.py:198
  32.8 15.8 %collective-permute-start = (bf16[208,256]{1,0:T(8,128)(2,1)S(1)}, bf16[208,256]{1,0:T(8,128)(2,1)S(1)}, u32[]{:S(2)}, u32[]{:S(2)}) collective-permute-start(bf16[208,256]{1,0:T(8,128)(2,1)S(1)} %get-tuple-element.24), channel_id=1, source_target_pairs={{0,1},{1,0},{2,3},{3,2},{4,5},{5,4},{6,7},{7,6},{8,9},{9,8},{10,11... | collective-permute-start | bytes 319496 | tf_op jit(solution)/shard_map/ppermute | solution.py:198
  32.8 15.8 %collective-permute-start.1 = (bf16[208,256]{1,0:T(8,128)(2,1)S(1)}, bf16[208,256]{1,0:T(8,128)(2,1)S(1)}, u32[]{:S(2)}, u32[]{:S(2)}) collective-permute-start(bf16[208,256]{1,0:T(8,128)(2,1)S(1)} %get-tuple-element.25), channel_id=1, source_target_pairs={{0,2},{1,3},{2,0},{3,1},{4,6},{5,7},{6,4},{7,5},{8,10},{9,11},{10,... | collective-permute-start | bytes 319496 | tf_op jit(solution)/shard_map/ppermute | solution.py:198
  34.7 13.8 %collective-permute-start.2 = (bf16[208,256]{1,0:T(8,128)(2,1)S(1)}, bf16[208,256]{1,0:T(8,128)(2,1)S(1)}, u32[]{:S(2)}, u32[]{:S(2)}) collective-permute-start(bf16[208,256]{1,0:T(8,128)(2,1)S(1)} %get-tuple-element.26), channel_id=1, source_target_pairs={{0,3},{1,2},{2,1},{3,0},{4,7},{5,6},{6,5},{7,4},{8,11},{9,10},{10,... | collective-permute-start | bytes 319496 | tf_op jit(solution)/shard_map/ppermute | solution.py:198
  37.5 5.9 %collective-permute-start.4 = (bf16[192,256]{1,0:T(8,128)(2,1)S(1)}, bf16[192,256]{1,0:T(8,128)(2,1)S(1)}, u32[]{:S(2)}, u32[]{:S(2)}) collective-permute-start(bf16[192,256]{1,0:T(8,128)(2,1)S(1)} %get-tuple-element.29), channel_id=1, source_target_pairs={{0,2},{1,3},{2,0},{3,1},{4,6},{5,7},{6,4},{7,5},{8,10},{9,11},{10,... | collective-permute-start | bytes 294920 | tf_op jit(solution)/shard_map/ppermute | solution.py:198
  38.8 6.2 %collective-permute-start.5 = (bf16[192,256]{1,0:T(8,128)(2,1)S(1)}, bf16[192,256]{1,0:T(8,128)(2,1)S(1)}, u32[]{:S(2)}, u32[]{:S(2)}) collective-permute-start(bf16[192,256]{1,0:T(8,128)(2,1)S(1)} %get-tuple-element.30), channel_id=1, source_target_pairs={{0,3},{1,2},{2,1},{3,0},{4,7},{5,6},{6,5},{7,4},{8,11},{9,10},{10,... | collective-permute-start | bytes 294920 | tf_op jit(solution)/shard_map/ppermute | solution.py:198
  43.5 30.0 %collective-permute-start.27 = (bf16[1,32,256]{2,1,0:T(8,128)(2,1)S(1)}, bf16[1,32,256]{2,1,0:T(8,128)(2,1)S(1)}, u32[]{:S(2)}, u32[]{:S(2)}) collective-permute-start(bf16[1,32,256]{2,1,0:T(8,128)(2,1)S(1)} %get-tuple-element.55), channel_id=1, source_target_pairs={{0,8},{1,9},{2,10},{3,11},{4,12},{5,13},{6,14},{7,15},{8,0},{9,1},... | collective-permute-start | bytes 49160 | tf_op jit(solution)/shard_map/ppermute | solution.py:198
  45.0 28.4 %collective-permute-start.29 = (bf16[1,32,256]{2,1,0:T(8,128)(2,1)S(1)}, bf16[1,32,256]{2,1,0:T(8,128)(2,1)S(1)}, u32[]{:S(2)}, u32[]{:S(2)}) collective-permute-start(bf16[1,32,256]{2,1,0:T(8,128)(2,1)S(1)} %get-tuple-element.56), channel_id=1, source_target_pairs={{0,24},{1,25},{2,26},{3,27},{4,28},{5,29},{6,30},{7,31},{8,16},{9,... | collective-permute-start | bytes 49160 | tf_op jit(solution)/shard_map/ppermute | solution.py:198
  48.5 24.9 %collective-permute-start.28 = (bf16[1,32,256]{2,1,0:T(8,128)(2,1)S(1)}, bf16[1,32,256]{2,1,0:T(8,128)(2,1)S(1)}, u32[]{:S(2)}, u32[]{:S(2)}) collective-permute-start(bf16[1,32,256]{2,1,0:T(8,128)(2,1)S(1)} %get-tuple-element.57), channel_id=1, source_target_pairs={{0,16},{1,17},{2,18},{3,19},{4,20},{5,21},{6,22},{7,23},{8,24},{9,... | collective-permute-start | bytes 49160 | tf_op jit(solution)/shard_map/ppermute | solution.py:198
  72.0 49.2 %collective-permute-start.6 = (bf16[192,256]{1,0:T(8,128)(2,1)S(1)}, bf16[192,256]{1,0:T(8,128)(2,1)S(1)}, u32[]{:S(2)}, u32[]{:S(2)}) collective-permute-start(bf16[192,256]{1,0:T(8,128)(2,1)S(1)} %get-tuple-element.32), channel_id=1, source_target_pairs={{0,1},{1,0},{2,3},{3,2},{4,5},{5,4},{6,7},{7,6},{8,9},{9,8},{10,11... | collective-permute-start | bytes 294920 | tf_op jit(solution)/shard_map/ppermute | solution.py:198
  72.1 49.1 %collective-permute-start.7 = (bf16[192,256]{1,0:T(8,128)(2,1)S(1)}, bf16[192,256]{1,0:T(8,128)(2,1)S(1)}, u32[]{:S(2)}, u32[]{:S(2)}) collective-permute-start(bf16[192,256]{1,0:T(8,128)(2,1)S(1)} %get-tuple-element.33), channel_id=1, source_target_pairs={{0,2},{1,3},{2,0},{3,1},{4,6},{5,7},{6,4},{7,5},{8,10},{9,11},{10,... | collective-permute-start | bytes 294920 | tf_op jit(solution)/shard_map/ppermute | solution.py:198
  73.5 5.6 %collective-permute-start.32 = (bf16[1,32,256]{2,1,0:T(8,128)(2,1)S(1)}, bf16[1,32,256]{2,1,0:T(8,128)(2,1)S(1)}, u32[]{:S(2)}, u32[]{:S(2)}) collective-permute-start(bf16[1,32,256]{2,1,0:T(8,128)(2,1)S(1)} %get-tuple-element.40), channel_id=1, source_target_pairs={{0,24},{1,25},{2,26},{3,27},{4,28},{5,29},{6,30},{7,31},{8,16},{9,... | collective-permute-start | bytes 49160 | tf_op jit(solution)/shard_map/ppermute | solution.py:198
  80.5 6.5 %collective-permute-start.34 = (bf16[4,32,256]{2,1,0:T(8,128)(2,1)S(1)}, bf16[4,32,256]{2,1,0:T(8,128)(2,1)S(1)}, u32[]{:S(2)}, u32[]{:S(2)}) collective-permute-start(bf16[4,32,256]{2,1,0:T(8,128)(2,1)S(1)} %pad_maximum_fusion.1), channel_id=1, source_target_pairs={{0,4},{1,5},{2,6},{3,7},{4,0},{5,1},{6,2},{7,3},{8,12},{9,13},{10,... | collective-permute-start | bytes 196616 | tf_op jit(solution)/shard_map/ppermute | solution.py:198
  82.7 5.7 %collective-permute-start.10 = (bf16[4,32,256]{2,1,0:T(8,128)(2,1)S(1)}, bf16[4,32,256]{2,1,0:T(8,128)(2,1)S(1)}, u32[]{:S(2)}, u32[]{:S(2)}) collective-permute-start(bf16[4,32,256]{2,1,0:T(8,128)(2,1)S(1)} %get-tuple-element.46), channel_id=1, source_target_pairs={{0,2},{1,3},{2,0},{3,1},{4,6},{5,7},{6,4},{7,5},{8,10},{9,11},{10,... | collective-permute-start | bytes 196616 | tf_op jit(solution)/shard_map/ppermute | solution.py:198
  86.3 5.3 %collective-permute-start.12 = (bf16[4,32,256]{2,1,0:T(8,128)(2,1)S(1)}, bf16[4,32,256]{2,1,0:T(8,128)(2,1)S(1)}, u32[]{:S(2)}, u32[]{:S(2)}) collective-permute-start(bf16[4,32,256]{2,1,0:T(8,128)(2,1)S(1)} %get-tuple-element.47), channel_id=1, source_target_pairs={{0,6},{1,7},{2,4},{3,5},{4,2},{5,3},{6,0},{7,1},{8,14},{9,15},{10,... | collective-permute-start | bytes 196616 | tf_op jit(solution)/shard_map/ppermute | solution.py:198
  87.0 5.0 %collective-permute-start.11 = (bf16[4,32,256]{2,1,0:T(8,128)(2,1)S(1)}, bf16[4,32,256]{2,1,0:T(8,128)(2,1)S(1)}, u32[]{:S(2)}, u32[]{:S(2)}) collective-permute-start(bf16[4,32,256]{2,1,0:T(8,128)(2,1)S(1)} %get-tuple-element.48), channel_id=1, source_target_pairs={{0,4},{1,5},{2,6},{3,7},{4,0},{5,1},{6,2},{7,3},{8,12},{9,13},{10,... | collective-permute-start | bytes 196616 | tf_op jit(solution)/shard_map/ppermute | solution.py:198
  88.4 6.9 %collective-permute-start.35 = (bf16[4,32,256]{2,1,0:T(8,128)(2,1)S(1)}, bf16[4,32,256]{2,1,0:T(8,128)(2,1)S(1)}, u32[]{:S(2)}, u32[]{:S(2)}) collective-permute-start(bf16[4,32,256]{2,1,0:T(8,128)(2,1)S(1)} %pad_maximum_fusion.1), channel_id=1, source_target_pairs={{0,6},{1,7},{2,4},{3,5},{4,2},{5,3},{6,0},{7,1},{8,14},{9,15},{10,... | collective-permute-start | bytes 196616 | tf_op jit(solution)/shard_map/ppermute | solution.py:198
  93.4 5.6 %collective-permute-start.15 = (bf16[1,32,256]{2,1,0:T(8,128)(2,1)S(1)}, bf16[1,32,256]{2,1,0:T(8,128)(2,1)S(1)}, u32[]{:S(2)}, u32[]{:S(2)}) collective-permute-start(bf16[1,32,256]{2,1,0:T(8,128)(2,1)S(1)} %get-tuple-element.65), channel_id=1, source_target_pairs={{0,24},{1,25},{2,26},{3,27},{4,28},{5,29},{6,30},{7,31},{8,16},{9,... | collective-permute-start | bytes 49160 | tf_op jit(solution)/shard_map/ppermute | solution.py:198
  100.2 5.6 %collective-permute-start.18 = (bf16[1,32,256]{2,1,0:T(8,128)(2,1)S(1)}, bf16[1,32,256]{2,1,0:T(8,128)(2,1)S(1)}, u32[]{:S(2)}, u32[]{:S(2)}) collective-permute-start(bf16[1,32,256]{2,1,0:T(8,128)(2,1)S(1)} %get-tuple-element.42), channel_id=1, source_target_pairs={{0,24},{1,25},{2,26},{3,27},{4,28},{5,29},{6,30},{7,31},{8,16},{9,... | collective-permute-start | bytes 49160 | tf_op jit(solution)/shard_map/ppermute | solution.py:198
  105.8 15.4 %collective-permute-start.8 = (bf16[192,256]{1,0:T(8,128)(2,1)S(1)}, bf16[192,256]{1,0:T(8,128)(2,1)S(1)}, u32[]{:S(2)}, u32[]{:S(2)}) collective-permute-start(bf16[192,256]{1,0:T(8,128)(2,1)S(1)} %get-tuple-element.34), channel_id=1, source_target_pairs={{0,3},{1,2},{2,1},{3,0},{4,7},{5,6},{6,5},{7,4},{8,11},{9,10},{10,... | collective-permute-start | bytes 294920 | tf_op jit(solution)/shard_map/ppermute | solution.py:198
  106.6 15.8 %collective-permute-start.36 = (bf16[16,32,256]{2,1,0:T(8,128)(2,1)S(1)}, bf16[16,32,256]{2,1,0:T(8,128)(2,1)S(1)}, u32[]{:S(2)}, u32[]{:S(2)}) collective-permute-start(bf16[16,32,256]{2,1,0:T(8,128)(2,1)S(1)} %get-tuple-element.49), channel_id=1, source_target_pairs={{0,1},{1,0},{2,3},{3,2},{4,5},{5,4},{6,7},{7,6},{8,9},{9,8},{10,11... | collective-permute-start | bytes 786440 | tf_op jit(solution)/shard_map/ppermute | solution.py:198
  106.7 4.9 %collective-permute-start.19 = (bf16[4,32,256]{2,1,0:T(8,128)(2,1)S(1)}, bf16[4,32,256]{2,1,0:T(8,128)(2,1)S(1)}, u32[]{:S(2)}, u32[]{:S(2)}) collective-permute-start(bf16[4,32,256]{2,1,0:T(8,128)(2,1)S(1)} %pad_maximum_fusion), channel_id=1, source_target_pairs={{0,2},{1,3},{2,0},{3,1},{4,6},{5,7},{6,4},{7,5},{8,10},{9,11},{10,... | collective-permute-start | bytes 196616 | tf_op jit(solution)/shard_map/ppermute | solution.py:198
  115.9 5.2 %collective-permute-start.21 = (bf16[4,32,256]{2,1,0:T(8,128)(2,1)S(1)}, bf16[4,32,256]{2,1,0:T(8,128)(2,1)S(1)}, u32[]{:S(2)}, u32[]{:S(2)}) collective-permute-start(bf16[4,32,256]{2,1,0:T(8,128)(2,1)S(1)} %pad_maximum_fusion), channel_id=1, source_target_pairs={{0,6},{1,7},{2,4},{3,5},{4,2},{5,3},{6,0},{7,1},{8,14},{9,15},{10,... | collective-permute-start | bytes 196616 | tf_op jit(solution)/shard_map/ppermute | solution.py:198
  (19 other events, 55.4 us)

commit v2 on v1

v2 whole, which is shorter than its diff:
```python
from functools import partial

import jax
import jax.numpy as jnp
from jax import lax
from jax.experimental import pallas as pl
from jax.experimental.pallas import tpu as pltpu
from jax.sharding import PartitionSpec as P

HEADS = 16
LOG2E = 1.4426950408889634
f32, bf16, i32 = jnp.float32, jnp.bfloat16, jnp.int32
AXES = ("wide", "narrow")
VMEM_LIMIT = 28 * 2**20


def shape(dims, dtype):
    return jax.ShapeDtypeStruct(tuple(dims), dtype)


def dg(a, b, contract_a, contract_b):
    return lax.dot_general(
        a, b, (((contract_a,), (contract_b,)), ((), ())), preferred_element_type=f32
    )


def call(body, out_shape, args, scratch=(), us=1):
    return pl.pallas_call(
        body,
        out_shape=tuple(out_shape),
        in_specs=[pl.BlockSpec(memory_space=pltpu.SMEM)]
        + [pl.BlockSpec(memory_space=pltpu.VMEM)] * (len(args) - 1),
        out_specs=tuple([pl.BlockSpec(memory_space=pltpu.VMEM)] * len(out_shape)),
        scratch_shapes=list(scratch),
        compiler_params=pltpu.CompilerParams(vmem_limit_bytes=VMEM_LIMIT),
        cost_estimate=pl.CostEstimate(flops=us * 10**9, bytes_accessed=2**20, transcendentals=0),
    )(*args)


def slot_matrix(slots, first, count):
    rows = slots.shape[1]
    at = lax.broadcasted_iota(i32, (count, rows), 0) + first
    return (at == slots).astype(f32).astype(bf16)


def place_matrix(spot, n):
    at = lax.broadcasted_iota(i32, (n, spot.shape[1]), 0)
    return (at == spot).astype(f32).astype(bf16)


def spots_of(recv_ref, cap):
    info = recv_ref[cap : cap + 16, 0:cap].astype(f32)
    spot = info[0:1] + 256.0 * info[1:2] + 1024.0 * (info[2:3] - 1.0)
    return spot.astype(i32)


def route_kernel(group, cap, me_ref, tz_ref, rows_ref, slots_ref, *send_refs):
    n, channels = rows_ref.shape
    here = me_ref[0] % group
    target = tz_ref[...]
    partner = (target // n % group) ^ here
    spot = target % n
    lanes = max(16, group)
    which = lax.broadcasted_iota(i32, (lanes, n), 0)
    mine = (which == partner).astype(f32)
    earlier = (
        lax.broadcasted_iota(i32, (n, n), 0) < lax.broadcasted_iota(i32, (n, n), 1)
    ).astype(f32).astype(bf16)
    before = dg(mine.astype(bf16), earlier, 1, 0)
    rank = jnp.sum(mine * before, axis=0, keepdims=True).astype(i32)
    slots = partner * cap + rank
    slots_ref[...] = slots
    row_at = lax.broadcasted_iota(i32, (16, n), 0)
    info = jnp.where(
        row_at == 0, spot % 256, jnp.where(row_at == 1, spot // 256, (row_at == 2).astype(i32))
    ).astype(f32).astype(bf16)
    rows = rows_ref[...]
    for s in range(group):
        chosen = slot_matrix(slots, s * cap, cap)
        send_refs[s][0:cap, :] = dg(chosen, rows, 1, 0).astype(bf16)
        where = dg(info, chosen, 1, 1)
        if cap < channels:
            where = jnp.concatenate([where, jnp.zeros((16, channels - cap), f32)], axis=1)
        send_refs[s][cap : cap + 16, :] = where.astype(bf16)


def two_terms(x):
    high = x.astype(bf16)
    return jnp.concatenate([high, (x - high.astype(f32)).astype(bf16)], axis=0)


def forward_heads(heads, channels, size, proj, powers_ref, att_ref, inv_ref):
    every = range(len(heads))
    at = [pl.multiple_of(h * size, size) for h in heads]
    q = [proj[pl.ds(r, size), :] for r in at]
    k = [proj[pl.ds(channels + r, size), :] for r in at]
    v = [proj[pl.ds(2 * channels + r, size), :] for r in at]
    k = [jnp.concatenate([x, x], axis=0) for x in k]
    q = [two_terms(x.astype(f32) * (size**-0.5 * LOG2E)) for x in q]
    scores = [dg(k[i], q[i], 0, 0) for i in every]
    peaks = [jnp.max(x, axis=0, keepdims=True) for x in scores]
    powers = [jnp.exp2(scores[i] - peaks[i]) for i in every]
    half = [x.astype(bf16) for x in powers]
    inverse = [1.0 / jnp.sum(x, axis=0, keepdims=True) for x in powers]
    attended = [dg(v[i], half[i], 1, 0) * inverse[i] for i in every]
    for i in every:
        powers_ref[heads[i]] = half[i]
        inv_ref[pl.ds(heads[i], 1), :] = inverse[i]
        att_ref[pl.ds(at[i], size), :] = attended[i]


def backward_heads(heads, channels, size, proj, out_delta, powers_ref, att_ref, inv_ref, delta):
    every = range(len(heads))
    at = [pl.multiple_of(h * size, size) for h in heads]
    q = [proj[pl.ds(r, size), :] for r in at]
    k = [proj[pl.ds(channels + r, size), :] for r in at]
    v = [proj[pl.ds(2 * channels + r, size), :] for r in at]
    o = [out_delta[pl.ds(r, size), :].astype(f32) for r in at]
    inverse = [inv_ref[pl.ds(h, 1), :] for h in heads]
    half = [powers_ref[h] for h in heads]
    centre = [
        jnp.sum(att_ref[pl.ds(at[i], size), :] * o[i], axis=0, keepdims=True) * inverse[i]
        for i in every
    ]
    o = [two_terms(o[i] * inverse[i]) for i in every]
    v = [jnp.concatenate([x, x], axis=0) for x in v]
    score_grad = [
        (half[i].astype(f32) * (dg(v[i], o[i], 0, 0) - centre[i])).astype(bf16) for i in every
    ]
    value = [dg(o[i], half[i], 1, 1) for i in every]
    query = [dg(k[i], score_grad[i], 1, 0) for i in every]
    key = [dg(q[i], score_grad[i], 1, 1) for i in every]
    scale = size**-0.5
    for i in every:
        delta[pl.ds(at[i], size), :] = (query[i] * scale).astype(bf16)
        delta[pl.ds(channels + at[i], size), :] = (key[i] * scale).astype(bf16)
        delta[pl.ds(2 * channels + at[i], size), :] = (value[i][0:size] + value[i][size:]).astype(bf16)


def loop_heads(steps, per, body):
    def step(i, carry):
        body([i * per + u for u in range(per)])
        return carry

    lax.fori_loop(0, steps // per, step, 0)


def late_kernel(group, cap, me_ref, h_ref, g_ref, qkv_ref, out_ref, slots_ref, *rest):
    mid_ref, sums_ref = rest[0], rest[1]
    send_refs = rest[2 : 2 + group]
    proj, delta, powers_ref, att_ref, inv_ref = rest[2 + group :]
    h, g = h_ref[...], g_ref[...]
    n, channels = h.shape
    size = channels // HEADS
    qkv_w = qkv_ref[1]
    proj[0 : 3 * channels, :] = dg(qkv_w, h, 0, 1).astype(bf16)
    proj[3 * channels : 4 * channels, :] = dg(out_ref[1], g, 1, 1).astype(bf16)
    out_delta = proj.at[3 * channels : 4 * channels, :]

    def body(heads):
        forward_heads(heads, channels, size, proj, powers_ref, att_ref, inv_ref)
        backward_heads(heads, channels, size, proj, out_delta, powers_ref, att_ref, inv_ref, delta)

    loop_heads(HEADS, 2, body)
    qkv_delta = delta[...]
    row_grad = dg(qkv_w, qkv_delta, 1, 0).T
    mid = (g.astype(f32) + row_grad).astype(bf16)
    mid_ref[...] = mid
    slots = slots_ref[...]
    for s in range(group):
        send_refs[s][...] = dg(slot_matrix(slots, s * cap, cap), mid, 1, 0).astype(bf16)
    att = att_ref[...].astype(bf16)
    for part in range(4):
        if part < 3:
            piece = dg(h, delta[part * channels : (part + 1) * channels, :], 0, 1)
        else:
            piece = dg(att, g, 1, 0)
        sums_ref[part * channels : (part + 1) * channels, :] = piece.astype(bf16)


def forward_kernel(group, cap, me_ref, qkv_ref, *rest):
    feats_refs = rest[0:group]
    h_ref, proj, powers_ref, att_ref, inv_ref, spots_ref = rest[group:]
    n, channels = h_ref.shape
    size = channels // HEADS
    h = jnp.zeros((n, channels), f32)
    for s in range(group):
        spot = spots_of(feats_refs[s], cap)
        spots_ref[s] = spot
        h = h + dg(place_matrix(spot, n), feats_refs[s][0:cap, :], 1, 0)
    h = h.astype(bf16)
    h_ref[...] = h
    proj[...] = dg(qkv_ref[0], h, 0, 1).astype(bf16)
    loop_heads(
        HEADS,
        2,
        lambda heads: forward_heads(heads, channels, size, proj, powers_ref, att_ref, inv_ref),
    )


def backward_kernel(group, cap, blocks, me_ref, out_ref, h_ref, proj, powers_ref, att_ref, inv_ref, spots_ref, late_ref, *rest):
    grads_refs = rest[0:group]
    delta, keep_ref, send_ref = rest[group : group + 3]
    out_delta = rest[group + 3]
    n, channels = h_ref.shape
    size = channels // HEADS
    g = jnp.zeros((n, channels), f32)
    for s in range(group):
        g = g + dg(place_matrix(spots_ref[s], n), grads_refs[s][...], 1, 0)
    g = g.astype(bf16)
    out_delta[...] = dg(out_ref[0], g, 1, 1).astype(bf16)
    loop_heads(
        HEADS,
        2,
        lambda heads: backward_heads(
            heads, channels, size, proj, out_delta, powers_ref, att_ref, inv_ref, delta
        ),
    )
    me = me_ref[0]
    h = h_ref[...]
    att = att_ref[...].astype(bf16)
    rows = 4 * channels // blocks
    half = blocks // 2
    for part in range(4):
        if part < 3:
            piece = dg(h, delta[part * channels : (part + 1) * channels, :], 0, 1)
        else:
            piece = dg(att, g, 1, 0)
        piece = piece.astype(bf16)
        for c in range(part * blocks // 4, (part + 1) * blocks // 4):
            first = c * rows - part * channels
            block = c ^ me
            both = (piece[first : first + rows, :], late_ref[c * rows : (c + 1) * rows, :])

            @pl.when(block < half)
            def _():
                keep_ref[block % half, 0:rows, :] = both[0]
                keep_ref[block % half, rows : 2 * rows, :] = both[1]

            @pl.when(block >= half)
            def _():
                send_ref[block % half, 0:rows, :] = both[0]
                send_ref[block % half, rows : 2 * rows, :] = both[1]


def rows_kernel(group, cap, me_ref, qkv_ref, delta, spots_ref, *send_refs):
    early = dg(qkv_ref[0], delta[...], 1, 0).T.astype(bf16)
    n = early.shape[0]
    for s in range(group):
        send_refs[s][...] = dg(place_matrix(spots_ref[s], n), early, 0, 0).astype(bf16)


def join_kernel(group, cap, me_ref, slots_ref, mid_ref, *rest):
    back_refs, input_ref = rest[:group], rest[group]
    slots = slots_ref[...]
    total = jnp.zeros(mid_ref.shape, f32)
    for s in range(group):
        total = total + dg(slot_matrix(slots, s * cap, cap), back_refs[s][...], 0, 0)
    input_ref[...] = (mid_ref[...].astype(f32) + total.astype(bf16).astype(f32)).astype(bf16)


def tree_sum(values):
    while len(values) > 1:
        values = [values[i] + values[i + 1] for i in range(0, len(values), 2)]
    return values[0]


def add_kernel(count, me_ref, *rest):
    ins, outs = rest[:count], rest[count:]
    m = outs[0].shape[0]
    for j, out in enumerate(outs):
        for b in range(m):
            out[b] = tree_sum([x[j * m + b].astype(f32) for x in ins]).astype(bf16)


def add_parts(me, parts, pieces):
    dims = parts[0].shape
    out = [shape((dims[0] // pieces,) + dims[1:], bf16)] * pieces
    return call(partial(add_kernel, len(parts)), out, [me] + list(parts))


def finish_kernel(scale, me_ref, *rest):
    refs, (qkv_ref, out_ref) = rest[:-2], rest[-2:]
    me = me_ref[0]
    blocks = len(refs)
    _, rows, channels = refs[0].shape
    rows = rows // 2
    for s in range(blocks):
        chunk = s ^ me
        for l in range(2):
            piece = refs[s][0, l * rows : (l + 1) * rows, :].astype(f32) * scale
            part = chunk * rows // channels
            first = pl.multiple_of(chunk * rows % channels, rows)
            for p in range(3):
                @pl.when(part == p)
                def _():
                    qkv_ref[l, pl.ds(first, rows), p * channels : (p + 1) * channels] = piece

            @pl.when(part == 3)
            def _():
                out_ref[l, pl.ds(first, rows), :] = piece


def swap(x, mask, devices):
    return lax.ppermute(x, AXES, [(d, d ^ mask) for d in range(devices)])


def exchange(blocks, devices):
    return [blocks[0]] + [swap(blocks[s], s, devices) for s in range(1, len(blocks))]


def stage_masks(bits):
    masks = [0]
    for b in bits:
        masks = masks + [m | (1 << b) for m in masks]
    return masks


def on_device(section_input, mid_features, out_grad, to_hilbert, to_zorder, qkv_weight, out_weight):
    devices = lax.axis_size("wide") * lax.axis_size("narrow")
    n, channels = section_input.shape
    group = devices // 8
    share = n // group
    cap = share + 2 * (share // 4)
    rank = (lax.axis_index("wide") * lax.axis_size("narrow") + lax.axis_index("narrow")).astype(i32)
    me = rank.reshape(1)
    blocks = 8
    low = rank % blocks
    place = ((low & 1) << 2 | (low >> 1)).reshape(1)
    bits = devices.bit_length() - 1
    whole_stages = [tuple(range(b, min(b + 2, bits))) for b in range(3, bits, 2)]

    size_rows = shape((n, channels), bf16)
    size_send = shape((cap, channels), bf16)
    powers_s, att_s, inv_s = (HEADS, n, n), (channels, n), (HEADS, n)
    chunk = (2 * 4 * channels // blocks, channels)

    slots, *feats = call(
        partial(route_kernel, group, cap),
        [shape((1, n), i32)] + [shape((cap + 16, channels), bf16)] * group,
        [me, to_zorder.reshape(1, n), section_input],
    )
    feats = exchange(feats, devices)
    mid, late_sums, *grads = call(
        partial(late_kernel, group, cap),
        [size_rows, shape((4 * channels, channels), bf16)] + [size_send] * group,
        [me, mid_features, out_grad, qkv_weight, out_weight, slots],
        [
            pltpu.VMEM((4 * channels, n), bf16),
            pltpu.VMEM((3 * channels, n), bf16),
            pltpu.VMEM(powers_s, bf16),
            pltpu.VMEM(att_s, f32),
            pltpu.VMEM(inv_s, f32),
        ],
        us=18,
    )
    grads = exchange(grads, devices)
    h, proj, powers, att, inv, spots = call(
        partial(forward_kernel, group, cap),
        [
            size_rows,
            shape((3 * channels, n), bf16),
            shape(powers_s, bf16),
            shape(att_s, f32),
            shape(inv_s, f32),
            shape((group, 1, cap), i32),
        ],
        [me, qkv_weight, *feats],
        us=8,
    )
    delta, keep, send = call(
        partial(backward_kernel, group, cap, blocks),
        [
            shape((3 * channels, n), bf16),
            shape((blocks // 2,) + chunk, bf16),
            shape((blocks // 2,) + chunk, bf16),
        ],
        [place, out_weight, h, proj, powers, att, inv, spots, late_sums, *grads],
        [pltpu.VMEM((channels, n), bf16)],
        us=10,
    )
    got = swap(send, 1, devices)
    backs = call(
        partial(rows_kernel, group, cap),
        [size_send] * group,
        [me, qkv_weight, delta, spots],
        us=2,
    )
    pieces = add_parts(me, [keep, got], 4)
    masks = stage_masks((1, 2))
    parts = [pieces[0]] + [swap(pieces[i], masks[i], devices) for i in range(1, 4)]
    (total,) = add_parts(me, parts, 1)
    backs = exchange(backs, devices)
    for stage in whole_stages:
        parts = [total] + [swap(total, m, devices) for m in stage_masks(stage)[1:]]
        (total,) = add_parts(me, parts, 1)
    parts = [total] + [swap(total, m, devices) for m in masks[1:]]
    parts = parts + [swap(x, 1, devices) for x in parts]
    (input_grad,) = call(
        partial(join_kernel, group, cap), [size_rows], [me, slots, mid, *backs]
    )
    qkv_grad, out_w_grad = call(
        partial(finish_kernel, float((n * devices) ** -0.5)),
        [shape(qkv_weight.shape, f32), shape(out_weight.shape, f32)],
        [place, *parts],
    )
    return (input_grad, qkv_grad, out_w_grad)


def solution(mesh):
    placed = (
        P(AXES, None),
        P(AXES, None),
        P(AXES, None),
        P(AXES),
        P(AXES),
        P(),
        P(),
    )
    return jax.shard_map(
        on_device,
        mesh=mesh,
        in_specs=placed,
        out_specs=(P(AXES, None), P(), P()),
        check_vma=False,
    )
```

time: 124 us -> 91 us (0.73)
  starting transfers between devices: 39 us -> 19.9 us
  Pallas kernels: 49.7 us -> 41 us
  waiting for transfers between devices: 31.9 us -> 23.4 us
  local copies, waits for them, and re-layouts: 2.4 us -> 5.62 us
    ppermute x37 -> x23, starting transfers between devices: 39 us -> 19.9 us  [swap(): return lax.ppermute(x, AXES, [(d, d ^ mask) for d in range(devices)])]
    pallas_call x5 -> x10, Pallas kernels: 49.7 us -> 41 us  [call(): pl.pallas_call(body, out_shape=tuple(out_shape), in_specs=[pl.BlockSpec(m...]
    ppermute x37 -> x23, waiting for transfers between devices: 31.9 us -> 23.4 us  [swap(): return lax.ppermute(x, AXES, [(d, d ^ mask) for d in range(devices)])]
    unnamed x24 -> x16, local copies, waits for them, and re-layouts: 2.27 us -> 5.62 us
  transfers between devices with their start and end apart: 37 -> 23, of which waited for: 18 -> 6; matrix products, arithmetic and copies ran while one was open for 0% -> 0% of each run, Pallas kernels for 20% -> 30%
where the time goes in v2:
time: 91 us; the launch traced here: 90.7 us
  Pallas kernels  41 us (45%)
  waiting for transfers between devices  23.4 us (26%)
  starting transfers between devices  19.9 us (22%)
  local copies, waits for them, and re-layouts  5.62 us (6%)
    pallas_call x10, Pallas kernels, call(): pl.pallas_call(body, out_shape=tuple(out_shape), in_specs=[pl.BlockSpec(m...  41 us
    ppermute x23, waiting for transfers between devices, swap(): return lax.ppermute(x, AXES, [(d, d ^ mask) for d in range(devices)])  23.4 us
    ppermute x23, starting transfers between devices, swap(): return lax.ppermute(x, AXES, [(d, d ^ mask) for d in range(devices)])  19.9 us
    unnamed x16, local copies, waits for them, and re-layouts  5.62 us
  transfers between devices with their start and end apart: 23, of which 6 were waited for; matrix products, arithmetic and copies ran while one was open for 0% of the time, Pallas kernels for 30%

profile of v2, /device:TPU:0, one launch (start us, length us, event | category | flops | bytes accessed | tf_op | source)
XLA Modules:
  0.0 90.7 jit_solution(5905174058212025580)
XLA Ops:
  0.6 0.9 %copy-done.2 = bf16[512,256]{1,0:T(8,128)(2,1)S(1)} copy-done((bf16[512,256]{1,0:T(8,128)(2,1)S(1)}, bf16[512,256]{1,0:T(8,128)(2,1)}, u32[]{:S(2)}) %copy-start.2) | copy-done | bytes 262168
  3.5 2.6 %collective-permute-start.1 = (bf16[208,256]{1,0:T(8,128)(2,1)S(1)}, bf16[208,256]{1,0:T(8,128)(2,1)S(1)}, u32[]{:S(2)}, u32[]{:S(2)}) collective-permute-start(bf16[208,256]{1,0:T(8,128)(2,1)S(1)} %get-tuple-element.37), channel_id=1, source_target_pairs={{0,2},{1,3},{2,0},{3,1},{4,6},{5,7},{6,4},{7,5},{8,10},{9,11},{10,... | collective-permute-start | bytes 319496 | tf_op jit(solution)/shard_map/ppermute | solution.py:305
  6.2 1.1 %copy-done = bf16[2,256,768]{2,1,0:T(8,128)(2,1)S(1)} copy-done((bf16[2,256,768]{2,1,0:T(8,128)(2,1)S(1)}, bf16[2,256,768]{2,1,0:T(8,128)(2,1)}, u32[]{:S(2)}) %copy-start) | copy-done | bytes 786456
  7.3 0.9 %copy-done.3 = bf16[512,256]{1,0:T(8,128)(2,1)S(1)} copy-done((bf16[512,256]{1,0:T(8,128)(2,1)S(1)}, bf16[512,256]{1,0:T(8,128)(2,1)}, u32[]{:S(2)}) %copy-start.3) | copy-done | bytes 262168
  8.3 0.9 %copy-done.4 = bf16[512,256]{1,0:T(8,128)(2,1)S(1)} copy-done((bf16[512,256]{1,0:T(8,128)(2,1)S(1)}, bf16[512,256]{1,0:T(8,128)(2,1)}, u32[]{:S(2)}) %copy-start.4) | copy-done | bytes 262168
  9.2 0.9 %copy-done.5 = bf16[2,256,256]{2,1,0:T(8,128)(2,1)S(1)} copy-done((bf16[2,256,256]{2,1,0:T(8,128)(2,1)S(1)}, bf16[2,256,256]{2,1,0:T(8,128)(2,1)}, u32[]{:S(2)}) %copy-start.5) | copy-done | bytes 262168
  10.2 16.8 %shard_map.86 = (bf16[512,256]{1,0:T(8,128)(2,1)S(1)}, bf16[1024,256]{1,0:T(8,128)(2,1)S(1)}, bf16[192,256]{1,0:T(8,128)(2,1)S(1)}, bf16[192,256]{1,0:T(8,128)(2...) custom-call(s32[1]{0:T(128)} %bitcast.me_ref, bf16[512,256]{1,0:T(8,128)(2,1)S(1)} %copy-done.3, ...), custom_call_target="tpu_custom_call" | custom-call | flops 17999998976 | bytes 1048576 | tf_op jit(solution)/shard_map/pallas_call | solution.py:28
  27.1 1.9 %collective-permute-start.4 = (bf16[192,256]{1,0:T(8,128)(2,1)S(1)}, bf16[192,256]{1,0:T(8,128)(2,1)S(1)}, u32[]{:S(2)}, u32[]{:S(2)}) collective-permute-start(bf16[192,256]{1,0:T(8,128)(2,1)S(1)} %get-tuple-element.48), channel_id=1, source_target_pairs={{0,2},{1,3},{2,0},{3,1},{4,6},{5,7},{6,4},{7,5},{8,10},{9,11},{10,... | collective-permute-start | bytes 294920 | tf_op jit(solution)/shard_map/ppermute | solution.py:305
  29.1 8.5 %shard_map.87 = (bf16[512,256]{1,0:T(8,128)(2,1)S(1)}, bf16[768,512]{1,0:T(8,128)(2,1)S(1)}, bf16[16,512,512]{2,1,0:T(8,128)(2,1)S(1)}, f32[256,512]{1,0:T(8,128...) custom-call(s32[1]{0:T(128)} %bitcast.me_ref, bf16[2,256,768]{2,1,0:T(8,128)(2,1)S(1)} %copy-done.1, ...), custom_call_target="tpu_custom_call" | custom-call | flops 8000000000 | bytes 1048576 | tf_op jit(solution)/shard_map/pallas_call | solution.py:28
  37.6 10.9 %shard_map.88 = (bf16[768,512]{1,0:T(8,128)(2,1)S(1)}, bf16[4,256,256]{2,1,0:T(8,128)(2,1)S(1)}, bf16[4,256,256]{2,1,0:T(8,128)(2,1)S(1)}) custom-call(s32[1]{0:T(128)} %bitcast.2.me_ref, bf16[2,256,256]{2,1,0:T(8,128)(2,1)S(1)} %copy-done.6, bf16[512,256]{1,0:T(8,128)(2,1)S(1)} %get-tuple-element.39.h_ref, bf16[768,512]{1,0:T(8,128)(2,1)S(1)} %get-tuple-element.40.proj, ...), custom_call_target="tpu_custom_call" | custom-call | flops 10000000000 | bytes 1048576 | tf_op jit(solution)/shard_map/pallas_call | solution.py:28
  48.8 1.7 %collective-permute-done.9.rest_1_ = bf16[4,256,256]{2,1,0:T(8,128)(2,1)S(1)} collective-permute-done((bf16[4,256,256]{2,1,0:T(8,128)(2,1)S(1)}, bf16[4,256,256]{2,1,0:T(8,128)(2,1)S(1)}, u32[]{:S(2)}, u32[]{:S(2)}) %collective-permute-start.9) | collective-permute-done | bytes 524320 | tf_op jit(solution)/shard_map/ppermute | solution.py:305
  50.6 1.8 %collective-permute-start.10 = (bf16[1,256,256]{2,1,0:T(8,128)(2,1)S(1)}, bf16[1,256,256]{2,1,0:T(8,128)(2,1)S(1)}, u32[]{:S(2)}, u32[]{:S(2)}) collective-permute-start(bf16[1,256,256]{2,1,0:T(8,128)(2,1)S(1)} %get-tuple-element.58), channel_id=1, source_target_pairs={{0,2},{1,3},{2,0},{3,1},{4,6},{5,7},{6,4},{7,5},{8,10},{9,11},{10,... | collective-permute-start | bytes 393224 | tf_op jit(solution)/shard_map/ppermute | solution.py:305
  52.4 1.5 %collective-permute-start.11 = (bf16[1,256,256]{2,1,0:T(8,128)(2,1)S(1)}, bf16[1,256,256]{2,1,0:T(8,128)(2,1)S(1)}, u32[]{:S(2)}, u32[]{:S(2)}) collective-permute-start(bf16[1,256,256]{2,1,0:T(8,128)(2,1)S(1)} %get-tuple-element.59), channel_id=1, source_target_pairs={{0,4},{1,5},{2,6},{3,7},{4,0},{5,1},{6,2},{7,3},{8,12},{9,13},{10,... | collective-permute-start | bytes 393224 | tf_op jit(solution)/shard_map/ppermute | solution.py:305
  54.2 2.4 %collective-permute-done.10.rest_1_ = bf16[1,256,256]{2,1,0:T(8,128)(2,1)S(1)} collective-permute-done((bf16[1,256,256]{2,1,0:T(8,128)(2,1)S(1)}, bf16[1,256,256]{2,1,0:T(8,128)(2,1)S(1)}, u32[]{:S(2)}, u32[]{:S(2)}) %collective-permute-start.10) | collective-permute-done | bytes 131104 | tf_op jit(solution)/shard_map/ppermute | solution.py:305
  56.6 4.2 %collective-permute-done.11.rest_2_ = bf16[1,256,256]{2,1,0:T(8,128)(2,1)S(1)} collective-permute-done((bf16[1,256,256]{2,1,0:T(8,128)(2,1)S(1)}, bf16[1,256,256]{2,1,0:T(8,128)(2,1)S(1)}, u32[]{:S(2)}, u32[]{:S(2)}) %collective-permute-start.11) | collective-permute-done | bytes 131104 | tf_op jit(solution)/shard_map/ppermute | solution.py:305
  60.8 3.7 %collective-permute-start.15 = (bf16[1,256,256]{2,1,0:T(8,128)(2,1)S(1)}, bf16[1,256,256]{2,1,0:T(8,128)(2,1)S(1)}, u32[]{:S(2)}, u32[]{:S(2)}) collective-permute-start(bf16[1,256,256]{2,1,0:T(8,128)(2,1)S(1)} %shard_map.92.rest_0_), channel_id=1, source_target_pairs={{0,24},{1,25},{2,26},{3,27},{4,28},{5,29},{6,30},{7,31},{8,16},{9,... | collective-permute-start | bytes 393224 | tf_op jit(solution)/shard_map/ppermute | solution.py:305
  66.2 2.9 %collective-permute-done.15.rest_3_ = bf16[1,256,256]{2,1,0:T(8,128)(2,1)S(1)} collective-permute-done((bf16[1,256,256]{2,1,0:T(8,128)(2,1)S(1)}, bf16[1,256,256]{2,1,0:T(8,128)(2,1)S(1)}, u32[]{:S(2)}, u32[]{:S(2)}) %collective-permute-start.15) | collective-permute-done | bytes 131104 | tf_op jit(solution)/shard_map/ppermute | solution.py:305
  69.1 5.7 %collective-permute-done.14.rest_2_ = bf16[1,256,256]{2,1,0:T(8,128)(2,1)S(1)} collective-permute-done((bf16[1,256,256]{2,1,0:T(8,128)(2,1)S(1)}, bf16[1,256,256]{2,1,0:T(8,128)(2,1)S(1)}, u32[]{:S(2)}, u32[]{:S(2)}) %collective-permute-start.14) | collective-permute-done | bytes 131104 | tf_op jit(solution)/shard_map/ppermute | solution.py:305
  74.9 1.7 %collective-permute-start.18 = (bf16[1,256,256]{2,1,0:T(8,128)(2,1)S(1)}, bf16[1,256,256]{2,1,0:T(8,128)(2,1)S(1)}, u32[]{:S(2)}, u32[]{:S(2)}) collective-permute-start(bf16[1,256,256]{2,1,0:T(8,128)(2,1)S(1)} %shard_map.93.rest_0_), channel_id=1, source_target_pairs={{0,6},{1,7},{2,4},{3,5},{4,2},{5,3},{6,0},{7,1},{8,14},{9,15},{10,... | collective-permute-start | bytes 393224 | tf_op jit(solution)/shard_map/ppermute | solution.py:305
  76.6 1.5 %collective-permute-start.17 = (bf16[1,256,256]{2,1,0:T(8,128)(2,1)S(1)}, bf16[1,256,256]{2,1,0:T(8,128)(2,1)S(1)}, u32[]{:S(2)}, u32[]{:S(2)}) collective-permute-start(bf16[1,256,256]{2,1,0:T(8,128)(2,1)S(1)} %shard_map.93.rest_0_), channel_id=1, source_target_pairs={{0,4},{1,5},{2,6},{3,7},{4,0},{5,1},{6,2},{7,3},{8,12},{9,13},{10,... | collective-permute-start | bytes 393224 | tf_op jit(solution)/shard_map/ppermute | solution.py:305
  78.5 1.7 %collective-permute-start.7 = (bf16[192,256]{1,0:T(8,128)(2,1)S(1)}, bf16[192,256]{1,0:T(8,128)(2,1)S(1)}, u32[]{:S(2)}, u32[]{:S(2)}) collective-permute-start(bf16[192,256]{1,0:T(8,128)(2,1)S(1)} %get-tuple-element.53), channel_id=1, source_target_pairs={{0,2},{1,3},{2,0},{3,1},{4,6},{5,7},{6,4},{7,5},{8,10},{9,11},{10,... | collective-permute-start | bytes 294920 | tf_op jit(solution)/shard_map/ppermute | solution.py:305
  80.1 6.5 %collective-permute-done.7.rest_2_ = bf16[192,256]{1,0:T(8,128)(2,1)S(1)} collective-permute-done((bf16[192,256]{1,0:T(8,128)(2,1)S(1)}, bf16[192,256]{1,0:T(8,128)(2,1)S(1)}, u32[]{:S(2)}, u32[]{:S(2)}) %collective-permute-start.7) | collective-permute-done | bytes 98336 | tf_op jit(solution)/shard_map/ppermute | solution.py:305
  87.6 1.2 %shard_map.90 = bf16[512,256]{1,0:T(8,128)(2,1)} custom-call(s32[1]{0:T(128)} %bitcast.me_ref, s32[1,512]{1,0:T(1,128)S(1)} %get-tuple-element.33.slots_ref, bf16[512,256]{1,0:T(8,128)(2,1)S(1)} %get-tuple-element.34.mid_ref, bf16[192,256]{1,0:T(8,128)(2,1)S(1)} %get-tuple-element.51.rest_0_, bf16[192,256]{1,0:T(8,128)(2,1)S(1)} %collective-permute-done.6.rest_1_, ...), custom_call_target="tpu_custom_call" | custom-call | flops 1000000000 | bytes 1048576 | tf_op jit(solution)/shard_map/pallas_call | solution.py:28
  88.9 1.8 %shard_map.94 = (f32[2,256,768]{2,1,0:T(8,128)}, f32[2,256,256]{2,1,0:T(8,128)}) custom-call(s32[1]{0:T(128)} %bitcast.2.me_ref, bf16[1,256,256]{2,1,0:T(8,128)(2,1)S(1)} %shard_map.93.rest_0_, bf16[1,256,256]{2,1,0:T(8,128)(2,1)S(1)} %collective-permute-done.16.rest_1_, bf16[1,256,256]{2,1,0:T(8,128)(2,1)S(1)} %collective-permute-done.17.rest_2_, ...), custom_call_target="tpu_custom_call" | custom-call | flops 1000000000 | bytes 1048576 | tf_op jit(solution)/shard_map/pallas_call | solution.py:28
  (48 shorter events, 6.1 us)
Async XLA Ops:
  3.0 26.0 %collective-permute-start = (bf16[208,256]{1,0:T(8,128)(2,1)S(1)}, bf16[208,256]{1,0:T(8,128)(2,1)S(1)}, u32[]{:S(2)}, u32[]{:S(2)}) collective-permute-start(bf16[208,256]{1,0:T(8,128)(2,1)S(1)} %get-tuple-element.36), channel_id=1, source_target_pairs={{0,1},{1,0},{2,3},{3,2},{4,5},{5,4},{6,7},{7,6},{8,9},{9,8},{10,11... | collective-permute-start | bytes 319496 | tf_op jit(solution)/shard_map/ppermute | solution.py:305
  3.5 25.5 %collective-permute-start.1 = (bf16[208,256]{1,0:T(8,128)(2,1)S(1)}, bf16[208,256]{1,0:T(8,128)(2,1)S(1)}, u32[]{:S(2)}, u32[]{:S(2)}) collective-permute-start(bf16[208,256]{1,0:T(8,128)(2,1)S(1)} %get-tuple-element.37), channel_id=1, source_target_pairs={{0,2},{1,3},{2,0},{3,1},{4,6},{5,7},{6,4},{7,5},{8,10},{9,11},{10,... | collective-permute-start | bytes 319496 | tf_op jit(solution)/shard_map/ppermute | solution.py:305
  6.1 23.0 %collective-permute-start.2 = (bf16[208,256]{1,0:T(8,128)(2,1)S(1)}, bf16[208,256]{1,0:T(8,128)(2,1)S(1)}, u32[]{:S(2)}, u32[]{:S(2)}) collective-permute-start(bf16[208,256]{1,0:T(8,128)(2,1)S(1)} %get-tuple-element.38), channel_id=1, source_target_pairs={{0,3},{1,2},{2,1},{3,0},{4,7},{5,6},{6,5},{7,4},{8,11},{9,10},{10,... | collective-permute-start | bytes 319496 | tf_op jit(solution)/shard_map/ppermute | solution.py:305
  10.2 18.9 %copy-start.1 = (bf16[2,256,768]{2,1,0:T(8,128)(2,1)S(1)}, bf16[2,256,768]{2,1,0:T(8,128)(2,1)}, u32[]{:S(2)}) copy-start(bf16[2,256,768]{2,1,0:T(8,128)(2,1)} %qkv_ref.5) | copy-start | bytes 2359300
  26.9 10.7 %collective-permute-start.3 = (bf16[192,256]{1,0:T(8,128)(2,1)S(1)}, bf16[192,256]{1,0:T(8,128)(2,1)S(1)}, u32[]{:S(2)}, u32[]{:S(2)}) collective-permute-start(bf16[192,256]{1,0:T(8,128)(2,1)S(1)} %get-tuple-element.47), channel_id=1, source_target_pairs={{0,1},{1,0},{2,3},{3,2},{4,5},{5,4},{6,7},{7,6},{8,9},{9,8},{10,11... | collective-permute-start | bytes 294920 | tf_op jit(solution)/shard_map/ppermute | solution.py:305
  27.1 10.5 %collective-permute-start.4 = (bf16[192,256]{1,0:T(8,128)(2,1)S(1)}, bf16[192,256]{1,0:T(8,128)(2,1)S(1)}, u32[]{:S(2)}, u32[]{:S(2)}) collective-permute-start(bf16[192,256]{1,0:T(8,128)(2,1)S(1)} %get-tuple-element.48), channel_id=1, source_target_pairs={{0,2},{1,3},{2,0},{3,1},{4,6},{5,7},{6,4},{7,5},{8,10},{9,11},{10,... | collective-permute-start | bytes 294920 | tf_op jit(solution)/shard_map/ppermute | solution.py:305
  29.1 8.5 %collective-permute-start.5 = (bf16[192,256]{1,0:T(8,128)(2,1)S(1)}, bf16[192,256]{1,0:T(8,128)(2,1)S(1)}, u32[]{:S(2)}, u32[]{:S(2)}) collective-permute-start(bf16[192,256]{1,0:T(8,128)(2,1)S(1)} %get-tuple-element.49), channel_id=1, source_target_pairs={{0,3},{1,2},{2,1},{3,0},{4,7},{5,6},{6,5},{7,4},{8,11},{9,10},{10,... | collective-permute-start | bytes 294920 | tf_op jit(solution)/shard_map/ppermute | solution.py:305
  48.5 2.0 %collective-permute-start.9 = (bf16[4,256,256]{2,1,0:T(8,128)(2,1)S(1)}, bf16[4,256,256]{2,1,0:T(8,128)(2,1)S(1)}, u32[]{:S(2)}, u32[]{:S(2)}) collective-permute-start(bf16[4,256,256]{2,1,0:T(8,128)(2,1)S(1)} %get-tuple-element.56), channel_id=1, source_target_pairs={{0,1},{1,0},{2,3},{3,2},{4,5},{5,4},{6,7},{7,6},{8,9},{9,8},{10,11... | collective-permute-start | bytes 1572872 | tf_op jit(solution)/shard_map/ppermute | solution.py:305
  50.6 6.0 %collective-permute-start.10 = (bf16[1,256,256]{2,1,0:T(8,128)(2,1)S(1)}, bf16[1,256,256]{2,1,0:T(8,128)(2,1)S(1)}, u32[]{:S(2)}, u32[]{:S(2)}) collective-permute-start(bf16[1,256,256]{2,1,0:T(8,128)(2,1)S(1)} %get-tuple-element.58), channel_id=1, source_target_pairs={{0,2},{1,3},{2,0},{3,1},{4,6},{5,7},{6,4},{7,5},{8,10},{9,11},{10,... | collective-permute-start | bytes 393224 | tf_op jit(solution)/shard_map/ppermute | solution.py:305
  52.4 8.3 %collective-permute-start.11 = (bf16[1,256,256]{2,1,0:T(8,128)(2,1)S(1)}, bf16[1,256,256]{2,1,0:T(8,128)(2,1)S(1)}, u32[]{:S(2)}, u32[]{:S(2)}) collective-permute-start(bf16[1,256,256]{2,1,0:T(8,128)(2,1)S(1)} %get-tuple-element.59), channel_id=1, source_target_pairs={{0,4},{1,5},{2,6},{3,7},{4,0},{5,1},{6,2},{7,3},{8,12},{9,13},{10,... | collective-permute-start | bytes 393224 | tf_op jit(solution)/shard_map/ppermute | solution.py:305
  54.0 6.8 %collective-permute-start.12 = (bf16[1,256,256]{2,1,0:T(8,128)(2,1)S(1)}, bf16[1,256,256]{2,1,0:T(8,128)(2,1)S(1)}, u32[]{:S(2)}, u32[]{:S(2)}) collective-permute-start(bf16[1,256,256]{2,1,0:T(8,128)(2,1)S(1)} %get-tuple-element.60), channel_id=1, source_target_pairs={{0,6},{1,7},{2,4},{3,5},{4,2},{5,3},{6,0},{7,1},{8,14},{9,15},{10,... | collective-permute-start | bytes 393224 | tf_op jit(solution)/shard_map/ppermute | solution.py:305
  60.8 8.3 %collective-permute-start.15 = (bf16[1,256,256]{2,1,0:T(8,128)(2,1)S(1)}, bf16[1,256,256]{2,1,0:T(8,128)(2,1)S(1)}, u32[]{:S(2)}, u32[]{:S(2)}) collective-permute-start(bf16[1,256,256]{2,1,0:T(8,128)(2,1)S(1)} %shard_map.92.rest_0_), channel_id=1, source_target_pairs={{0,24},{1,25},{2,26},{3,27},{4,28},{5,29},{6,30},{7,31},{8,16},{9,... | collective-permute-start | bytes 393224 | tf_op jit(solution)/shard_map/ppermute | solution.py:305
  64.5 10.4 %collective-permute-start.14 = (bf16[1,256,256]{2,1,0:T(8,128)(2,1)S(1)}, bf16[1,256,256]{2,1,0:T(8,128)(2,1)S(1)}, u32[]{:S(2)}, u32[]{:S(2)}) collective-permute-start(bf16[1,256,256]{2,1,0:T(8,128)(2,1)S(1)} %shard_map.92.rest_0_), channel_id=1, source_target_pairs={{0,16},{1,17},{2,18},{3,19},{4,20},{5,21},{6,22},{7,23},{8,24},{9,... | collective-permute-start | bytes 393224 | tf_op jit(solution)/shard_map/ppermute | solution.py:305
  64.5 10.4 %collective-permute-start.13 = (bf16[1,256,256]{2,1,0:T(8,128)(2,1)S(1)}, bf16[1,256,256]{2,1,0:T(8,128)(2,1)S(1)}, u32[]{:S(2)}, u32[]{:S(2)}) collective-permute-start(bf16[1,256,256]{2,1,0:T(8,128)(2,1)S(1)} %shard_map.92.rest_0_), channel_id=1, source_target_pairs={{0,8},{1,9},{2,10},{3,11},{4,12},{5,13},{6,14},{7,15},{8,0},{9,1},... | collective-permute-start | bytes 393224 | tf_op jit(solution)/shard_map/ppermute | solution.py:305
  66.1 14.0 %collective-permute-start.6 = (bf16[192,256]{1,0:T(8,128)(2,1)S(1)}, bf16[192,256]{1,0:T(8,128)(2,1)S(1)}, u32[]{:S(2)}, u32[]{:S(2)}) collective-permute-start(bf16[192,256]{1,0:T(8,128)(2,1)S(1)} %get-tuple-element.52), channel_id=1, source_target_pairs={{0,1},{1,0},{2,3},{3,2},{4,5},{5,4},{6,7},{7,6},{8,9},{9,8},{10,11... | collective-permute-start | bytes 294920 | tf_op jit(solution)/shard_map/ppermute | solution.py:305
  74.9 11.7 %collective-permute-start.18 = (bf16[1,256,256]{2,1,0:T(8,128)(2,1)S(1)}, bf16[1,256,256]{2,1,0:T(8,128)(2,1)S(1)}, u32[]{:S(2)}, u32[]{:S(2)}) collective-permute-start(bf16[1,256,256]{2,1,0:T(8,128)(2,1)S(1)} %shard_map.93.rest_0_), channel_id=1, source_target_pairs={{0,6},{1,7},{2,4},{3,5},{4,2},{5,3},{6,0},{7,1},{8,14},{9,15},{10,... | collective-permute-start | bytes 393224 | tf_op jit(solution)/shard_map/ppermute | solution.py:305
  76.6 10.5 %collective-permute-start.17 = (bf16[1,256,256]{2,1,0:T(8,128)(2,1)S(1)}, bf16[1,256,256]{2,1,0:T(8,128)(2,1)S(1)}, u32[]{:S(2)}, u32[]{:S(2)}) collective-permute-start(bf16[1,256,256]{2,1,0:T(8,128)(2,1)S(1)} %shard_map.93.rest_0_), channel_id=1, source_target_pairs={{0,4},{1,5},{2,6},{3,7},{4,0},{5,1},{6,2},{7,3},{8,12},{9,13},{10,... | collective-permute-start | bytes 393224 | tf_op jit(solution)/shard_map/ppermute | solution.py:305
  78.1 9.1 %collective-permute-start.16 = (bf16[1,256,256]{2,1,0:T(8,128)(2,1)S(1)}, bf16[1,256,256]{2,1,0:T(8,128)(2,1)S(1)}, u32[]{:S(2)}, u32[]{:S(2)}) collective-permute-start(bf16[1,256,256]{2,1,0:T(8,128)(2,1)S(1)} %shard_map.93.rest_0_), channel_id=1, source_target_pairs={{0,2},{1,3},{2,0},{3,1},{4,6},{5,7},{6,4},{7,5},{8,10},{9,11},{10,... | collective-permute-start | bytes 393224 | tf_op jit(solution)/shard_map/ppermute | solution.py:305
  78.5 8.1 %collective-permute-start.7 = (bf16[192,256]{1,0:T(8,128)(2,1)S(1)}, bf16[192,256]{1,0:T(8,128)(2,1)S(1)}, u32[]{:S(2)}, u32[]{:S(2)}) collective-permute-start(bf16[192,256]{1,0:T(8,128)(2,1)S(1)} %get-tuple-element.53), channel_id=1, source_target_pairs={{0,2},{1,3},{2,0},{3,1},{4,6},{5,7},{6,4},{7,5},{8,10},{9,11},{10,... | collective-permute-start | bytes 294920 | tf_op jit(solution)/shard_map/ppermute | solution.py:305
  80.1 7.5 %collective-permute-start.8 = (bf16[192,256]{1,0:T(8,128)(2,1)S(1)}, bf16[192,256]{1,0:T(8,128)(2,1)S(1)}, u32[]{:S(2)}, u32[]{:S(2)}) collective-permute-start(bf16[192,256]{1,0:T(8,128)(2,1)S(1)} %get-tuple-element.54), channel_id=1, source_target_pairs={{0,3},{1,2},{2,1},{3,0},{4,7},{5,6},{6,5},{7,4},{8,11},{9,10},{10,... | collective-permute-start | bytes 294920 | tf_op jit(solution)/shard_map/ppermute | solution.py:305
  86.6 2.2 %collective-permute-start.19 = (bf16[1,256,256]{2,1,0:T(8,128)(2,1)S(1)}, bf16[1,256,256]{2,1,0:T(8,128)(2,1)S(1)}, u32[]{:S(2)}, u32[]{:S(2)}) collective-permute-start(bf16[1,256,256]{2,1,0:T(8,128)(2,1)S(1)} %shard_map.93.rest_0_), channel_id=1, source_target_pairs={{0,1},{1,0},{2,3},{3,2},{4,5},{5,4},{6,7},{7,6},{8,9},{9,8},{10,11... | collective-permute-start | bytes 393224 | tf_op jit(solution)/shard_map/ppermute | solution.py:305
  86.6 2.2 %collective-permute-start.22 = (bf16[1,256,256]{2,1,0:T(8,128)(2,1)S(1)}, bf16[1,256,256]{2,1,0:T(8,128)(2,1)S(1)}, u32[]{:S(2)}, u32[]{:S(2)}) collective-permute-start(bf16[1,256,256]{2,1,0:T(8,128)(2,1)S(1)} %collective-permute-done.18.rest_3_), channel_id=1, source_target_pairs={{0,1},{1,0},{2,3},{3,2},{4,5},{5,4},{6,7},{7,6},{8,9},{9,8},{10,11... | collective-permute-start | bytes 393224 | tf_op jit(solution)/shard_map/ppermute | solution.py:305
  87.1 1.7 %collective-permute-start.21 = (bf16[1,256,256]{2,1,0:T(8,128)(2,1)S(1)}, bf16[1,256,256]{2,1,0:T(8,128)(2,1)S(1)}, u32[]{:S(2)}, u32[]{:S(2)}) collective-permute-start(bf16[1,256,256]{2,1,0:T(8,128)(2,1)S(1)} %collective-permute-done.17.rest_2_), channel_id=1, source_target_pairs={{0,1},{1,0},{2,3},{3,2},{4,5},{5,4},{6,7},{7,6},{8,9},{9,8},{10,11... | collective-permute-start | bytes 393224 | tf_op jit(solution)/shard_map/ppermute | solution.py:305
  87.2 1.7 %collective-permute-start.20 = (bf16[1,256,256]{2,1,0:T(8,128)(2,1)S(1)}, bf16[1,256,256]{2,1,0:T(8,128)(2,1)S(1)}, u32[]{:S(2)}, u32[]{:S(2)}) collective-permute-start(bf16[1,256,256]{2,1,0:T(8,128)(2,1)S(1)} %collective-permute-done.16.rest_1_), channel_id=1, source_target_pairs={{0,1},{1,0},{2,3},{3,2},{4,5},{5,4},{6,7},{7,6},{8,9},{9,8},{10,11... | collective-permute-start | bytes 393224 | tf_op jit(solution)/shard_map/ppermute | solution.py:305
  (7 other events, 14.1 us)

commit v3 on v2

--- a/solution.py
+++ b/solution.py
@@ -11,7 +11,8 @@
 LOG2E = 1.4426950408889634
 f32, bf16, i32 = jnp.float32, jnp.bfloat16, jnp.int32
 AXES = ("wide", "narrow")
-VMEM_LIMIT = 28 * 2**20
+VMEM_LIMIT = 40 * 2**20
+TOGETHER = 4
 
 
 def shape(dims, dtype):
@@ -24,12 +25,16 @@
     )
 
 
-def call(body, out_shape, args, scratch=(), us=1):
+def call(body, out_shape, args, scratch=(), us=1, in_hbm=0):
+    args = list(args)
+    for i in range(len(args) - in_hbm, len(args)):
+        args[i] = pltpu.with_memory_space_constraint(args[i], pltpu.HBM)
     return pl.pallas_call(
         body,
         out_shape=tuple(out_shape),
         in_specs=[pl.BlockSpec(memory_space=pltpu.SMEM)]
-        + [pl.BlockSpec(memory_space=pltpu.VMEM)] * (len(args) - 1),
+        + [pl.BlockSpec(memory_space=pltpu.VMEM)] * (len(args) - 1 - in_hbm)
+        + [pl.BlockSpec(memory_space=pltpu.HBM)] * in_hbm,
         out_specs=tuple([pl.BlockSpec(memory_space=pltpu.VMEM)] * len(out_shape)),
         scratch_shapes=list(scratch),
         compiler_params=pltpu.CompilerParams(vmem_limit_bytes=VMEM_LIMIT),
@@ -54,7 +59,18 @@
     return spot.astype(i32)
 
 
-def route_kernel(group, cap, me_ref, tz_ref, rows_ref, slots_ref, *send_refs):
+def route_kernel(group, cap, me_ref, tz_hbm, rows_hbm, h_hbm, g_hbm, qkv_hbm, out_hbm, *rest):
+    slots_ref, send_refs = rest[0], rest[1 : 1 + group]
+    tz_ref, rows_ref, sems = rest[5 + group :]
+    sources = (tz_hbm, rows_hbm, h_hbm, g_hbm, qkv_hbm, out_hbm)
+    targets = (tz_ref, rows_ref) + tuple(rest[1 + group : 5 + group])
+    copies = [
+        pltpu.make_async_copy(a, b, sems.at[i]) for i, (a, b) in enumerate(zip(sources, targets))
+    ]
+    for copy in copies:
+        copy.start()
+    copies[0].wait()
+    copies[1].wait()
     n, channels = rows_ref.shape
     here = me_ref[0] % group
     target = tz_ref[...]
@@ -82,6 +98,8 @@
         if cap < channels:
             where = jnp.concatenate([where, jnp.zeros((16, channels - cap), f32)], axis=1)
         send_refs[s][cap : cap + 16, :] = where.astype(bf16)
+    for copy in copies[2:]:
+        copy.wait()
 
 
 def two_terms(x):
@@ -89,7 +107,7 @@
     return jnp.concatenate([high, (x - high.astype(f32)).astype(bf16)], axis=0)
 
 
-def forward_heads(heads, channels, size, proj, powers_ref, att_ref, inv_ref):
+def forward_heads(heads, kept, channels, size, proj, powers_ref, att_ref, inv_ref):
     every = range(len(heads))
     at = [pl.multiple_of(h * size, size) for h in heads]
     q = [proj[pl.ds(r, size), :] for r in at]
@@ -104,12 +122,14 @@
     inverse = [1.0 / jnp.sum(x, axis=0, keepdims=True) for x in powers]
     attended = [dg(v[i], half[i], 1, 0) * inverse[i] for i in every]
     for i in every:
-        powers_ref[heads[i]] = half[i]
+        powers_ref[kept[i]] = half[i]
         inv_ref[pl.ds(heads[i], 1), :] = inverse[i]
         att_ref[pl.ds(at[i], size), :] = attended[i]
 
 
-def backward_heads(heads, channels, size, proj, out_delta, powers_ref, att_ref, inv_ref, delta):
+def backward_heads(
+    heads, kept, channels, size, proj, out_delta, powers_ref, att_ref, inv_ref, delta, turned_ref
+):
     every = range(len(heads))
     at = [pl.multiple_of(h * size, size) for h in heads]
     q = [proj[pl.ds(r, size), :] for r in at]
@@ -117,7 +137,7 @@
     v = [proj[pl.ds(2 * channels + r, size), :] for r in at]
     o = [out_delta[pl.ds(r, size), :].astype(f32) for r in at]
     inverse = [inv_ref[pl.ds(h, 1), :] for h in heads]
-    half = [powers_ref[h] for h in heads]
+    half = [powers_ref[x] for x in kept]
     centre = [
         jnp.sum(att_ref[pl.ds(at[i], size), :] * o[i], axis=0, keepdims=True) * inverse[i]
         for i in every
@@ -127,9 +147,13 @@
     score_grad = [
         (half[i].astype(f32) * (dg(v[i], o[i], 0, 0) - centre[i])).astype(bf16) for i in every
     ]
-    value = [dg(o[i], half[i], 1, 1) for i in every]
+    for i in every:
+        turned_ref[0, i] = half[i].T
+    value = [dg(o[i], turned_ref[0, i], 1, 0) for i in every]
     query = [dg(k[i], score_grad[i], 1, 0) for i in every]
-    key = [dg(q[i], score_grad[i], 1, 1) for i in every]
+    for i in every:
+        turned_ref[1, i] = score_grad[i].T
+    key = [dg(q[i], turned_ref[1, i], 1, 0) for i in every]
     scale = size**-0.5
     for i in every:
         delta[pl.ds(at[i], size), :] = (query[i] * scale).astype(bf16)
@@ -137,18 +161,18 @@
         delta[pl.ds(2 * channels + at[i], size), :] = (value[i][0:size] + value[i][size:]).astype(bf16)
 
 
-def loop_heads(steps, per, body):
+def loop_heads(body):
     def step(i, carry):
-        body([i * per + u for u in range(per)])
+        body([i * TOGETHER + u for u in range(TOGETHER)])
         return carry
 
-    lax.fori_loop(0, steps // per, step, 0)
+    lax.fori_loop(0, HEADS // TOGETHER, step, 0)
 
 
 def late_kernel(group, cap, me_ref, h_ref, g_ref, qkv_ref, out_ref, slots_ref, *rest):
     mid_ref, sums_ref = rest[0], rest[1]
     send_refs = rest[2 : 2 + group]
-    proj, delta, powers_ref, att_ref, inv_ref = rest[2 + group :]
+    proj, delta, powers_ref, att_ref, inv_ref, turned_ref = rest[2 + group :]
     h, g = h_ref[...], g_ref[...]
     n, channels = h.shape
     size = channels // HEADS
@@ -158,10 +182,23 @@
     out_delta = proj.at[3 * channels : 4 * channels, :]
 
     def body(heads):
-        forward_heads(heads, channels, size, proj, powers_ref, att_ref, inv_ref)
-        backward_heads(heads, channels, size, proj, out_delta, powers_ref, att_ref, inv_ref, delta)
-
-    loop_heads(HEADS, 2, body)
+        kept = range(TOGETHER)
+        forward_heads(heads, kept, channels, size, proj, powers_ref, att_ref, inv_ref)
+        backward_heads(
+            heads,
+            kept,
+            channels,
+            size,
+            proj,
+            out_delta,
+            powers_ref,
+            att_ref,
+            inv_ref,
+            delta,
+            turned_ref,
+        )
+
+    loop_heads(body)
     qkv_delta = delta[...]
     row_grad = dg(qkv_w, qkv_delta, 1, 0).T
     mid = (g.astype(f32) + row_grad).astype(bf16)
@@ -192,16 +229,16 @@
     h_ref[...] = h
     proj[...] = dg(qkv_ref[0], h, 0, 1).astype(bf16)
     loop_heads(
-        HEADS,
-        2,
-        lambda heads: forward_heads(heads, channels, size, proj, powers_ref, att_ref, inv_ref),
+        lambda heads: forward_heads(
+            heads, heads, channels, size, proj, powers_ref, att_ref, inv_ref
+        )
     )
 
 
 def backward_kernel(group, cap, blocks, me_ref, out_ref, h_ref, proj, powers_ref, att_ref, inv_ref, spots_ref, late_ref, *rest):
     grads_refs = rest[0:group]
     delta, keep_ref, send_ref = rest[group : group + 3]
-    out_delta = rest[group + 3]
+    out_delta, turned_ref = rest[group + 3 :]
     n, channels = h_ref.shape
     size = channels // HEADS
     g = jnp.zeros((n, channels), f32)
@@ -210,11 +247,19 @@
     g = g.astype(bf16)
     out_delta[...] = dg(out_ref[0], g, 1, 1).astype(bf16)
     loop_heads(
-        HEADS,
-        2,
         lambda heads: backward_heads(
-            heads, channels, size, proj, out_delta, powers_ref, att_ref, inv_ref, delta
-        ),
+            heads,
+            heads,
+            channels,
+            size,
+            proj,
+            out_delta,
+            powers_ref,
+            att_ref,
+            inv_ref,
+            delta,
+            turned_ref,
+        )
     )
     me = me_ref[0]
     h = h_ref[...]
@@ -332,27 +377,40 @@
 
     size_rows = shape((n, channels), bf16)
     size_send = shape((cap, channels), bf16)
+    turned = pltpu.VMEM((2, TOGETHER, n, n), bf16)
     powers_s, att_s, inv_s = (HEADS, n, n), (channels, n), (HEADS, n)
     chunk = (2 * 4 * channels // blocks, channels)
 
-    slots, *feats = call(
+    moved = [mid_features, out_grad, qkv_weight, out_weight]
+    slots, *rest = call(
         partial(route_kernel, group, cap),
-        [shape((1, n), i32)] + [shape((cap + 16, channels), bf16)] * group,
-        [me, to_zorder.reshape(1, n), section_input],
-    )
-    feats = exchange(feats, devices)
+        [shape((1, n), i32)]
+        + [shape((cap + 16, channels), bf16)] * group
+        + [shape(x.shape, bf16) for x in moved],
+        [me, to_zorder.reshape(1, n), section_input] + moved,
+        [
+            pltpu.VMEM((1, n), i32),
+            pltpu.VMEM((n, channels), bf16),
+            pltpu.SemaphoreType.DMA((6,)),
+        ],
+        us=2,
+        in_hbm=6,
+    )
+    feats = exchange(rest[:group], devices)
+    mid_features, out_grad, qkv_w, out_w = rest[group:]
     mid, late_sums, *grads = call(
         partial(late_kernel, group, cap),
         [size_rows, shape((4 * channels, channels), bf16)] + [size_send] * group,
-        [me, mid_features, out_grad, qkv_weight, out_weight, slots],
+        [me, mid_features, out_grad, qkv_w, out_w, slots],
         [
             pltpu.VMEM((4 * channels, n), bf16),
             pltpu.VMEM((3 * channels, n), bf16),
-            pltpu.VMEM(powers_s, bf16),
+            pltpu.VMEM((TOGETHER, n, n), bf16),
             pltpu.VMEM(att_s, f32),
             pltpu.VMEM(inv_s, f32),
+            turned,
         ],
-        us=18,
+        us=16,
     )
     grads = exchange(grads, devices)
     h, proj, powers, att, inv, spots = call(
@@ -365,7 +423,7 @@
             shape(inv_s, f32),
             shape((group, 1, cap), i32),
         ],
-        [me, qkv_weight, *feats],
+        [me, qkv_w, *feats],
         us=8,
     )
     delta, keep, send = call(
@@ -375,15 +433,15 @@
             shape((blocks // 2,) + chunk, bf16),
             shape((blocks // 2,) + chunk, bf16),
         ],
-        [place, out_weight, h, proj, powers, att, inv, spots, late_sums, *grads],
-        [pltpu.VMEM((channels, n), bf16)],
-        us=10,
+        [place, out_w, h, proj, powers, att, inv, spots, late_sums, *grads],
+        [pltpu.VMEM((channels, n), bf16), turned],
+        us=9,
     )
     got = swap(send, 1, devices)
     backs = call(
         partial(rows_kernel, group, cap),
         [size_send] * group,
-        [me, qkv_weight, delta, spots],
+        [me, qkv_w, delta, spots],
         us=2,
     )
     pieces = add_parts(me, [keep, got], 4)
@@ -394,11 +452,12 @@
     for stage in whole_stages:
         parts = [total] + [swap(total, m, devices) for m in stage_masks(stage)[1:]]
         (total,) = add_parts(me, parts, 1)
+    (input_grad,) = call(
+        partial(join_kernel, group, cap), [size_rows], [me, slots, mid, *backs]
+    )
+    total, input_grad = lax.optimization_barrier((total, input_grad))
     parts = [total] + [swap(total, m, devices) for m in masks[1:]]
     parts = parts + [swap(x, 1, devices) for x in parts]
-    (input_grad,) = call(
-        partial(join_kernel, group, cap), [size_rows], [me, slots, mid, *backs]
-    )
     qkv_grad, out_w_grad = call(
         partial(finish_kernel, float((n * devices) ** -0.5)),
         [shape(qkv_weight.shape, f32), shape(out_weight.shape, f32)],

time: 91 us -> 76.7 us (0.84)
  local copies, waits for them, and re-layouts: 5.62 us -> 0 us
  Pallas kernels: 41 us -> 36.7 us
  waiting for transfers between devices: 23.4 us -> 19.4 us
    unnamed x16 -> x0, local copies, waits for them, and re-layouts: 5.62 us -> none
    pallas_call x10, Pallas kernels: 41 us -> 36.7 us  [call(): pl.pallas_call(body, out_shape=tuple(out_shape), in_specs=[pl.BlockSpec(m...]
    ppermute x23, waiting for transfers between devices: 23.4 us -> 19.4 us  [swap(): return lax.ppermute(x, AXES, [(d, d ^ mask) for d in range(devices)])]
  transfers between devices with their start and end apart: 23 -> 23, of which waited for: 6 -> 10; matrix products, arithmetic and copies ran while one was open for 0% -> 0% of each run, Pallas kernels for 30% -> 30%
where the time goes in v3:
time: 76.7 us; the launch traced here: 76.6 us
  Pallas kernels  36.7 us (48%)
  starting transfers between devices  19.8 us (26%)
  waiting for transfers between devices  19.4 us (25%)
    pallas_call x10, Pallas kernels, call(): pl.pallas_call(body, out_shape=tuple(out_shape), in_specs=[pl.BlockSpec(m...  36.7 us
    ppermute x23, starting transfers between devices, swap(): return lax.ppermute(x, AXES, [(d, d ^ mask) for d in range(devices)])  19.8 us
    ppermute x23, waiting for transfers between devices, swap(): return lax.ppermute(x, AXES, [(d, d ^ mask) for d in range(devices)])  19.4 us
  transfers between devices with their start and end apart: 23, of which 10 were waited for; matrix products, arithmetic and copies ran while one was open for 0% of the time, Pallas kernels for 30%

profile of v3, /device:TPU:0, one launch (start us, length us, event | category | flops | bytes accessed | tf_op | source)
XLA Modules:
  0.0 76.6 jit_solution(14140157718243874339)
XLA Ops:
  0.6 1.8 %shard_map.85 = (s32[1,512]{1,0:T(1,128)S(1)}, bf16[208,256]{1,0:T(8,128)(2,1)S(1)}, bf16[208,256]{1,0:T(8,128)(2,1)S(1)}, bf16[208,256]{1,0:T(8,128)(2,1)S(1)},...) custom-call(s32[1]{0:T(128)} %bitcast.me_ref, ...), custom_call_target="tpu_custom_call" | custom-call | flops 2000000000 | bytes 1048576 | tf_op jit(solution)/shard_map/pallas_call | solution.py:32
  2.9 2.6 %collective-permute-start.1 = (bf16[208,256]{1,0:T(8,128)(2,1)S(1)}, bf16[208,256]{1,0:T(8,128)(2,1)S(1)}, u32[]{:S(2)}, u32[]{:S(2)}) collective-permute-start(bf16[208,256]{1,0:T(8,128)(2,1)S(1)} %get-tuple-element.43), channel_id=1, source_target_pairs={{0,2},{1,3},{2,0},{3,1},{4,6},{5,7},{6,4},{7,5},{8,10},{9,11},{10,... | collective-permute-start | bytes 319496 | tf_op jit(solution)/shard_map/ppermute | solution.py:350
  5.6 13.4 %shard_map.87 = (bf16[512,256]{1,0:T(8,128)(2,1)S(1)}, bf16[1024,256]{1,0:T(8,128)(2,1)S(1)}, bf16[192,256]{1,0:T(8,128)(2,1)S(1)}, bf16[192,256]{1,0:T(8,128)(2...) custom-call(s32[1]{0:T(128)} %bitcast.me_ref, bf16[512,256]{1,0:T(8,128)(2,1)S(1)} %get-tuple-element.51.h_ref, ...), custom_call_target="tpu_custom_call" | custom-call | flops 16000000000 | bytes 1048576 | tf_op jit(solution)/shard_map/pallas_call | solution.py:32
  19.2 1.9 %collective-permute-start.4 = (bf16[192,256]{1,0:T(8,128)(2,1)S(1)}, bf16[192,256]{1,0:T(8,128)(2,1)S(1)}, u32[]{:S(2)}, u32[]{:S(2)}) collective-permute-start(bf16[192,256]{1,0:T(8,128)(2,1)S(1)} %get-tuple-element.57), channel_id=1, source_target_pairs={{0,2},{1,3},{2,0},{3,1},{4,6},{5,7},{6,4},{7,5},{8,10},{9,11},{10,... | collective-permute-start | bytes 294920 | tf_op jit(solution)/shard_map/ppermute | solution.py:350
  21.2 7.5 %shard_map.86 = (bf16[512,256]{1,0:T(8,128)(2,1)S(1)}, bf16[768,512]{1,0:T(8,128)(2,1)S(1)}, bf16[16,512,512]{2,1,0:T(8,128)(2,1)S(1)}, f32[256,512]{1,0:T(8,128...) custom-call(s32[1]{0:T(128)} %bitcast.me_ref, bf16[2,256,768]{2,1,0:T(8,128)(2,1)S(1)} %get-tuple-element.40.qkv_ref, ...), custom_call_target="tpu_custom_call" | custom-call | flops 8000000000 | bytes 1048576 | tf_op jit(solution)/shard_map/pallas_call | solution.py:32
  28.7 9.9 %shard_map.88 = (bf16[768,512]{1,0:T(8,128)(2,1)S(1)}, bf16[4,256,256]{2,1,0:T(8,128)(2,1)S(1)}, bf16[4,256,256]{2,1,0:T(8,128)(2,1)S(1)}) custom-call(s32[1]{0:T(128)} %bitcast.1.me_ref, bf16[2,256,256]{2,1,0:T(8,128)(2,1)S(1)} %get-tuple-element.39.out_ref, bf16[512,256]{1,0:T(8,128)(2,1)S(1)} %get-tuple-element.45.h_ref, ...), custom_call_target="tpu_custom_call" | custom-call | flops 8999999488 | bytes 1048576 | tf_op jit(solution)/shard_map/pallas_call | solution.py:32
  38.9 1.7 %collective-permute-done.6.rest_1_ = bf16[4,256,256]{2,1,0:T(8,128)(2,1)S(1)} collective-permute-done((bf16[4,256,256]{2,1,0:T(8,128)(2,1)S(1)}, bf16[4,256,256]{2,1,0:T(8,128)(2,1)S(1)}, u32[]{:S(2)}, u32[]{:S(2)}) %collective-permute-start.6) | collective-permute-done | bytes 524320 | tf_op jit(solution)/shard_map/ppermute | solution.py:350
  40.7 1.8 %collective-permute-start.7 = (bf16[1,256,256]{2,1,0:T(8,128)(2,1)S(1)}, bf16[1,256,256]{2,1,0:T(8,128)(2,1)S(1)}, u32[]{:S(2)}, u32[]{:S(2)}) collective-permute-start(bf16[1,256,256]{2,1,0:T(8,128)(2,1)S(1)} %get-tuple-element.62), channel_id=1, source_target_pairs={{0,2},{1,3},{2,0},{3,1},{4,6},{5,7},{6,4},{7,5},{8,10},{9,11},{10,... | collective-permute-start | bytes 393224 | tf_op jit(solution)/shard_map/ppermute | solution.py:350
  42.5 1.5 %collective-permute-start.8 = (bf16[1,256,256]{2,1,0:T(8,128)(2,1)S(1)}, bf16[1,256,256]{2,1,0:T(8,128)(2,1)S(1)}, u32[]{:S(2)}, u32[]{:S(2)}) collective-permute-start(bf16[1,256,256]{2,1,0:T(8,128)(2,1)S(1)} %get-tuple-element.63), channel_id=1, source_target_pairs={{0,4},{1,5},{2,6},{3,7},{4,0},{5,1},{6,2},{7,3},{8,12},{9,13},{10,... | collective-permute-start | bytes 393224 | tf_op jit(solution)/shard_map/ppermute | solution.py:350
  44.2 0.9 %shard_map.92 = (bf16[192,256]{1,0:T(8,128)(2,1)S(1)}, bf16[192,256]{1,0:T(8,128)(2,1)S(1)}, bf16[192,256]{1,0:T(8,128)(2,1)S(1)}, bf16[192,256]{1,0:T(8,128)(2,1)S(1)}) custom-call(s32[1]{0:T(128)} %bitcast.me_ref, bf16[2,256,768]{2,1,0:T(8,128)(2,1)S(1)} %get-tuple-element.40.qkv_ref, bf16[768,512]{1,0:T(8,128)(2,1)S(1)} %get-tuple-element.66.delta, ...), custom_call_target="tpu_custom_call" | custom-call | flops 2000000000 | bytes 1048576 | tf_op jit(solution)/shard_map/pallas_call | solution.py:32
  45.2 1.9 %collective-permute-start.14 = (bf16[192,256]{1,0:T(8,128)(2,1)S(1)}, bf16[192,256]{1,0:T(8,128)(2,1)S(1)}, u32[]{:S(2)}, u32[]{:S(2)}) collective-permute-start(bf16[192,256]{1,0:T(8,128)(2,1)S(1)} %get-tuple-element.69), channel_id=1, source_target_pairs={{0,2},{1,3},{2,0},{3,1},{4,6},{5,7},{6,4},{7,5},{8,10},{9,11},{10,... | collective-permute-start | bytes 294920 | tf_op jit(solution)/shard_map/ppermute | solution.py:350
  47.4 2.8 %collective-permute-done.8.rest_2_ = bf16[1,256,256]{2,1,0:T(8,128)(2,1)S(1)} collective-permute-done((bf16[1,256,256]{2,1,0:T(8,128)(2,1)S(1)}, bf16[1,256,256]{2,1,0:T(8,128)(2,1)S(1)}, u32[]{:S(2)}, u32[]{:S(2)}) %collective-permute-start.8) | collective-permute-done | bytes 131104 | tf_op jit(solution)/shard_map/ppermute | solution.py:350
  50.2 1.1 %collective-permute-done.9.rest_3_ = bf16[1,256,256]{2,1,0:T(8,128)(2,1)S(1)} collective-permute-done((bf16[1,256,256]{2,1,0:T(8,128)(2,1)S(1)}, bf16[1,256,256]{2,1,0:T(8,128)(2,1)S(1)}, u32[]{:S(2)}, u32[]{:S(2)}) %collective-permute-start.9) | collective-permute-done | bytes 131104 | tf_op jit(solution)/shard_map/ppermute | solution.py:350
  51.4 3.7 %collective-permute-start.12 = (bf16[1,256,256]{2,1,0:T(8,128)(2,1)S(1)}, bf16[1,256,256]{2,1,0:T(8,128)(2,1)S(1)}, u32[]{:S(2)}, u32[]{:S(2)}) collective-permute-start(bf16[1,256,256]{2,1,0:T(8,128)(2,1)S(1)} %shard_map.90.rest_0_), channel_id=1, source_target_pairs={{0,24},{1,25},{2,26},{3,27},{4,28},{5,29},{6,30},{7,31},{8,16},{9,... | collective-permute-start | bytes 393224 | tf_op jit(solution)/shard_map/ppermute | solution.py:350
  55.1 0.8 %collective-permute-start.10 = (bf16[1,256,256]{2,1,0:T(8,128)(2,1)S(1)}, bf16[1,256,256]{2,1,0:T(8,128)(2,1)S(1)}, u32[]{:S(2)}, u32[]{:S(2)}) collective-permute-start(bf16[1,256,256]{2,1,0:T(8,128)(2,1)S(1)} %shard_map.90.rest_0_), channel_id=1, source_target_pairs={{0,8},{1,9},{2,10},{3,11},{4,12},{5,13},{6,14},{7,15},{8,0},{9,1},... | collective-permute-start | bytes 393224 | tf_op jit(solution)/shard_map/ppermute | solution.py:350
  55.9 1.2 %shard_map.93 = bf16[512,256]{1,0:T(8,128)(2,1)} custom-call(s32[1]{0:T(128)} %bitcast.me_ref, s32[1,512]{1,0:T(1,128)S(1)} %get-tuple-element.53.slots_ref, bf16[512,256]{1,0:T(8,128)(2,1)S(1)} %get-tuple-element.65.mid_ref, bf16[192,256]{1,0:T(8,128)(2,1)S(1)} %get-tuple-element.67.rest_0_, bf16[192,256]{1,0:T(8,128)(2,1)S(1)} %collective-permute-done.13.rest_1_, ...), custom_call_target="tpu_custom_call" | custom-call | flops 1000000000 | bytes 1048576 | tf_op jit(solution)/shard_map/pallas_call | solution.py:32
  57.1 2.4 %collective-permute-done.12.rest_3_ = bf16[1,256,256]{2,1,0:T(8,128)(2,1)S(1)} collective-permute-done((bf16[1,256,256]{2,1,0:T(8,128)(2,1)S(1)}, bf16[1,256,256]{2,1,0:T(8,128)(2,1)S(1)}, u32[]{:S(2)}, u32[]{:S(2)}) %collective-permute-start.12) | collective-permute-done | bytes 131104 | tf_op jit(solution)/shard_map/ppermute | solution.py:350
  59.5 5.4 %collective-permute-done.11.rest_2_ = bf16[1,256,256]{2,1,0:T(8,128)(2,1)S(1)} collective-permute-done((bf16[1,256,256]{2,1,0:T(8,128)(2,1)S(1)}, bf16[1,256,256]{2,1,0:T(8,128)(2,1)S(1)}, u32[]{:S(2)}, u32[]{:S(2)}) %collective-permute-start.11) | collective-permute-done | bytes 131104 | tf_op jit(solution)/shard_map/ppermute | solution.py:350
  65.0 1.8 %collective-permute-start.18 = (bf16[1,256,256]{2,1,0:T(8,128)(2,1)S(1)}, bf16[1,256,256]{2,1,0:T(8,128)(2,1)S(1)}, u32[]{:S(2)}, u32[]{:S(2)}) collective-permute-start(bf16[1,256,256]{2,1,0:T(8,128)(2,1)S(1)} %shard_map.91.rest_0_), channel_id=1, source_target_pairs={{0,6},{1,7},{2,4},{3,5},{4,2},{5,3},{6,0},{7,1},{8,14},{9,15},{10,... | collective-permute-start | bytes 393224 | tf_op jit(solution)/shard_map/ppermute | solution.py:350
  66.8 1.4 %collective-permute-start.17 = (bf16[1,256,256]{2,1,0:T(8,128)(2,1)S(1)}, bf16[1,256,256]{2,1,0:T(8,128)(2,1)S(1)}, u32[]{:S(2)}, u32[]{:S(2)}) collective-permute-start(bf16[1,256,256]{2,1,0:T(8,128)(2,1)S(1)} %shard_map.91.rest_0_), channel_id=1, source_target_pairs={{0,4},{1,5},{2,6},{3,7},{4,0},{5,1},{6,2},{7,3},{8,12},{9,13},{10,... | collective-permute-start | bytes 393224 | tf_op jit(solution)/shard_map/ppermute | solution.py:350
  68.5 3.7 %collective-permute-done.18.rest_3_ = bf16[1,256,256]{2,1,0:T(8,128)(2,1)S(1)} collective-permute-done((bf16[1,256,256]{2,1,0:T(8,128)(2,1)S(1)}, bf16[1,256,256]{2,1,0:T(8,128)(2,1)S(1)}, u32[]{:S(2)}, u32[]{:S(2)}) %collective-permute-start.18) | collective-permute-done | bytes 131104 | tf_op jit(solution)/shard_map/ppermute | solution.py:350
  72.2 0.9 %collective-permute-done.17.rest_2_ = bf16[1,256,256]{2,1,0:T(8,128)(2,1)S(1)} collective-permute-done((bf16[1,256,256]{2,1,0:T(8,128)(2,1)S(1)}, bf16[1,256,256]{2,1,0:T(8,128)(2,1)S(1)}, u32[]{:S(2)}, u32[]{:S(2)}) %collective-permute-start.17) | collective-permute-done | bytes 131104 | tf_op jit(solution)/shard_map/ppermute | solution.py:350
  73.7 0.8 %collective-permute-done.21.rest_6_ = bf16[1,256,256]{2,1,0:T(8,128)(2,1)S(1)} collective-permute-done((bf16[1,256,256]{2,1,0:T(8,128)(2,1)S(1)}, bf16[1,256,256]{2,1,0:T(8,128)(2,1)S(1)}, u32[]{:S(2)}, u32[]{:S(2)}) %collective-permute-start.21) | collective-permute-done | bytes 131104 | tf_op jit(solution)/shard_map/ppermute | solution.py:350
  74.8 1.8 %shard_map.94 = (f32[2,256,768]{2,1,0:T(8,128)}, f32[2,256,256]{2,1,0:T(8,128)}) custom-call(s32[1]{0:T(128)} %bitcast.1.me_ref, bf16[1,256,256]{2,1,0:T(8,128)(2,1)S(1)} %shard_map.91.rest_0_, bf16[1,256,256]{2,1,0:T(8,128)(2,1)S(1)} %collective-permute-done.16.rest_1_, bf16[1,256,256]{2,1,0:T(8,128)(2,1)S(1)} %collective-permute-done.17.rest_2_, ...), custom_call_target="tpu_custom_call" | custom-call | flops 1000000000 | bytes 1048576 | tf_op jit(solution)/shard_map/pallas_call | solution.py:32
  (32 shorter events, 3.1 us)
Async XLA Ops:
  2.4 18.7 %collective-permute-start = (bf16[208,256]{1,0:T(8,128)(2,1)S(1)}, bf16[208,256]{1,0:T(8,128)(2,1)S(1)}, u32[]{:S(2)}, u32[]{:S(2)}) collective-permute-start(bf16[208,256]{1,0:T(8,128)(2,1)S(1)} %get-tuple-element.42), channel_id=1, source_target_pairs={{0,1},{1,0},{2,3},{3,2},{4,5},{5,4},{6,7},{7,6},{8,9},{9,8},{10,11... | collective-permute-start | bytes 319496 | tf_op jit(solution)/shard_map/ppermute | solution.py:350
  2.9 18.2 %collective-permute-start.1 = (bf16[208,256]{1,0:T(8,128)(2,1)S(1)}, bf16[208,256]{1,0:T(8,128)(2,1)S(1)}, u32[]{:S(2)}, u32[]{:S(2)}) collective-permute-start(bf16[208,256]{1,0:T(8,128)(2,1)S(1)} %get-tuple-element.43), channel_id=1, source_target_pairs={{0,2},{1,3},{2,0},{3,1},{4,6},{5,7},{6,4},{7,5},{8,10},{9,11},{10,... | collective-permute-start | bytes 319496 | tf_op jit(solution)/shard_map/ppermute | solution.py:350
  5.5 15.7 %collective-permute-start.2 = (bf16[208,256]{1,0:T(8,128)(2,1)S(1)}, bf16[208,256]{1,0:T(8,128)(2,1)S(1)}, u32[]{:S(2)}, u32[]{:S(2)}) collective-permute-start(bf16[208,256]{1,0:T(8,128)(2,1)S(1)} %get-tuple-element.44), channel_id=1, source_target_pairs={{0,3},{1,2},{2,1},{3,0},{4,7},{5,6},{6,5},{7,4},{8,11},{9,10},{10,... | collective-permute-start | bytes 319496 | tf_op jit(solution)/shard_map/ppermute | solution.py:350
  19.0 9.6 %collective-permute-start.3 = (bf16[192,256]{1,0:T(8,128)(2,1)S(1)}, bf16[192,256]{1,0:T(8,128)(2,1)S(1)}, u32[]{:S(2)}, u32[]{:S(2)}) collective-permute-start(bf16[192,256]{1,0:T(8,128)(2,1)S(1)} %get-tuple-element.56), channel_id=1, source_target_pairs={{0,1},{1,0},{2,3},{3,2},{4,5},{5,4},{6,7},{7,6},{8,9},{9,8},{10,11... | collective-permute-start | bytes 294920 | tf_op jit(solution)/shard_map/ppermute | solution.py:350
  19.2 9.4 %collective-permute-start.4 = (bf16[192,256]{1,0:T(8,128)(2,1)S(1)}, bf16[192,256]{1,0:T(8,128)(2,1)S(1)}, u32[]{:S(2)}, u32[]{:S(2)}) collective-permute-start(bf16[192,256]{1,0:T(8,128)(2,1)S(1)} %get-tuple-element.57), channel_id=1, source_target_pairs={{0,2},{1,3},{2,0},{3,1},{4,6},{5,7},{6,4},{7,5},{8,10},{9,11},{10,... | collective-permute-start | bytes 294920 | tf_op jit(solution)/shard_map/ppermute | solution.py:350
  21.1 7.5 %collective-permute-start.5 = (bf16[192,256]{1,0:T(8,128)(2,1)S(1)}, bf16[192,256]{1,0:T(8,128)(2,1)S(1)}, u32[]{:S(2)}, u32[]{:S(2)}) collective-permute-start(bf16[192,256]{1,0:T(8,128)(2,1)S(1)} %get-tuple-element.58), channel_id=1, source_target_pairs={{0,3},{1,2},{2,1},{3,0},{4,7},{5,6},{6,5},{7,4},{8,11},{9,10},{10,... | collective-permute-start | bytes 294920 | tf_op jit(solution)/shard_map/ppermute | solution.py:350
  38.6 2.0 %collective-permute-start.6 = (bf16[4,256,256]{2,1,0:T(8,128)(2,1)S(1)}, bf16[4,256,256]{2,1,0:T(8,128)(2,1)S(1)}, u32[]{:S(2)}, u32[]{:S(2)}) collective-permute-start(bf16[4,256,256]{2,1,0:T(8,128)(2,1)S(1)} %get-tuple-element.60), channel_id=1, source_target_pairs={{0,1},{1,0},{2,3},{3,2},{4,5},{5,4},{6,7},{7,6},{8,9},{9,8},{10,11... | collective-permute-start | bytes 1572872 | tf_op jit(solution)/shard_map/ppermute | solution.py:350
  40.7 6.4 %collective-permute-start.7 = (bf16[1,256,256]{2,1,0:T(8,128)(2,1)S(1)}, bf16[1,256,256]{2,1,0:T(8,128)(2,1)S(1)}, u32[]{:S(2)}, u32[]{:S(2)}) collective-permute-start(bf16[1,256,256]{2,1,0:T(8,128)(2,1)S(1)} %get-tuple-element.62), channel_id=1, source_target_pairs={{0,2},{1,3},{2,0},{3,1},{4,6},{5,7},{6,4},{7,5},{8,10},{9,11},{10,... | collective-permute-start | bytes 393224 | tf_op jit(solution)/shard_map/ppermute | solution.py:350
  42.5 7.7 %collective-permute-start.8 = (bf16[1,256,256]{2,1,0:T(8,128)(2,1)S(1)}, bf16[1,256,256]{2,1,0:T(8,128)(2,1)S(1)}, u32[]{:S(2)}, u32[]{:S(2)}) collective-permute-start(bf16[1,256,256]{2,1,0:T(8,128)(2,1)S(1)} %get-tuple-element.63), channel_id=1, source_target_pairs={{0,4},{1,5},{2,6},{3,7},{4,0},{5,1},{6,2},{7,3},{8,12},{9,13},{10,... | collective-permute-start | bytes 393224 | tf_op jit(solution)/shard_map/ppermute | solution.py:350
  44.0 7.3 %collective-permute-start.9 = (bf16[1,256,256]{2,1,0:T(8,128)(2,1)S(1)}, bf16[1,256,256]{2,1,0:T(8,128)(2,1)S(1)}, u32[]{:S(2)}, u32[]{:S(2)}) collective-permute-start(bf16[1,256,256]{2,1,0:T(8,128)(2,1)S(1)} %get-tuple-element.64), channel_id=1, source_target_pairs={{0,6},{1,7},{2,4},{3,5},{4,2},{5,3},{6,0},{7,1},{8,14},{9,15},{10,... | collective-permute-start | bytes 393224 | tf_op jit(solution)/shard_map/ppermute | solution.py:350
  45.1 10.0 %collective-permute-start.13 = (bf16[192,256]{1,0:T(8,128)(2,1)S(1)}, bf16[192,256]{1,0:T(8,128)(2,1)S(1)}, u32[]{:S(2)}, u32[]{:S(2)}) collective-permute-start(bf16[192,256]{1,0:T(8,128)(2,1)S(1)} %get-tuple-element.68), channel_id=1, source_target_pairs={{0,1},{1,0},{2,3},{3,2},{4,5},{5,4},{6,7},{7,6},{8,9},{9,8},{10,11... | collective-permute-start | bytes 294920 | tf_op jit(solution)/shard_map/ppermute | solution.py:350
  45.2 10.7 %collective-permute-start.14 = (bf16[192,256]{1,0:T(8,128)(2,1)S(1)}, bf16[192,256]{1,0:T(8,128)(2,1)S(1)}, u32[]{:S(2)}, u32[]{:S(2)}) collective-permute-start(bf16[192,256]{1,0:T(8,128)(2,1)S(1)} %get-tuple-element.69), channel_id=1, source_target_pairs={{0,2},{1,3},{2,0},{3,1},{4,6},{5,7},{6,4},{7,5},{8,10},{9,11},{10,... | collective-permute-start | bytes 294920 | tf_op jit(solution)/shard_map/ppermute | solution.py:350
  47.0 8.9 %collective-permute-start.15 = (bf16[192,256]{1,0:T(8,128)(2,1)S(1)}, bf16[192,256]{1,0:T(8,128)(2,1)S(1)}, u32[]{:S(2)}, u32[]{:S(2)}) collective-permute-start(bf16[192,256]{1,0:T(8,128)(2,1)S(1)} %get-tuple-element.70), channel_id=1, source_target_pairs={{0,3},{1,2},{2,1},{3,0},{4,7},{5,6},{6,5},{7,4},{8,11},{9,10},{10,... | collective-permute-start | bytes 294920 | tf_op jit(solution)/shard_map/ppermute | solution.py:350
  51.4 8.1 %collective-permute-start.12 = (bf16[1,256,256]{2,1,0:T(8,128)(2,1)S(1)}, bf16[1,256,256]{2,1,0:T(8,128)(2,1)S(1)}, u32[]{:S(2)}, u32[]{:S(2)}) collective-permute-start(bf16[1,256,256]{2,1,0:T(8,128)(2,1)S(1)} %shard_map.90.rest_0_), channel_id=1, source_target_pairs={{0,24},{1,25},{2,26},{3,27},{4,28},{5,29},{6,30},{7,31},{8,16},{9,... | collective-permute-start | bytes 393224 | tf_op jit(solution)/shard_map/ppermute | solution.py:350
  55.1 9.8 %collective-permute-start.11 = (bf16[1,256,256]{2,1,0:T(8,128)(2,1)S(1)}, bf16[1,256,256]{2,1,0:T(8,128)(2,1)S(1)}, u32[]{:S(2)}, u32[]{:S(2)}) collective-permute-start(bf16[1,256,256]{2,1,0:T(8,128)(2,1)S(1)} %shard_map.90.rest_0_), channel_id=1, source_target_pairs={{0,16},{1,17},{2,18},{3,19},{4,20},{5,21},{6,22},{7,23},{8,24},{9,... | collective-permute-start | bytes 393224 | tf_op jit(solution)/shard_map/ppermute | solution.py:350
  55.1 9.8 %collective-permute-start.10 = (bf16[1,256,256]{2,1,0:T(8,128)(2,1)S(1)}, bf16[1,256,256]{2,1,0:T(8,128)(2,1)S(1)}, u32[]{:S(2)}, u32[]{:S(2)}) collective-permute-start(bf16[1,256,256]{2,1,0:T(8,128)(2,1)S(1)} %shard_map.90.rest_0_), channel_id=1, source_target_pairs={{0,8},{1,9},{2,10},{3,11},{4,12},{5,13},{6,14},{7,15},{8,0},{9,1},... | collective-permute-start | bytes 393224 | tf_op jit(solution)/shard_map/ppermute | solution.py:350
  65.0 7.3 %collective-permute-start.18 = (bf16[1,256,256]{2,1,0:T(8,128)(2,1)S(1)}, bf16[1,256,256]{2,1,0:T(8,128)(2,1)S(1)}, u32[]{:S(2)}, u32[]{:S(2)}) collective-permute-start(bf16[1,256,256]{2,1,0:T(8,128)(2,1)S(1)} %shard_map.91.rest_0_), channel_id=1, source_target_pairs={{0,6},{1,7},{2,4},{3,5},{4,2},{5,3},{6,0},{7,1},{8,14},{9,15},{10,... | collective-permute-start | bytes 393224 | tf_op jit(solution)/shard_map/ppermute | solution.py:350
  66.8 6.4 %collective-permute-start.17 = (bf16[1,256,256]{2,1,0:T(8,128)(2,1)S(1)}, bf16[1,256,256]{2,1,0:T(8,128)(2,1)S(1)}, u32[]{:S(2)}, u32[]{:S(2)}) collective-permute-start(bf16[1,256,256]{2,1,0:T(8,128)(2,1)S(1)} %shard_map.91.rest_0_), channel_id=1, source_target_pairs={{0,4},{1,5},{2,6},{3,7},{4,0},{5,1},{6,2},{7,3},{8,12},{9,13},{10,... | collective-permute-start | bytes 393224 | tf_op jit(solution)/shard_map/ppermute | solution.py:350
  68.2 5.2 %collective-permute-start.16 = (bf16[1,256,256]{2,1,0:T(8,128)(2,1)S(1)}, bf16[1,256,256]{2,1,0:T(8,128)(2,1)S(1)}, u32[]{:S(2)}, u32[]{:S(2)}) collective-permute-start(bf16[1,256,256]{2,1,0:T(8,128)(2,1)S(1)} %shard_map.91.rest_0_), channel_id=1, source_target_pairs={{0,2},{1,3},{2,0},{3,1},{4,6},{5,7},{6,4},{7,5},{8,10},{9,11},{10,... | collective-permute-start | bytes 393224 | tf_op jit(solution)/shard_map/ppermute | solution.py:350
  68.5 5.2 %collective-permute-start.19 = (bf16[1,256,256]{2,1,0:T(8,128)(2,1)S(1)}, bf16[1,256,256]{2,1,0:T(8,128)(2,1)S(1)}, u32[]{:S(2)}, u32[]{:S(2)}) collective-permute-start(bf16[1,256,256]{2,1,0:T(8,128)(2,1)S(1)} %shard_map.91.rest_0_), channel_id=1, source_target_pairs={{0,1},{1,0},{2,3},{3,2},{4,5},{5,4},{6,7},{7,6},{8,9},{9,8},{10,11... | collective-permute-start | bytes 393224 | tf_op jit(solution)/shard_map/ppermute | solution.py:350
  72.2 1.5 %collective-permute-start.22 = (bf16[1,256,256]{2,1,0:T(8,128)(2,1)S(1)}, bf16[1,256,256]{2,1,0:T(8,128)(2,1)S(1)}, u32[]{:S(2)}, u32[]{:S(2)}) collective-permute-start(bf16[1,256,256]{2,1,0:T(8,128)(2,1)S(1)} %collective-permute-done.18.rest_3_), channel_id=1, source_target_pairs={{0,1},{1,0},{2,3},{3,2},{4,5},{5,4},{6,7},{7,6},{8,9},{9,8},{10,11... | collective-permute-start | bytes 393224 | tf_op jit(solution)/shard_map/ppermute | solution.py:350
  73.2 1.3 %collective-permute-start.21 = (bf16[1,256,256]{2,1,0:T(8,128)(2,1)S(1)}, bf16[1,256,256]{2,1,0:T(8,128)(2,1)S(1)}, u32[]{:S(2)}, u32[]{:S(2)}) collective-permute-start(bf16[1,256,256]{2,1,0:T(8,128)(2,1)S(1)} %collective-permute-done.17.rest_2_), channel_id=1, source_target_pairs={{0,1},{1,0},{2,3},{3,2},{4,5},{5,4},{6,7},{7,6},{8,9},{9,8},{10,11... | collective-permute-start | bytes 393224 | tf_op jit(solution)/shard_map/ppermute | solution.py:350
  73.4 1.3 %collective-permute-start.20 = (bf16[1,256,256]{2,1,0:T(8,128)(2,1)S(1)}, bf16[1,256,256]{2,1,0:T(8,128)(2,1)S(1)}, u32[]{:S(2)}, u32[]{:S(2)}) collective-permute-start(bf16[1,256,256]{2,1,0:T(8,128)(2,1)S(1)} %collective-permute-done.16.rest_1_), channel_id=1, source_target_pairs={{0,1},{1,0},{2,3},{3,2},{4,5},{5,4},{6,7},{7,6},{8,9},{9,8},{10,11... | collective-permute-start | bytes 393224 | tf_op jit(solution)/shard_map/ppermute | solution.py:350

commit v4 on v3

v4 whole, which is shorter than its diff:
```python
from functools import partial

import jax
import jax.numpy as jnp
from jax import lax
from jax.experimental import pallas as pl
from jax.experimental.pallas import tpu as pltpu
from jax.sharding import PartitionSpec as P

HEADS = 16
LOG2E = 1.4426950408889634
f32, bf16, i32 = jnp.float32, jnp.bfloat16, jnp.int32
AXES = ("wide", "narrow")
VMEM_LIMIT = 26 * 2**20
KEPT = 4


def shape(dims, dtype):
    return jax.ShapeDtypeStruct(tuple(dims), dtype)


def dg(a, b, contract_a, contract_b):
    return lax.dot_general(
        a, b, (((contract_a,), (contract_b,)), ((), ())), preferred_element_type=f32
    )


def call(body, out_shape, args, scratch=(), us=1, in_hbm=0, out=pltpu.VMEM):
    args = list(args)
    for i in range(len(args) - in_hbm, len(args)):
        args[i] = pltpu.with_memory_space_constraint(args[i], pltpu.HBM)
    return pl.pallas_call(
        body,
        out_shape=tuple(out_shape),
        in_specs=[pl.BlockSpec(memory_space=pltpu.SMEM)]
        + [pl.BlockSpec(memory_space=pltpu.VMEM)] * (len(args) - 1 - in_hbm)
        + [pl.BlockSpec(memory_space=pltpu.HBM)] * in_hbm,
        out_specs=tuple([pl.BlockSpec(memory_space=out)] * len(out_shape)),
        scratch_shapes=list(scratch),
        compiler_params=pltpu.CompilerParams(vmem_limit_bytes=VMEM_LIMIT),
        cost_estimate=pl.CostEstimate(flops=us * 10**9, bytes_accessed=2**20, transcendentals=0),
    )(*args)


def slot_matrix(slots, first, count):
    rows = slots.shape[1]
    at = lax.broadcasted_iota(i32, (count, rows), 0) + first
    return (at == slots).astype(f32).astype(bf16)


def place_matrix(spot, n):
    at = lax.broadcasted_iota(i32, (n, spot.shape[1]), 0)
    return (at == spot).astype(f32).astype(bf16)


def spots_of(recv_ref, cap):
    info = recv_ref[cap : cap + 16, 0:cap].astype(f32)
    spot = info[0:1] + 256.0 * info[1:2] + 1024.0 * (info[2:3] - 1.0)
    return spot.astype(i32)


def route_kernel(group, cap, me_ref, tz_hbm, rows_hbm, h_hbm, g_hbm, qkv_hbm, out_hbm, *rest):
    slots_ref, send_refs = rest[0], rest[1 : 1 + group]
    tz_ref, rows_ref, sems = rest[5 + group :]
    sources = (tz_hbm, rows_hbm, h_hbm, g_hbm, qkv_hbm, out_hbm)
    targets = (tz_ref, rows_ref) + tuple(rest[1 + group : 5 + group])
    copies = [
        pltpu.make_async_copy(a, b, sems.at[i]) for i, (a, b) in enumerate(zip(sources, targets))
    ]
    for copy in copies:
        copy.start()
    copies[0].wait()
    copies[1].wait()
    n, channels = rows_ref.shape
    here = me_ref[0] % group
    target = tz_ref[...]
    partner = (target // n % group) ^ here
    spot = target % n
    lanes = max(16, group)
    which = lax.broadcasted_iota(i32, (lanes, n), 0)
    mine = (which == partner).astype(f32)
    earlier = (
        lax.broadcasted_iota(i32, (n, n), 0) < lax.broadcasted_iota(i32, (n, n), 1)
    ).astype(f32).astype(bf16)
    before = dg(mine.astype(bf16), earlier, 1, 0)
    rank = jnp.sum(mine * before, axis=0, keepdims=True).astype(i32)
    slots = partner * cap + rank
    slots_ref[...] = slots
    row_at = lax.broadcasted_iota(i32, (16, n), 0)
    info = jnp.where(
        row_at == 0, spot % 256, jnp.where(row_at == 1, spot // 256, (row_at == 2).astype(i32))
    ).astype(f32).astype(bf16)
    rows = rows_ref[...]
    for s in range(group):
        chosen = slot_matrix(slots, s * cap, cap)
        send_refs[s][0:cap, :] = dg(chosen, rows, 1, 0).astype(bf16)
        where = dg(info, chosen, 1, 1)
        if cap < channels:
            where = jnp.concatenate([where, jnp.zeros((16, channels - cap), f32)], axis=1)
        send_refs[s][cap : cap + 16, :] = where.astype(bf16)
    for copy in copies[2:]:
        copy.wait()


def two_terms(x):
    high = x.astype(bf16)
    return jnp.concatenate([high, (x - high.astype(f32)).astype(bf16)], axis=0)


class Heads:

    def __init__(self, channels, proj, out_delta, delta, powers, turned, att, inv, grads, turned_grads):
        self.channels, self.size = channels, channels // HEADS
        self.proj, self.out_delta, self.delta = proj, out_delta, delta
        self.powers, self.turned, self.att, self.inv = powers, turned, att, inv
        self.grads, self.turned_grads = grads, turned_grads
        self.held = {}

    def rows(self, ref, part, head):
        first = part * self.channels + head * self.size
        return ref[first : first + self.size, :]

    def scores(self, head):
        k = self.rows(self.proj, 1, head)
        q = self.rows(self.proj, 0, head).astype(f32) * (self.size**-0.5 * LOG2E)
        self.held["s", head] = dg(jnp.concatenate([k, k], axis=0), two_terms(q), 0, 0)

    def softmax(self, head):
        scores = self.held.pop(("s", head))
        powers = jnp.exp2(scores - jnp.max(scores, axis=0, keepdims=True))
        self.powers[head % self.powers.shape[0]] = powers.astype(bf16)
        self.inv[head : head + 1, :] = 1.0 / jnp.sum(powers, axis=0, keepdims=True)

    def attend(self, head):
        slot = head % self.powers.shape[0]
        powers = self.powers[slot]
        first = head * self.size
        self.att[first : first + self.size, :] = (
            dg(self.rows(self.proj, 2, head), powers, 1, 0) * self.inv[head : head + 1, :]
        )
        self.turned[slot] = powers.T

    def prob_grad(self, head):
        o = self.rows(self.out_delta, 0, head).astype(f32)
        inverse = self.inv[head : head + 1, :]
        centre = jnp.sum(self.rows(self.att, 0, head) * o, axis=0, keepdims=True) * inverse
        v = self.rows(self.proj, 2, head)
        o = two_terms(o * inverse)
        self.held["p", head] = dg(jnp.concatenate([v, v], axis=0), o, 0, 0) - centre
        self.held["o", head] = o

    def score_grad(self, head):
        slot = head % self.grads.shape[0]
        powers = self.powers[head % self.powers.shape[0]].astype(f32)
        grad = (powers * self.held.pop(("p", head))).astype(bf16)
        self.grads[slot] = grad
        self.turned_grads[slot] = grad.T

    def products(self, head):
        slot = head % self.grads.shape[0]
        scale = self.size**-0.5
        value = dg(self.held.pop(("o", head)), self.turned[head % self.turned.shape[0]], 1, 0)
        query = dg(self.rows(self.proj, 1, head), self.grads[slot], 1, 0) * scale
        key = dg(self.rows(self.proj, 0, head), self.turned_grads[slot], 1, 0) * scale
        value = value[0 : self.size] + value[self.size :]
        for part, grad in enumerate((query, key, value)):
            first = part * self.channels + head * self.size
            self.delta[first : first + self.size, :] = grad.astype(bf16)


def pipeline(*stages):
    for step in range(HEADS + max(lag for _, lag in stages)):
        for work, lag in stages:
            if 0 <= step - lag < HEADS:
                work(step - lag)


def late_kernel(group, cap, me_ref, h_ref, g_ref, qkv_ref, out_ref, slots_ref, *rest):
    mid_ref, sums_ref = rest[0], rest[1]
    send_refs = rest[2 : 2 + group]
    proj, delta, powers, turned, att_ref, inv_ref, grads, turned_grads = rest[2 + group :]
    h, g = h_ref[...], g_ref[...]
    n, channels = h.shape
    qkv_w = qkv_ref[1]
    proj[0 : 3 * channels, :] = dg(qkv_w, h, 0, 1).astype(bf16)
    proj[3 * channels : 4 * channels, :] = dg(out_ref[1], g, 1, 1).astype(bf16)
    out_delta = proj.at[3 * channels : 4 * channels, :]
    heads = Heads(
        channels, proj, out_delta, delta, powers, turned, att_ref, inv_ref, grads, turned_grads
    )
    pipeline(
        (heads.scores, 0),
        (heads.score_grad, 3),
        (heads.softmax, 1),
        (heads.products, 4),
        (heads.attend, 2),
        (heads.prob_grad, 2),
    )
    qkv_delta = delta[...]
    row_grad = dg(qkv_w, qkv_delta, 1, 0).T
    mid = (g.astype(f32) + row_grad).astype(bf16)
    mid_ref[...] = mid
    slots = slots_ref[...]
    for s in range(group):
        send_refs[s][...] = dg(slot_matrix(slots, s * cap, cap), mid, 1, 0).astype(bf16)
    qkv_grad = dg(h.T, qkv_delta, 1, 1).astype(bf16)
    for part in range(3):
        columns = slice(part * channels, (part + 1) * channels)
        sums_ref[columns, :] = qkv_grad[:, columns]
    sums_ref[3 * channels :, :] = dg(att_ref[...].astype(bf16), g, 1, 0).astype(bf16)


def forward_kernel(group, cap, me_ref, qkv_ref, *rest):
    feats_refs = rest[0:group]
    place_ref, turned_h_ref, proj, powers, turned, att_ref, inv_ref = rest[group:]
    channels, n = turned_h_ref.shape
    for s in range(group):
        place_ref[s] = place_matrix(spots_of(feats_refs[s], cap), n)
    h = sum(dg(place_ref[s], feats_refs[s][0:cap, :], 1, 0) for s in range(group)).astype(bf16)
    turned_h_ref[...] = h.T
    for part in range(3):
        rows = slice(part * channels, (part + 1) * channels)
        proj[rows, :] = dg(qkv_ref[0, :, rows], turned_h_ref[...], 0, 0).astype(bf16)
    heads = Heads(channels, proj, None, None, powers, turned, att_ref, inv_ref, None, None)
    pipeline((heads.softmax, 1), (heads.scores, 0), (heads.attend, 2))


def backward_kernel(group, blocks, me_ref, out_ref, place_ref, turned_h_ref, proj, *rest):
    powers, turned, att_ref, inv_ref, late_ref = rest[0:5]
    grads_refs = rest[5 : 5 + group]
    delta, keep_ref, send_ref, out_delta, grads, turned_grads = rest[5 + group :]
    channels, n = turned_h_ref.shape
    g = sum(dg(place_ref[s], grads_refs[s][...], 1, 0) for s in range(group)).astype(bf16)
    out_delta[...] = dg(out_ref[0], g, 1, 1).astype(bf16)
    heads = Heads(
        channels, proj, out_delta, delta, powers, turned, att_ref, inv_ref, grads, turned_grads
    )
    pipeline((heads.score_grad, 1), (heads.prob_grad, 0), (heads.products, 2))
    me = me_ref[0]
    qkv_grad = dg(turned_h_ref[...], delta[...], 1, 1).astype(bf16)
    out_grad = dg(att_ref[...].astype(bf16), g, 1, 0).astype(bf16)
    rows = 4 * channels // blocks
    half = blocks // 2

    def store(first_ref, second_ref):
        for c in range(blocks):
            ref = first_ref if c < half else second_ref
            part, first = c * rows // channels, c * rows % channels
            if part < 3:
                piece = qkv_grad[first : first + rows, part * channels : (part + 1) * channels]
            else:
                piece = out_grad[first : first + rows, :]
            block = (c ^ me) % half
            ref[block, 0:rows, :] = piece
            ref[block, rows : 2 * rows, :] = late_ref[c * rows : (c + 1) * rows, :]

    @pl.when(me < half)
    def _():
        store(keep_ref, send_ref)

    @pl.when(me >= half)
    def _():
        store(send_ref, keep_ref)


def rows_kernel(group, me_ref, qkv_ref, delta, place_ref, *send_refs):
    early = dg(qkv_ref[0], delta[...], 1, 0).T.astype(bf16)
    for s in range(group):
        send_refs[s][...] = dg(place_ref[s], early, 0, 0).astype(bf16)


def join_kernel(group, cap, me_ref, slots_ref, mid_ref, *rest):
    back_refs, input_ref = rest[:group], rest[group]
    slots = slots_ref[...]
    total = jnp.zeros(mid_ref.shape, f32)
    for s in range(group):
        total = total + dg(slot_matrix(slots, s * cap, cap), back_refs[s][...], 0, 0)
    input_ref[...] = (mid_ref[...].astype(f32) + total.astype(bf16).astype(f32)).astype(bf16)


def tree_sum(values):
    while len(values) > 1:
        values = [values[i] + values[i + 1] for i in range(0, len(values), 2)]
    return values[0]


def add_kernel(count, me_ref, *rest):
    ins, outs = rest[:count], rest[count:]
    m = outs[0].shape[0]
    for j, out in enumerate(outs):
        for b in range(m):
            out[b] = tree_sum([x[j * m + b].astype(f32) for x in ins]).astype(bf16)


def add_parts(me, parts, pieces):
    dims = parts[0].shape
    out = [shape((dims[0] // pieces,) + dims[1:], bf16)] * pieces
    return call(partial(add_kernel, len(parts)), out, [me] + list(parts))


def finish_kernel(scale, me_ref, *rest):
    refs, (qkv_ref, out_ref, ready, sems) = rest[:-4], rest[-4:]
    me = me_ref[0]
    _, rows, channels = refs[0].shape
    rows = rows // 2

    def each(s, l, act):
        chunk = s ^ me
        part = chunk * rows // channels
        first = pl.multiple_of(chunk * rows % channels, rows)

        @pl.when(part < 3)
        def _():
            column = pl.multiple_of(part * channels, channels)
            to = qkv_ref.at[l, pl.ds(first, rows), pl.ds(column, channels)]
            act(pltpu.make_async_copy(ready.at[s, l], to, sems.at[s, l]))

        @pl.when(part == 3)
        def _():
            to = out_ref.at[l, pl.ds(first, rows), :]
            act(pltpu.make_async_copy(ready.at[s, l], to, sems.at[s, l]))

    work = [(s, l) for s in range(len(refs)) for l in range(2)]
    for s, l in work:
        ready[s, l] = refs[s][0, l * rows : (l + 1) * rows, :].astype(f32) * scale
        each(s, l, lambda copy: copy.start())
    for s, l in work:
        each(s, l, lambda copy: copy.wait())


def swap(x, mask, devices):
    return lax.ppermute(x, AXES, [(d, d ^ mask) for d in range(devices)])


def exchange(blocks, devices):
    return [blocks[0]] + [swap(blocks[s], s, devices) for s in range(1, len(blocks))]


def stage_masks(bits):
    masks = [0]
    for b in bits:
        masks = masks + [m | (1 << b) for m in masks]
    return masks


def on_device(section_input, mid_features, out_grad, to_hilbert, to_zorder, qkv_weight, out_weight):
    devices = lax.axis_size("wide") * lax.axis_size("narrow")
    n, channels = section_input.shape
    group = devices // 8
    share = n // group
    cap = share + 2 * (share // 4)
    rank = (lax.axis_index("wide") * lax.axis_size("narrow") + lax.axis_index("narrow")).astype(i32)
    me = rank.reshape(1)
    blocks = 8
    low = rank % blocks
    place = ((low & 1) << 2 | (low >> 1)).reshape(1)
    bits = devices.bit_length() - 1
    whole_stages = [tuple(range(b, min(b + 2, bits))) for b in range(3, bits, 2)]

    size_rows = shape((n, channels), bf16)
    size_send = shape((cap, channels), bf16)
    some_heads = pltpu.VMEM((KEPT, n, n), bf16)
    powers_s, att_s, inv_s = (HEADS, n, n), (channels, n), (HEADS, n)
    chunk = (2 * 4 * channels // blocks, channels)

    moved = [mid_features, out_grad, qkv_weight, out_weight]
    slots, *rest = call(
        partial(route_kernel, group, cap),
        [shape((1, n), i32)]
        + [shape((cap + 16, channels), bf16)] * group
        + [shape(x.shape, bf16) for x in moved],
        [me, to_zorder.reshape(1, n), section_input] + moved,
        [
            pltpu.VMEM((1, n), i32),
            pltpu.VMEM((n, channels), bf16),
            pltpu.SemaphoreType.DMA((6,)),
        ],
        us=2,
        in_hbm=6,
    )
    feats = exchange(rest[:group], devices)
    mid_features, out_grad, qkv_w, out_w = rest[group:]
    mid, late_sums, *grads = call(
        partial(late_kernel, group, cap),
        [size_rows, shape((4 * channels, channels), bf16)] + [size_send] * group,
        [me, mid_features, out_grad, qkv_w, out_w, slots],
        [
            pltpu.VMEM((4 * channels, n), bf16),
            pltpu.VMEM((3 * channels, n), bf16),
            some_heads,
            some_heads,
            pltpu.VMEM(att_s, f32),
            pltpu.VMEM(inv_s, f32),
            some_heads,
            some_heads,
        ],
        us=16,
    )
    grads = exchange(grads, devices)
    place_rows, *layer = call(
        partial(forward_kernel, group, cap),
        [
            shape((group, n, cap), bf16),
            shape((channels, n), bf16),
            shape((3 * channels, n), bf16),
            shape(powers_s, bf16),
            shape(powers_s, bf16),
            shape(att_s, f32),
            shape(inv_s, f32),
        ],
        [me, qkv_w, *feats],
        us=7,
    )
    delta, keep, send = call(
        partial(backward_kernel, group, blocks),
        [
            shape((3 * channels, n), bf16),
            shape((blocks // 2,) + chunk, bf16),
            shape((blocks // 2,) + chunk, bf16),
        ],
        [place, out_w, place_rows, *layer, late_sums, *grads],
        [pltpu.VMEM((channels, n), bf16), some_heads, some_heads],
        us=9,
    )
    got = swap(send, 1, devices)
    backs = call(
        partial(rows_kernel, group),
        [size_send] * group,
        [me, qkv_w, delta, place_rows],
        us=2,
    )
    pieces = add_parts(me, [keep, got], 4)
    masks = stage_masks((1, 2))
    parts = [pieces[0]] + [swap(pieces[i], masks[i], devices) for i in range(1, 4)]
    (total,) = add_parts(me, parts, 1)
    backs = exchange(backs, devices)
    for stage in whole_stages:
        parts = [total] + [swap(total, m, devices) for m in stage_masks(stage)[1:]]
        (total,) = add_parts(me, parts, 1)
    (input_grad,) = call(
        partial(join_kernel, group, cap), [size_rows], [me, slots, mid, *backs]
    )
    total, input_grad = lax.optimization_barrier((total, input_grad))
    parts = [total] + [swap(total, m, devices) for m in masks[1:]]
    parts = parts + [swap(x, 1, devices) for x in parts]
    qkv_grad, out_w_grad = call(
        partial(finish_kernel, float((n * devices) ** -0.5)),
        [shape(qkv_weight.shape, f32), shape(out_weight.shape, f32)],
        [place, *parts],
        [pltpu.VMEM((blocks, 2) + (chunk[0] // 2, channels), f32), pltpu.SemaphoreType.DMA((blocks, 2))],
        out=pltpu.HBM,
    )
    return (input_grad, qkv_grad, out_w_grad)


def solution(mesh):
    placed = (
        P(AXES, None),
        P(AXES, None),
        P(AXES, None),
        P(AXES),
        P(AXES),
        P(),
        P(),
    )
    return jax.shard_map(
        on_device,
        mesh=mesh,
        in_specs=placed,
        out_specs=(P(AXES, None), P(), P()),
        check_vma=False,
    )
```

time: 76.7 us -> 72.1 us (0.940)
  Pallas kernels: 36.7 us -> 31.8 us
    pallas_call x10, Pallas kernels: 36.7 us -> 31.8 us  [call(): pl.pallas_call(body, out_shape=tuple(out_shape), in_specs=[pl.BlockSpec(m...]
  transfers between devices with their start and end apart: 23 -> 23, of which waited for: 10 -> 10; matrix products, arithmetic and copies ran while one was open for 0% -> 0% of each run, Pallas kernels for 30% -> 29%
where the time goes in v4:
time: 72.1 us; the launch traced here: 71.9 us
  Pallas kernels  31.8 us (44%)
  starting transfers between devices  19.8 us (27%)
  waiting for transfers between devices  19.4 us (27%)
  between operations  0.91 us (1%)
    pallas_call x10, Pallas kernels, call(): pl.pallas_call(body, out_shape=tuple(out_shape), in_specs=[pl.BlockSpec(m...  31.8 us
    ppermute x23, starting transfers between devices, swap(): return lax.ppermute(x, AXES, [(d, d ^ mask) for d in range(devices)])  19.8 us
    ppermute x23, waiting for transfers between devices, swap(): return lax.ppermute(x, AXES, [(d, d ^ mask) for d in range(devices)])  19.4 us
  transfers between devices with their start and end apart: 23, of which 10 were waited for; matrix products, arithmetic and copies ran while one was open for 0% of the time, Pallas kernels for 29%

profile of v4, /device:TPU:0, one launch (start us, length us, event | category | flops | bytes accessed | tf_op | source)
XLA Modules:
  0.0 71.9 jit_solution(17986661112661883753)
XLA Ops:
  0.6 1.8 %shard_map.85 = (s32[1,512]{1,0:T(1,128)S(1)}, bf16[208,256]{1,0:T(8,128)(2,1)S(1)}, bf16[208,256]{1,0:T(8,128)(2,1)S(1)}, bf16[208,256]{1,0:T(8,128)(2,1)S(1)},...) custom-call(s32[1]{0:T(128)} %bitcast.me_ref, ...), custom_call_target="tpu_custom_call" | custom-call | flops 2000000000 | bytes 1048576 | tf_op jit(solution)/shard_map/pallas_call | solution.py:32
  2.9 2.6 %collective-permute-start.1 = (bf16[208,256]{1,0:T(8,128)(2,1)S(1)}, bf16[208,256]{1,0:T(8,128)(2,1)S(1)}, u32[]{:S(2)}, u32[]{:S(2)}) collective-permute-start(bf16[208,256]{1,0:T(8,128)(2,1)S(1)} %get-tuple-element.44), channel_id=1, source_target_pairs={{0,2},{1,3},{2,0},{3,1},{4,6},{5,7},{6,4},{7,5},{8,10},{9,11},{10,... | collective-permute-start | bytes 319496 | tf_op jit(solution)/shard_map/ppermute | solution.py:332
  5.6 11.9 %shard_map.87 = (bf16[512,256]{1,0:T(8,128)(2,1)S(1)}, bf16[1024,256]{1,0:T(8,128)(2,1)S(1)}, bf16[192,256]{1,0:T(8,128)(2,1)S(1)}, bf16[192,256]{1,0:T(8,128)(2...) custom-call(s32[1]{0:T(128)} %bitcast.me_ref, bf16[512,256]{1,0:T(8,128)(2,1)S(1)} %get-tuple-element.53.h_ref, ...), custom_call_target="tpu_custom_call" | custom-call | flops 16000000000 | bytes 1048576 | tf_op jit(solution)/shard_map/pallas_call | solution.py:32
  17.7 2.0 %collective-permute-start.4 = (bf16[192,256]{1,0:T(8,128)(2,1)S(1)}, bf16[192,256]{1,0:T(8,128)(2,1)S(1)}, u32[]{:S(2)}, u32[]{:S(2)}) collective-permute-start(bf16[192,256]{1,0:T(8,128)(2,1)S(1)} %get-tuple-element.59), channel_id=1, source_target_pairs={{0,2},{1,3},{2,0},{3,1},{4,6},{5,7},{6,4},{7,5},{8,10},{9,11},{10,... | collective-permute-start | bytes 294920 | tf_op jit(solution)/shard_map/ppermute | solution.py:332
  19.7 6.8 %shard_map.86 = (bf16[4,512,192]{2,1,0:T(8,128)(2,1)S(1)}, bf16[256,512]{1,0:T(8,128)(2,1)S(1)}, bf16[768,512]{1,0:T(8,128)(2,1)S(1)}, bf16[16,512,512]{2,1,0:T(...) custom-call(s32[1]{0:T(128)} %bitcast.me_ref, ...), custom_call_target="tpu_custom_call" | custom-call | flops 7000000000 | bytes 1048576 | tf_op jit(solution)/shard_map/pallas_call | solution.py:32
  26.5 7.5 %shard_map.88 = (bf16[768,512]{1,0:T(8,128)(2,1)S(1)}, bf16[4,256,256]{2,1,0:T(8,128)(2,1)S(1)}, bf16[4,256,256]{2,1,0:T(8,128)(2,1)S(1)}) custom-call(s32[1]{0:T(128)} %bitcast.1.me_ref, bf16[2,256,256]{2,1,0:T(8,128)(2,1)S(1)} %get-tuple-element.40.out_ref, bf16[4,512,192]{2,1,0:T(8,128)(2,1)S(1)} %get-tuple-element.46.place_ref, ...), custom_call_target="tpu_custom_call" | custom-call | flops 8999999488 | bytes 1048576 | tf_op jit(solution)/shard_map/pallas_call | solution.py:32
  34.3 1.7 %collective-permute-done.6.rest_1_ = bf16[4,256,256]{2,1,0:T(8,128)(2,1)S(1)} collective-permute-done((bf16[4,256,256]{2,1,0:T(8,128)(2,1)S(1)}, bf16[4,256,256]{2,1,0:T(8,128)(2,1)S(1)}, u32[]{:S(2)}, u32[]{:S(2)}) %collective-permute-start.6) | collective-permute-done | bytes 524320 | tf_op jit(solution)/shard_map/ppermute | solution.py:332
  36.1 1.8 %collective-permute-start.7 = (bf16[1,256,256]{2,1,0:T(8,128)(2,1)S(1)}, bf16[1,256,256]{2,1,0:T(8,128)(2,1)S(1)}, u32[]{:S(2)}, u32[]{:S(2)}) collective-permute-start(bf16[1,256,256]{2,1,0:T(8,128)(2,1)S(1)} %get-tuple-element.64), channel_id=1, source_target_pairs={{0,2},{1,3},{2,0},{3,1},{4,6},{5,7},{6,4},{7,5},{8,10},{9,11},{10,... | collective-permute-start | bytes 393224 | tf_op jit(solution)/shard_map/ppermute | solution.py:332
  38.0 1.5 %collective-permute-start.8 = (bf16[1,256,256]{2,1,0:T(8,128)(2,1)S(1)}, bf16[1,256,256]{2,1,0:T(8,128)(2,1)S(1)}, u32[]{:S(2)}, u32[]{:S(2)}) collective-permute-start(bf16[1,256,256]{2,1,0:T(8,128)(2,1)S(1)} %get-tuple-element.65), channel_id=1, source_target_pairs={{0,4},{1,5},{2,6},{3,7},{4,0},{5,1},{6,2},{7,3},{8,12},{9,13},{10,... | collective-permute-start | bytes 393224 | tf_op jit(solution)/shard_map/ppermute | solution.py:332
  39.7 0.9 %shard_map.92 = (bf16[192,256]{1,0:T(8,128)(2,1)S(1)}, bf16[192,256]{1,0:T(8,128)(2,1)S(1)}, bf16[192,256]{1,0:T(8,128)(2,1)S(1)}, bf16[192,256]{1,0:T(8,128)(2,1)S(1)}) custom-call(s32[1]{0:T(128)} %bitcast.me_ref, bf16[2,256,768]{2,1,0:T(8,128)(2,1)S(1)} %get-tuple-element.41.qkv_ref, bf16[768,512]{1,0:T(8,128)(2,1)S(1)} %get-tuple-element.68.delta, ...), custom_call_target="tpu_custom_call" | custom-call | flops 2000000000 | bytes 1048576 | tf_op jit(solution)/shard_map/pallas_call | solution.py:32
  40.6 1.8 %collective-permute-start.14 = (bf16[192,256]{1,0:T(8,128)(2,1)S(1)}, bf16[192,256]{1,0:T(8,128)(2,1)S(1)}, u32[]{:S(2)}, u32[]{:S(2)}) collective-permute-start(bf16[192,256]{1,0:T(8,128)(2,1)S(1)} %get-tuple-element.71), channel_id=1, source_target_pairs={{0,2},{1,3},{2,0},{3,1},{4,6},{5,7},{6,4},{7,5},{8,10},{9,11},{10,... | collective-permute-start | bytes 294920 | tf_op jit(solution)/shard_map/ppermute | solution.py:332
  42.9 2.8 %collective-permute-done.8.rest_2_ = bf16[1,256,256]{2,1,0:T(8,128)(2,1)S(1)} collective-permute-done((bf16[1,256,256]{2,1,0:T(8,128)(2,1)S(1)}, bf16[1,256,256]{2,1,0:T(8,128)(2,1)S(1)}, u32[]{:S(2)}, u32[]{:S(2)}) %collective-permute-start.8) | collective-permute-done | bytes 131104 | tf_op jit(solution)/shard_map/ppermute | solution.py:332
  45.7 1.1 %collective-permute-done.9.rest_3_ = bf16[1,256,256]{2,1,0:T(8,128)(2,1)S(1)} collective-permute-done((bf16[1,256,256]{2,1,0:T(8,128)(2,1)S(1)}, bf16[1,256,256]{2,1,0:T(8,128)(2,1)S(1)}, u32[]{:S(2)}, u32[]{:S(2)}) %collective-permute-start.9) | collective-permute-done | bytes 131104 | tf_op jit(solution)/shard_map/ppermute | solution.py:332
  46.9 3.7 %collective-permute-start.12 = (bf16[1,256,256]{2,1,0:T(8,128)(2,1)S(1)}, bf16[1,256,256]{2,1,0:T(8,128)(2,1)S(1)}, u32[]{:S(2)}, u32[]{:S(2)}) collective-permute-start(bf16[1,256,256]{2,1,0:T(8,128)(2,1)S(1)} %shard_map.90.rest_0_), channel_id=1, source_target_pairs={{0,24},{1,25},{2,26},{3,27},{4,28},{5,29},{6,30},{7,31},{8,16},{9,... | collective-permute-start | bytes 393224 | tf_op jit(solution)/shard_map/ppermute | solution.py:332
  50.6 0.8 %collective-permute-start.10 = (bf16[1,256,256]{2,1,0:T(8,128)(2,1)S(1)}, bf16[1,256,256]{2,1,0:T(8,128)(2,1)S(1)}, u32[]{:S(2)}, u32[]{:S(2)}) collective-permute-start(bf16[1,256,256]{2,1,0:T(8,128)(2,1)S(1)} %shard_map.90.rest_0_), channel_id=1, source_target_pairs={{0,8},{1,9},{2,10},{3,11},{4,12},{5,13},{6,14},{7,15},{8,0},{9,1},... | collective-permute-start | bytes 393224 | tf_op jit(solution)/shard_map/ppermute | solution.py:332
  51.3 1.2 %shard_map.93 = bf16[512,256]{1,0:T(8,128)(2,1)} custom-call(s32[1]{0:T(128)} %bitcast.me_ref, s32[1,512]{1,0:T(1,128)S(1)} %get-tuple-element.55.slots_ref, bf16[512,256]{1,0:T(8,128)(2,1)S(1)} %get-tuple-element.67.mid_ref, bf16[192,256]{1,0:T(8,128)(2,1)S(1)} %get-tuple-element.69.rest_0_, bf16[192,256]{1,0:T(8,128)(2,1)S(1)} %collective-permute-done.13.rest_1_, ...), custom_call_target="tpu_custom_call" | custom-call | flops 1000000000 | bytes 1048576 | tf_op jit(solution)/shard_map/pallas_call | solution.py:32
  52.5 2.4 %collective-permute-done.12.rest_3_ = bf16[1,256,256]{2,1,0:T(8,128)(2,1)S(1)} collective-permute-done((bf16[1,256,256]{2,1,0:T(8,128)(2,1)S(1)}, bf16[1,256,256]{2,1,0:T(8,128)(2,1)S(1)}, u32[]{:S(2)}, u32[]{:S(2)}) %collective-permute-start.12) | collective-permute-done | bytes 131104 | tf_op jit(solution)/shard_map/ppermute | solution.py:332
  54.9 5.4 %collective-permute-done.11.rest_2_ = bf16[1,256,256]{2,1,0:T(8,128)(2,1)S(1)} collective-permute-done((bf16[1,256,256]{2,1,0:T(8,128)(2,1)S(1)}, bf16[1,256,256]{2,1,0:T(8,128)(2,1)S(1)}, u32[]{:S(2)}, u32[]{:S(2)}) %collective-permute-start.11) | collective-permute-done | bytes 131104 | tf_op jit(solution)/shard_map/ppermute | solution.py:332
  60.4 1.7 %collective-permute-start.18 = (bf16[1,256,256]{2,1,0:T(8,128)(2,1)S(1)}, bf16[1,256,256]{2,1,0:T(8,128)(2,1)S(1)}, u32[]{:S(2)}, u32[]{:S(2)}) collective-permute-start(bf16[1,256,256]{2,1,0:T(8,128)(2,1)S(1)} %shard_map.91.rest_0_), channel_id=1, source_target_pairs={{0,6},{1,7},{2,4},{3,5},{4,2},{5,3},{6,0},{7,1},{8,14},{9,15},{10,... | collective-permute-start | bytes 393224 | tf_op jit(solution)/shard_map/ppermute | solution.py:332
  62.2 1.5 %collective-permute-start.17 = (bf16[1,256,256]{2,1,0:T(8,128)(2,1)S(1)}, bf16[1,256,256]{2,1,0:T(8,128)(2,1)S(1)}, u32[]{:S(2)}, u32[]{:S(2)}) collective-permute-start(bf16[1,256,256]{2,1,0:T(8,128)(2,1)S(1)} %shard_map.91.rest_0_), channel_id=1, source_target_pairs={{0,4},{1,5},{2,6},{3,7},{4,0},{5,1},{6,2},{7,3},{8,12},{9,13},{10,... | collective-permute-start | bytes 393224 | tf_op jit(solution)/shard_map/ppermute | solution.py:332
  64.0 3.6 %collective-permute-done.18.rest_3_ = bf16[1,256,256]{2,1,0:T(8,128)(2,1)S(1)} collective-permute-done((bf16[1,256,256]{2,1,0:T(8,128)(2,1)S(1)}, bf16[1,256,256]{2,1,0:T(8,128)(2,1)S(1)}, u32[]{:S(2)}, u32[]{:S(2)}) %collective-permute-start.18) | collective-permute-done | bytes 131104 | tf_op jit(solution)/shard_map/ppermute | solution.py:332
  67.6 1.1 %collective-permute-done.17.rest_2_ = bf16[1,256,256]{2,1,0:T(8,128)(2,1)S(1)} collective-permute-done((bf16[1,256,256]{2,1,0:T(8,128)(2,1)S(1)}, bf16[1,256,256]{2,1,0:T(8,128)(2,1)S(1)}, u32[]{:S(2)}, u32[]{:S(2)}) %collective-permute-start.17) | collective-permute-done | bytes 131104 | tf_op jit(solution)/shard_map/ppermute | solution.py:332
  69.2 0.8 %collective-permute-done.21.rest_6_ = bf16[1,256,256]{2,1,0:T(8,128)(2,1)S(1)} collective-permute-done((bf16[1,256,256]{2,1,0:T(8,128)(2,1)S(1)}, bf16[1,256,256]{2,1,0:T(8,128)(2,1)S(1)}, u32[]{:S(2)}, u32[]{:S(2)}) %collective-permute-start.21) | collective-permute-done | bytes 131104 | tf_op jit(solution)/shard_map/ppermute | solution.py:332
  70.3 1.5 %shard_map.94 = (f32[2,256,768]{2,1,0:T(8,128)}, f32[2,256,256]{2,1,0:T(8,128)}) custom-call(s32[1]{0:T(128)} %bitcast.1.me_ref, bf16[1,256,256]{2,1,0:T(8,128)(2,1)S(1)} %shard_map.91.rest_0_, bf16[1,256,256]{2,1,0:T(8,128)(2,1)S(1)} %collective-permute-done.16.rest_1_, bf16[1,256,256]{2,1,0:T(8,128)(2,1)S(1)} %collective-permute-done.17.rest_2_, ...), custom_call_target="tpu_custom_call" | custom-call | flops 1000000000 | bytes 1048576 | tf_op jit(solution)/shard_map/pallas_call | solution.py:32
  (32 shorter events, 3.1 us)
Async XLA Ops:
  2.4 17.2 %collective-permute-start = (bf16[208,256]{1,0:T(8,128)(2,1)S(1)}, bf16[208,256]{1,0:T(8,128)(2,1)S(1)}, u32[]{:S(2)}, u32[]{:S(2)}) collective-permute-start(bf16[208,256]{1,0:T(8,128)(2,1)S(1)} %get-tuple-element.43), channel_id=1, source_target_pairs={{0,1},{1,0},{2,3},{3,2},{4,5},{5,4},{6,7},{7,6},{8,9},{9,8},{10,11... | collective-permute-start | bytes 319496 | tf_op jit(solution)/shard_map/ppermute | solution.py:332
  2.9 16.7 %collective-permute-start.1 = (bf16[208,256]{1,0:T(8,128)(2,1)S(1)}, bf16[208,256]{1,0:T(8,128)(2,1)S(1)}, u32[]{:S(2)}, u32[]{:S(2)}) collective-permute-start(bf16[208,256]{1,0:T(8,128)(2,1)S(1)} %get-tuple-element.44), channel_id=1, source_target_pairs={{0,2},{1,3},{2,0},{3,1},{4,6},{5,7},{6,4},{7,5},{8,10},{9,11},{10,... | collective-permute-start | bytes 319496 | tf_op jit(solution)/shard_map/ppermute | solution.py:332
  5.5 14.2 %collective-permute-start.2 = (bf16[208,256]{1,0:T(8,128)(2,1)S(1)}, bf16[208,256]{1,0:T(8,128)(2,1)S(1)}, u32[]{:S(2)}, u32[]{:S(2)}) collective-permute-start(bf16[208,256]{1,0:T(8,128)(2,1)S(1)} %get-tuple-element.45), channel_id=1, source_target_pairs={{0,3},{1,2},{2,1},{3,0},{4,7},{5,6},{6,5},{7,4},{8,11},{9,10},{10,... | collective-permute-start | bytes 319496 | tf_op jit(solution)/shard_map/ppermute | solution.py:332
  17.5 9.0 %collective-permute-start.3 = (bf16[192,256]{1,0:T(8,128)(2,1)S(1)}, bf16[192,256]{1,0:T(8,128)(2,1)S(1)}, u32[]{:S(2)}, u32[]{:S(2)}) collective-permute-start(bf16[192,256]{1,0:T(8,128)(2,1)S(1)} %get-tuple-element.58), channel_id=1, source_target_pairs={{0,1},{1,0},{2,3},{3,2},{4,5},{5,4},{6,7},{7,6},{8,9},{9,8},{10,11... | collective-permute-start | bytes 294920 | tf_op jit(solution)/shard_map/ppermute | solution.py:332
  17.7 8.8 %collective-permute-start.4 = (bf16[192,256]{1,0:T(8,128)(2,1)S(1)}, bf16[192,256]{1,0:T(8,128)(2,1)S(1)}, u32[]{:S(2)}, u32[]{:S(2)}) collective-permute-start(bf16[192,256]{1,0:T(8,128)(2,1)S(1)} %get-tuple-element.59), channel_id=1, source_target_pairs={{0,2},{1,3},{2,0},{3,1},{4,6},{5,7},{6,4},{7,5},{8,10},{9,11},{10,... | collective-permute-start | bytes 294920 | tf_op jit(solution)/shard_map/ppermute | solution.py:332
  19.7 6.9 %collective-permute-start.5 = (bf16[192,256]{1,0:T(8,128)(2,1)S(1)}, bf16[192,256]{1,0:T(8,128)(2,1)S(1)}, u32[]{:S(2)}, u32[]{:S(2)}) collective-permute-start(bf16[192,256]{1,0:T(8,128)(2,1)S(1)} %get-tuple-element.60), channel_id=1, source_target_pairs={{0,3},{1,2},{2,1},{3,0},{4,7},{5,6},{6,5},{7,4},{8,11},{9,10},{10,... | collective-permute-start | bytes 294920 | tf_op jit(solution)/shard_map/ppermute | solution.py:332
  34.0 2.0 %collective-permute-start.6 = (bf16[4,256,256]{2,1,0:T(8,128)(2,1)S(1)}, bf16[4,256,256]{2,1,0:T(8,128)(2,1)S(1)}, u32[]{:S(2)}, u32[]{:S(2)}) collective-permute-start(bf16[4,256,256]{2,1,0:T(8,128)(2,1)S(1)} %get-tuple-element.62), channel_id=1, source_target_pairs={{0,1},{1,0},{2,3},{3,2},{4,5},{5,4},{6,7},{7,6},{8,9},{9,8},{10,11... | collective-permute-start | bytes 1572872 | tf_op jit(solution)/shard_map/ppermute | solution.py:332
  36.1 6.3 %collective-permute-start.7 = (bf16[1,256,256]{2,1,0:T(8,128)(2,1)S(1)}, bf16[1,256,256]{2,1,0:T(8,128)(2,1)S(1)}, u32[]{:S(2)}, u32[]{:S(2)}) collective-permute-start(bf16[1,256,256]{2,1,0:T(8,128)(2,1)S(1)} %get-tuple-element.64), channel_id=1, source_target_pairs={{0,2},{1,3},{2,0},{3,1},{4,6},{5,7},{6,4},{7,5},{8,10},{9,11},{10,... | collective-permute-start | bytes 393224 | tf_op jit(solution)/shard_map/ppermute | solution.py:332
  38.0 7.8 %collective-permute-start.8 = (bf16[1,256,256]{2,1,0:T(8,128)(2,1)S(1)}, bf16[1,256,256]{2,1,0:T(8,128)(2,1)S(1)}, u32[]{:S(2)}, u32[]{:S(2)}) collective-permute-start(bf16[1,256,256]{2,1,0:T(8,128)(2,1)S(1)} %get-tuple-element.65), channel_id=1, source_target_pairs={{0,4},{1,5},{2,6},{3,7},{4,0},{5,1},{6,2},{7,3},{8,12},{9,13},{10,... | collective-permute-start | bytes 393224 | tf_op jit(solution)/shard_map/ppermute | solution.py:332
  39.5 7.3 %collective-permute-start.9 = (bf16[1,256,256]{2,1,0:T(8,128)(2,1)S(1)}, bf16[1,256,256]{2,1,0:T(8,128)(2,1)S(1)}, u32[]{:S(2)}, u32[]{:S(2)}) collective-permute-start(bf16[1,256,256]{2,1,0:T(8,128)(2,1)S(1)} %get-tuple-element.66), channel_id=1, source_target_pairs={{0,6},{1,7},{2,4},{3,5},{4,2},{5,3},{6,0},{7,1},{8,14},{9,15},{10,... | collective-permute-start | bytes 393224 | tf_op jit(solution)/shard_map/ppermute | solution.py:332
  40.6 10.0 %collective-permute-start.13 = (bf16[192,256]{1,0:T(8,128)(2,1)S(1)}, bf16[192,256]{1,0:T(8,128)(2,1)S(1)}, u32[]{:S(2)}, u32[]{:S(2)}) collective-permute-start(bf16[192,256]{1,0:T(8,128)(2,1)S(1)} %get-tuple-element.70), channel_id=1, source_target_pairs={{0,1},{1,0},{2,3},{3,2},{4,5},{5,4},{6,7},{7,6},{8,9},{9,8},{10,11... | collective-permute-start | bytes 294920 | tf_op jit(solution)/shard_map/ppermute | solution.py:332
  40.6 10.7 %collective-permute-start.14 = (bf16[192,256]{1,0:T(8,128)(2,1)S(1)}, bf16[192,256]{1,0:T(8,128)(2,1)S(1)}, u32[]{:S(2)}, u32[]{:S(2)}) collective-permute-start(bf16[192,256]{1,0:T(8,128)(2,1)S(1)} %get-tuple-element.71), channel_id=1, source_target_pairs={{0,2},{1,3},{2,0},{3,1},{4,6},{5,7},{6,4},{7,5},{8,10},{9,11},{10,... | collective-permute-start | bytes 294920 | tf_op jit(solution)/shard_map/ppermute | solution.py:332
  42.5 8.8 %collective-permute-start.15 = (bf16[192,256]{1,0:T(8,128)(2,1)S(1)}, bf16[192,256]{1,0:T(8,128)(2,1)S(1)}, u32[]{:S(2)}, u32[]{:S(2)}) collective-permute-start(bf16[192,256]{1,0:T(8,128)(2,1)S(1)} %get-tuple-element.72), channel_id=1, source_target_pairs={{0,3},{1,2},{2,1},{3,0},{4,7},{5,6},{6,5},{7,4},{8,11},{9,10},{10,... | collective-permute-start | bytes 294920 | tf_op jit(solution)/shard_map/ppermute | solution.py:332
  46.9 8.1 %collective-permute-start.12 = (bf16[1,256,256]{2,1,0:T(8,128)(2,1)S(1)}, bf16[1,256,256]{2,1,0:T(8,128)(2,1)S(1)}, u32[]{:S(2)}, u32[]{:S(2)}) collective-permute-start(bf16[1,256,256]{2,1,0:T(8,128)(2,1)S(1)} %shard_map.90.rest_0_), channel_id=1, source_target_pairs={{0,24},{1,25},{2,26},{3,27},{4,28},{5,29},{6,30},{7,31},{8,16},{9,... | collective-permute-start | bytes 393224 | tf_op jit(solution)/shard_map/ppermute | solution.py:332
  50.6 9.8 %collective-permute-start.11 = (bf16[1,256,256]{2,1,0:T(8,128)(2,1)S(1)}, bf16[1,256,256]{2,1,0:T(8,128)(2,1)S(1)}, u32[]{:S(2)}, u32[]{:S(2)}) collective-permute-start(bf16[1,256,256]{2,1,0:T(8,128)(2,1)S(1)} %shard_map.90.rest_0_), channel_id=1, source_target_pairs={{0,16},{1,17},{2,18},{3,19},{4,20},{5,21},{6,22},{7,23},{8,24},{9,... | collective-permute-start | bytes 393224 | tf_op jit(solution)/shard_map/ppermute | solution.py:332
  50.6 9.8 %collective-permute-start.10 = (bf16[1,256,256]{2,1,0:T(8,128)(2,1)S(1)}, bf16[1,256,256]{2,1,0:T(8,128)(2,1)S(1)}, u32[]{:S(2)}, u32[]{:S(2)}) collective-permute-start(bf16[1,256,256]{2,1,0:T(8,128)(2,1)S(1)} %shard_map.90.rest_0_), channel_id=1, source_target_pairs={{0,8},{1,9},{2,10},{3,11},{4,12},{5,13},{6,14},{7,15},{8,0},{9,1},... | collective-permute-start | bytes 393224 | tf_op jit(solution)/shard_map/ppermute | solution.py:332
  60.4 7.1 %collective-permute-start.18 = (bf16[1,256,256]{2,1,0:T(8,128)(2,1)S(1)}, bf16[1,256,256]{2,1,0:T(8,128)(2,1)S(1)}, u32[]{:S(2)}, u32[]{:S(2)}) collective-permute-start(bf16[1,256,256]{2,1,0:T(8,128)(2,1)S(1)} %shard_map.91.rest_0_), channel_id=1, source_target_pairs={{0,6},{1,7},{2,4},{3,5},{4,2},{5,3},{6,0},{7,1},{8,14},{9,15},{10,... | collective-permute-start | bytes 393224 | tf_op jit(solution)/shard_map/ppermute | solution.py:332
  62.2 6.6 %collective-permute-start.17 = (bf16[1,256,256]{2,1,0:T(8,128)(2,1)S(1)}, bf16[1,256,256]{2,1,0:T(8,128)(2,1)S(1)}, u32[]{:S(2)}, u32[]{:S(2)}) collective-permute-start(bf16[1,256,256]{2,1,0:T(8,128)(2,1)S(1)} %shard_map.91.rest_0_), channel_id=1, source_target_pairs={{0,4},{1,5},{2,6},{3,7},{4,0},{5,1},{6,2},{7,3},{8,12},{9,13},{10,... | collective-permute-start | bytes 393224 | tf_op jit(solution)/shard_map/ppermute | solution.py:332
  63.6 5.3 %collective-permute-start.16 = (bf16[1,256,256]{2,1,0:T(8,128)(2,1)S(1)}, bf16[1,256,256]{2,1,0:T(8,128)(2,1)S(1)}, u32[]{:S(2)}, u32[]{:S(2)}) collective-permute-start(bf16[1,256,256]{2,1,0:T(8,128)(2,1)S(1)} %shard_map.91.rest_0_), channel_id=1, source_target_pairs={{0,2},{1,3},{2,0},{3,1},{4,6},{5,7},{6,4},{7,5},{8,10},{9,11},{10,... | collective-permute-start | bytes 393224 | tf_op jit(solution)/shard_map/ppermute | solution.py:332
  64.0 5.2 %collective-permute-start.19 = (bf16[1,256,256]{2,1,0:T(8,128)(2,1)S(1)}, bf16[1,256,256]{2,1,0:T(8,128)(2,1)S(1)}, u32[]{:S(2)}, u32[]{:S(2)}) collective-permute-start(bf16[1,256,256]{2,1,0:T(8,128)(2,1)S(1)} %shard_map.91.rest_0_), channel_id=1, source_target_pairs={{0,1},{1,0},{2,3},{3,2},{4,5},{5,4},{6,7},{7,6},{8,9},{9,8},{10,11... | collective-permute-start | bytes 393224 | tf_op jit(solution)/shard_map/ppermute | solution.py:332
  67.6 1.7 %collective-permute-start.22 = (bf16[1,256,256]{2,1,0:T(8,128)(2,1)S(1)}, bf16[1,256,256]{2,1,0:T(8,128)(2,1)S(1)}, u32[]{:S(2)}, u32[]{:S(2)}) collective-permute-start(bf16[1,256,256]{2,1,0:T(8,128)(2,1)S(1)} %collective-permute-done.18.rest_3_), channel_id=1, source_target_pairs={{0,1},{1,0},{2,3},{3,2},{4,5},{5,4},{6,7},{7,6},{8,9},{9,8},{10,11... | collective-permute-start | bytes 393224 | tf_op jit(solution)/shard_map/ppermute | solution.py:332
  68.7 1.3 %collective-permute-start.21 = (bf16[1,256,256]{2,1,0:T(8,128)(2,1)S(1)}, bf16[1,256,256]{2,1,0:T(8,128)(2,1)S(1)}, u32[]{:S(2)}, u32[]{:S(2)}) collective-permute-start(bf16[1,256,256]{2,1,0:T(8,128)(2,1)S(1)} %collective-permute-done.17.rest_2_), channel_id=1, source_target_pairs={{0,1},{1,0},{2,3},{3,2},{4,5},{5,4},{6,7},{7,6},{8,9},{9,8},{10,11... | collective-permute-start | bytes 393224 | tf_op jit(solution)/shard_map/ppermute | solution.py:332
  68.9 1.3 %collective-permute-start.20 = (bf16[1,256,256]{2,1,0:T(8,128)(2,1)S(1)}, bf16[1,256,256]{2,1,0:T(8,128)(2,1)S(1)}, u32[]{:S(2)}, u32[]{:S(2)}) collective-permute-start(bf16[1,256,256]{2,1,0:T(8,128)(2,1)S(1)} %collective-permute-done.16.rest_1_), channel_id=1, source_target_pairs={{0,1},{1,0},{2,3},{3,2},{4,5},{5,4},{6,7},{7,6},{8,9},{9,8},{10,11... | collective-permute-start | bytes 393224 | tf_op jit(solution)/shard_map/ppermute | solution.py:332

commit v5 on v4

--- a/solution.py
+++ b/solution.py
@@ -45,12 +45,19 @@
 def slot_matrix(slots, first, count):
     rows = slots.shape[1]
     at = lax.broadcasted_iota(i32, (count, rows), 0) + first
-    return (at == slots).astype(f32).astype(bf16)
+    return jnp.where(at == slots, 1.0, 0.0).astype(bf16)
 
 
 def place_matrix(spot, n):
     at = lax.broadcasted_iota(i32, (n, spot.shape[1]), 0)
-    return (at == spot).astype(f32).astype(bf16)
+    return jnp.where(at == spot, 1.0, 0.0).astype(bf16)
+
+
+def placed_rows(place_ref, blocks):
+    rows = jnp.concatenate(blocks, axis=0)
+    n = place_ref.shape[0]
+    halves = [dg(place_ref[i : i + n // 2, :], rows, 1, 0) for i in (0, n // 2)]
+    return jnp.concatenate(halves, axis=0).astype(bf16)
 
 
 def spots_of(recv_ref, cap):
@@ -78,10 +85,10 @@
     spot = target % n
     lanes = max(16, group)
     which = lax.broadcasted_iota(i32, (lanes, n), 0)
-    mine = (which == partner).astype(f32)
-    earlier = (
-        lax.broadcasted_iota(i32, (n, n), 0) < lax.broadcasted_iota(i32, (n, n), 1)
-    ).astype(f32).astype(bf16)
+    mine = jnp.where(which == partner, 1.0, 0.0)
+    earlier = jnp.where(
+        lax.broadcasted_iota(i32, (n, n), 0) < lax.broadcasted_iota(i32, (n, n), 1), 1.0, 0.0
+    ).astype(bf16)
     before = dg(mine.astype(bf16), earlier, 1, 0)
     rank = jnp.sum(mine * before, axis=0, keepdims=True).astype(i32)
     slots = partner * cap + rank
@@ -175,10 +182,32 @@
                 work(step - lag)
 
 
+def store_blocks(me, qkv_grad, out_grad, keep_ref, send_ref):
+    half, rows, channels = keep_ref.shape
+
+    def store(first_ref, second_ref):
+        for c in range(2 * half):
+            ref = first_ref if c < half else second_ref
+            part, first = c * rows // channels, c * rows % channels
+            if part < 3:
+                piece = qkv_grad[first : first + rows, part * channels : (part + 1) * channels]
+            else:
+                piece = out_grad[first : first + rows, :]
+            ref[(c ^ me) % half] = piece
+
+    @pl.when(me < half)
+    def _():
+        store(keep_ref, send_ref)
+
+    @pl.when(me >= half)
+    def _():
+        store(send_ref, keep_ref)
+
+
 def late_kernel(group, cap, me_ref, h_ref, g_ref, qkv_ref, out_ref, slots_ref, *rest):
-    mid_ref, sums_ref = rest[0], rest[1]
-    send_refs = rest[2 : 2 + group]
-    proj, delta, powers, turned, att_ref, inv_ref, grads, turned_grads = rest[2 + group :]
+    mid_ref, keep_ref, send_ref = rest[0:3]
+    send_refs = rest[3 : 3 + group]
+    proj, delta, powers, turned, att_ref, inv_ref, grads, turned_grads = rest[3 + group :]
     h, g = h_ref[...], g_ref[...]
     n, channels = h.shape
     qkv_w = qkv_ref[1]
@@ -204,19 +233,17 @@
     for s in range(group):
         send_refs[s][...] = dg(slot_matrix(slots, s * cap, cap), mid, 1, 0).astype(bf16)
     qkv_grad = dg(h.T, qkv_delta, 1, 1).astype(bf16)
-    for part in range(3):
-        columns = slice(part * channels, (part + 1) * channels)
-        sums_ref[columns, :] = qkv_grad[:, columns]
-    sums_ref[3 * channels :, :] = dg(att_ref[...].astype(bf16), g, 1, 0).astype(bf16)
+    out_grad = dg(att_ref[...].astype(bf16), g, 1, 0).astype(bf16)
+    store_blocks(me_ref[0], qkv_grad, out_grad, keep_ref, send_ref)
 
 
 def forward_kernel(group, cap, me_ref, qkv_ref, *rest):
     feats_refs = rest[0:group]
     place_ref, turned_h_ref, proj, powers, turned, att_ref, inv_ref = rest[group:]
     channels, n = turned_h_ref.shape
-    for s in range(group):
-        place_ref[s] = place_matrix(spots_of(feats_refs[s], cap), n)
-    h = sum(dg(place_ref[s], feats_refs[s][0:cap, :], 1, 0) for s in range(group)).astype(bf16)
+    spots = jnp.concatenate([spots_of(ref, cap) for ref in feats_refs], axis=1)
+    place_ref[...] = place_matrix(spots, n)
+    h = placed_rows(place_ref, [ref[0:cap, :] for ref in feats_refs])
     turned_h_ref[...] = h.T
     for part in range(3):
         rows = slice(part * channels, (part + 1) * channels)
@@ -225,48 +252,27 @@
     pipeline((heads.softmax, 1), (heads.scores, 0), (heads.attend, 2))
 
 
-def backward_kernel(group, blocks, me_ref, out_ref, place_ref, turned_h_ref, proj, *rest):
-    powers, turned, att_ref, inv_ref, late_ref = rest[0:5]
-    grads_refs = rest[5 : 5 + group]
-    delta, keep_ref, send_ref, out_delta, grads, turned_grads = rest[5 + group :]
+def backward_kernel(group, me_ref, out_ref, place_ref, turned_h_ref, proj, *rest):
+    powers, turned, att_ref, inv_ref = rest[0:4]
+    grads_refs = rest[4 : 4 + group]
+    delta, keep_ref, send_ref, out_delta, grads, turned_grads = rest[4 + group :]
     channels, n = turned_h_ref.shape
-    g = sum(dg(place_ref[s], grads_refs[s][...], 1, 0) for s in range(group)).astype(bf16)
+    g = placed_rows(place_ref, [ref[...] for ref in grads_refs])
     out_delta[...] = dg(out_ref[0], g, 1, 1).astype(bf16)
     heads = Heads(
         channels, proj, out_delta, delta, powers, turned, att_ref, inv_ref, grads, turned_grads
     )
     pipeline((heads.score_grad, 1), (heads.prob_grad, 0), (heads.products, 2))
-    me = me_ref[0]
     qkv_grad = dg(turned_h_ref[...], delta[...], 1, 1).astype(bf16)
     out_grad = dg(att_ref[...].astype(bf16), g, 1, 0).astype(bf16)
-    rows = 4 * channels // blocks
-    half = blocks // 2
-
-    def store(first_ref, second_ref):
-        for c in range(blocks):
-            ref = first_ref if c < half else second_ref
-            part, first = c * rows // channels, c * rows % channels
-            if part < 3:
-                piece = qkv_grad[first : first + rows, part * channels : (part + 1) * channels]
-            else:
-                piece = out_grad[first : first + rows, :]
-            block = (c ^ me) % half
-            ref[block, 0:rows, :] = piece
-            ref[block, rows : 2 * rows, :] = late_ref[c * rows : (c + 1) * rows, :]
-
-    @pl.when(me < half)
-    def _():
-        store(keep_ref, send_ref)
-
-    @pl.when(me >= half)
-    def _():
-        store(send_ref, keep_ref)
-
-
-def rows_kernel(group, me_ref, qkv_ref, delta, place_ref, *send_refs):
+    store_blocks(me_ref[0], qkv_grad, out_grad, keep_ref, send_ref)
+
+
+def rows_kernel(cap, me_ref, qkv_ref, delta, place_ref, *send_refs):
     early = dg(qkv_ref[0], delta[...], 1, 0).T.astype(bf16)
-    for s in range(group):
-        send_refs[s][...] = dg(place_ref[s], early, 0, 0).astype(bf16)
+    rows = dg(place_ref[...], early, 0, 0).astype(bf16)
+    for s, ref in enumerate(send_refs):
+        ref[...] = rows[s * cap : (s + 1) * cap, :]
 
 
 def join_kernel(group, cap, me_ref, slots_ref, mid_ref, *rest):
@@ -284,18 +290,25 @@
     return values[0]
 
 
-def add_kernel(count, me_ref, *rest):
-    ins, outs = rest[:count], rest[count:]
-    m = outs[0].shape[0]
-    for j, out in enumerate(outs):
-        for b in range(m):
-            out[b] = tree_sum([x[j * m + b].astype(f32) for x in ins]).astype(bf16)
-
-
-def add_parts(me, parts, pieces):
-    dims = parts[0].shape
-    out = [shape((dims[0] // pieces,) + dims[1:], bf16)] * pieces
-    return call(partial(add_kernel, len(parts)), out, [me] + list(parts))
+def add_kernel(counts, me_ref, *rest):
+    ins, outs = rest[: sum(counts)], rest[sum(counts) :]
+    first = at = 0
+    for count in counts:
+        group = ins[at : at + count]
+        rows = group[0].shape[1]
+        for j, out in enumerate(outs):
+            out[0, first : first + rows, :] = tree_sum([x[j].astype(f32) for x in group]).astype(bf16)
+        first, at = first + rows, at + count
+
+
+def add_parts(me, groups):
+    pieces, _, channels = groups[0][0].shape
+    rows = sum(g[0].shape[1] for g in groups)
+    return call(
+        partial(add_kernel, [len(g) for g in groups]),
+        [shape((1, rows, channels), bf16)] * pieces,
+        [me] + [x for g in groups for x in g],
+    )
 
 
 def finish_kernel(scale, me_ref, *rest):
@@ -361,7 +374,7 @@
     size_send = shape((cap, channels), bf16)
     some_heads = pltpu.VMEM((KEPT, n, n), bf16)
     powers_s, att_s, inv_s = (HEADS, n, n), (channels, n), (HEADS, n)
-    chunk = (2 * 4 * channels // blocks, channels)
+    half = shape((blocks // 2, 4 * channels // blocks, channels), bf16)
 
     moved = [mid_features, out_grad, qkv_weight, out_weight]
     slots, *rest = call(
@@ -380,10 +393,10 @@
     )
     feats = exchange(rest[:group], devices)
     mid_features, out_grad, qkv_w, out_w = rest[group:]
-    mid, late_sums, *grads = call(
+    mid, late_keep, late_send, *grads = call(
         partial(late_kernel, group, cap),
-        [size_rows, shape((4 * channels, channels), bf16)] + [size_send] * group,
-        [me, mid_features, out_grad, qkv_w, out_w, slots],
+        [size_rows, half, half] + [size_send] * group,
+        [place, mid_features, out_grad, qkv_w, out_w, slots],
         [
             pltpu.VMEM((4 * channels, n), bf16),
             pltpu.VMEM((3 * channels, n), bf16),
@@ -397,10 +410,11 @@
         us=16,
     )
     grads = exchange(grads, devices)
+    late_got = swap(late_send, 1, devices)
     place_rows, *layer = call(
         partial(forward_kernel, group, cap),
         [
-            shape((group, n, cap), bf16),
+            shape((n, group * cap), bf16),
             shape((channels, n), bf16),
             shape((3 * channels, n), bf16),
             shape(powers_s, bf16),
@@ -412,31 +426,31 @@
         us=7,
     )
     delta, keep, send = call(
-        partial(backward_kernel, group, blocks),
+        partial(backward_kernel, group),
         [
             shape((3 * channels, n), bf16),
-            shape((blocks // 2,) + chunk, bf16),
-            shape((blocks // 2,) + chunk, bf16),
+            half,
+            half,
         ],
-        [place, out_w, place_rows, *layer, late_sums, *grads],
+        [place, out_w, place_rows, *layer, *grads],
         [pltpu.VMEM((channels, n), bf16), some_heads, some_heads],
         us=9,
     )
     got = swap(send, 1, devices)
     backs = call(
-        partial(rows_kernel, group),
+        partial(rows_kernel, cap),
         [size_send] * group,
         [me, qkv_w, delta, place_rows],
         us=2,
     )
-    pieces = add_parts(me, [keep, got], 4)
+    pieces = add_parts(me, [[keep, got], [late_keep, late_got]])
     masks = stage_masks((1, 2))
     parts = [pieces[0]] + [swap(pieces[i], masks[i], devices) for i in range(1, 4)]
-    (total,) = add_parts(me, parts, 1)
+    (total,) = add_parts(me, [parts])
     backs = exchange(backs, devices)
     for stage in whole_stages:
         parts = [total] + [swap(total, m, devices) for m in stage_masks(stage)[1:]]
-        (total,) = add_parts(me, parts, 1)
+        (total,) = add_parts(me, [parts])
     (input_grad,) = call(
         partial(join_kernel, group, cap), [size_rows], [me, slots, mid, *backs]
     )
@@ -447,7 +461,10 @@
         partial(finish_kernel, float((n * devices) ** -0.5)),
         [shape(qkv_weight.shape, f32), shape(out_weight.shape, f32)],
         [place, *parts],
-        [pltpu.VMEM((blocks, 2) + (chunk[0] // 2, channels), f32), pltpu.SemaphoreType.DMA((blocks, 2))],
+        [
+            pltpu.VMEM((blocks, 2) + half.shape[1:], f32),
+            pltpu.SemaphoreType.DMA((blocks, 2)),
+        ],
         out=pltpu.HBM,
     )
     return (input_grad, qkv_grad, out_w_grad)

time: 72.1 us -> 71.3 us (0.989)
  waiting for transfers between devices: 19.4 us -> 18.6 us
    ppermute x23 -> x24, waiting for transfers between devices: 19.4 us -> 18.6 us  [swap(): return lax.ppermute(x, AXES, [(d, d ^ mask) for d in range(devices)])]
    ppermute x23 -> x24, starting transfers between devices: 19.8 us -> 20.1 us  [swap(): return lax.ppermute(x, AXES, [(d, d ^ mask) for d in range(devices)])]
  transfers between devices with their start and end apart: 23 -> 24, of which waited for: 10 -> 10; matrix products, arithmetic and copies ran while one was open for 0% -> 0% of each run, Pallas kernels for 29% -> 39%
where the time goes in v5:
time: 71.3 us; the launch traced here: 71.2 us
  Pallas kernels  31.5 us (44%)
  starting transfers between devices  20.1 us (28%)
  waiting for transfers between devices  18.6 us (26%)
  between operations  0.92 us (1%)
    pallas_call x10, Pallas kernels, call(): pl.pallas_call(body, out_shape=tuple(out_shape), in_specs=[pl.BlockSpec(m...  31.5 us
    ppermute x24, starting transfers between devices, swap(): return lax.ppermute(x, AXES, [(d, d ^ mask) for d in range(devices)])  20.1 us
    ppermute x24, waiting for transfers between devices, swap(): return lax.ppermute(x, AXES, [(d, d ^ mask) for d in range(devices)])  18.6 us
  transfers between devices with their start and end apart: 24, of which 10 were waited for; matrix products, arithmetic and copies ran while one was open for 0% of the time, Pallas kernels for 39%

profile of v5, /device:TPU:0, one launch (start us, length us, event | category | flops | bytes accessed | tf_op | source)
XLA Modules:
  0.0 71.2 jit_solution(14682188253524493644)
XLA Ops:
  0.6 1.8 %shard_map.85 = (s32[1,512]{1,0:T(1,128)S(1)}, bf16[208,256]{1,0:T(8,128)(2,1)S(1)}, bf16[208,256]{1,0:T(8,128)(2,1)S(1)}, bf16[208,256]{1,0:T(8,128)(2,1)S(1)},...) custom-call(s32[1]{0:T(128)} %bitcast.me_ref, ...), custom_call_target="tpu_custom_call" | custom-call | flops 2000000000 | bytes 1048576 | tf_op jit(solution)/shard_map/pallas_call | solution.py:32
  2.9 2.6 %collective-permute-start.1 = (bf16[208,256]{1,0:T(8,128)(2,1)S(1)}, bf16[208,256]{1,0:T(8,128)(2,1)S(1)}, u32[]{:S(2)}, u32[]{:S(2)}) collective-permute-start(bf16[208,256]{1,0:T(8,128)(2,1)S(1)} %get-tuple-element.45), channel_id=1, source_target_pairs={{0,2},{1,3},{2,0},{3,1},{4,6},{5,7},{6,4},{7,5},{8,10},{9,11},{10,... | collective-permute-start | bytes 319496 | tf_op jit(solution)/shard_map/ppermute | solution.py:345
  5.6 12.1 %shard_map.87 = (bf16[512,256]{1,0:T(8,128)(2,1)S(1)}, bf16[4,128,256]{2,1,0:T(8,128)(2,1)S(1)}, bf16[4,128,256]{2,1,0:T(8,128)(2,1)S(1)}, bf16[192,256]{1,0:T(8...) custom-call(s32[1]{0:T(128)} %bitcast.1.me_ref, ...), custom_call_target="tpu_custom_call" | custom-call | flops 16000000000 | bytes 1048576 | tf_op jit(solution)/shard_map/pallas_call | solution.py:32
  17.9 1.9 %collective-permute-start.4 = (bf16[192,256]{1,0:T(8,128)(2,1)S(1)}, bf16[192,256]{1,0:T(8,128)(2,1)S(1)}, u32[]{:S(2)}, u32[]{:S(2)}) collective-permute-start(bf16[192,256]{1,0:T(8,128)(2,1)S(1)} %get-tuple-element.59), channel_id=1, source_target_pairs={{0,2},{1,3},{2,0},{3,1},{4,6},{5,7},{6,4},{7,5},{8,10},{9,11},{10,... | collective-permute-start | bytes 294920 | tf_op jit(solution)/shard_map/ppermute | solution.py:345
  20.1 6.8 %shard_map.86 = (bf16[512,768]{1,0:T(8,128)(2,1)S(1)}, bf16[256,512]{1,0:T(8,128)(2,1)S(1)}, bf16[768,512]{1,0:T(8,128)(2,1)S(1)}, bf16[16,512,512]{2,1,0:T(8,12...) custom-call(s32[1]{0:T(128)} %bitcast.me_ref, ...), custom_call_target="tpu_custom_call" | custom-call | flops 7000000000 | bytes 1048576 | tf_op jit(solution)/shard_map/pallas_call | solution.py:32
  26.9 7.1 %shard_map.88 = (bf16[768,512]{1,0:T(8,128)(2,1)S(1)}, bf16[4,128,256]{2,1,0:T(8,128)(2,1)S(1)}, bf16[4,128,256]{2,1,0:T(8,128)(2,1)S(1)}) custom-call(s32[1]{0:T(128)} %bitcast.1.me_ref, bf16[2,256,256]{2,1,0:T(8,128)(2,1)S(1)} %get-tuple-element.41.out_ref, bf16[512,768]{1,0:T(8,128)(2,1)S(1)} %get-tuple-element.47.place_ref, ...), custom_call_target="tpu_custom_call" | custom-call | flops 8999999488 | bytes 1048576 | tf_op jit(solution)/shard_map/pallas_call | solution.py:32
  34.4 1.2 %collective-permute-done.6.rest_1_ = bf16[4,128,256]{2,1,0:T(8,128)(2,1)S(1)} collective-permute-done((bf16[4,128,256]{2,1,0:T(8,128)(2,1)S(1)}, bf16[4,128,256]{2,1,0:T(8,128)(2,1)S(1)}, u32[]{:S(2)}, u32[]{:S(2)}) %collective-permute-start.6) | collective-permute-done | bytes 262176 | tf_op jit(solution)/shard_map/ppermute | solution.py:345
  35.7 2.0 %collective-permute-start.8 = (bf16[1,256,256]{2,1,0:T(8,128)(2,1)S(1)}, bf16[1,256,256]{2,1,0:T(8,128)(2,1)S(1)}, u32[]{:S(2)}, u32[]{:S(2)}) collective-permute-start(bf16[1,256,256]{2,1,0:T(8,128)(2,1)S(1)} %get-tuple-element.66), channel_id=1, source_target_pairs={{0,2},{1,3},{2,0},{3,1},{4,6},{5,7},{6,4},{7,5},{8,10},{9,11},{10,... | collective-permute-start | bytes 393224 | tf_op jit(solution)/shard_map/ppermute | solution.py:345
  37.7 1.5 %collective-permute-start.9 = (bf16[1,256,256]{2,1,0:T(8,128)(2,1)S(1)}, bf16[1,256,256]{2,1,0:T(8,128)(2,1)S(1)}, u32[]{:S(2)}, u32[]{:S(2)}) collective-permute-start(bf16[1,256,256]{2,1,0:T(8,128)(2,1)S(1)} %get-tuple-element.67), channel_id=1, source_target_pairs={{0,4},{1,5},{2,6},{3,7},{4,0},{5,1},{6,2},{7,3},{8,12},{9,13},{10,... | collective-permute-start | bytes 393224 | tf_op jit(solution)/shard_map/ppermute | solution.py:345
  39.3 0.8 %shard_map.92 = (bf16[192,256]{1,0:T(8,128)(2,1)S(1)}, bf16[192,256]{1,0:T(8,128)(2,1)S(1)}, bf16[192,256]{1,0:T(8,128)(2,1)S(1)}, bf16[192,256]{1,0:T(8,128)(2,1)S(1)}) custom-call(s32[1]{0:T(128)} %bitcast.me_ref, bf16[2,256,768]{2,1,0:T(8,128)(2,1)S(1)} %get-tuple-element.42.qkv_ref, bf16[768,512]{1,0:T(8,128)(2,1)S(1)} %get-tuple-element.70.delta, ...), custom_call_target="tpu_custom_call" | custom-call | flops 2000000000 | bytes 1048576 | tf_op jit(solution)/shard_map/pallas_call | solution.py:32
  40.2 2.0 %collective-permute-start.15 = (bf16[192,256]{1,0:T(8,128)(2,1)S(1)}, bf16[192,256]{1,0:T(8,128)(2,1)S(1)}, u32[]{:S(2)}, u32[]{:S(2)}) collective-permute-start(bf16[192,256]{1,0:T(8,128)(2,1)S(1)} %get-tuple-element.73), channel_id=1, source_target_pairs={{0,2},{1,3},{2,0},{3,1},{4,6},{5,7},{6,4},{7,5},{8,10},{9,11},{10,... | collective-permute-start | bytes 294920 | tf_op jit(solution)/shard_map/ppermute | solution.py:345
  42.2 2.8 %collective-permute-done.9.rest_2_ = bf16[1,256,256]{2,1,0:T(8,128)(2,1)S(1)} collective-permute-done((bf16[1,256,256]{2,1,0:T(8,128)(2,1)S(1)}, bf16[1,256,256]{2,1,0:T(8,128)(2,1)S(1)}, u32[]{:S(2)}, u32[]{:S(2)}) %collective-permute-start.9) | collective-permute-done | bytes 131104 | tf_op jit(solution)/shard_map/ppermute | solution.py:345
  45.1 1.4 %collective-permute-done.10.rest_3_ = bf16[1,256,256]{2,1,0:T(8,128)(2,1)S(1)} collective-permute-done((bf16[1,256,256]{2,1,0:T(8,128)(2,1)S(1)}, bf16[1,256,256]{2,1,0:T(8,128)(2,1)S(1)}, u32[]{:S(2)}, u32[]{:S(2)}) %collective-permute-start.10) | collective-permute-done | bytes 131104 | tf_op jit(solution)/shard_map/ppermute | solution.py:345
  46.5 3.7 %collective-permute-start.13 = (bf16[1,256,256]{2,1,0:T(8,128)(2,1)S(1)}, bf16[1,256,256]{2,1,0:T(8,128)(2,1)S(1)}, u32[]{:S(2)}, u32[]{:S(2)}) collective-permute-start(bf16[1,256,256]{2,1,0:T(8,128)(2,1)S(1)} %shard_map.90.rest_0_), channel_id=1, source_target_pairs={{0,24},{1,25},{2,26},{3,27},{4,28},{5,29},{6,30},{7,31},{8,16},{9,... | collective-permute-start | bytes 393224 | tf_op jit(solution)/shard_map/ppermute | solution.py:345
  50.2 0.8 %collective-permute-start.11 = (bf16[1,256,256]{2,1,0:T(8,128)(2,1)S(1)}, bf16[1,256,256]{2,1,0:T(8,128)(2,1)S(1)}, u32[]{:S(2)}, u32[]{:S(2)}) collective-permute-start(bf16[1,256,256]{2,1,0:T(8,128)(2,1)S(1)} %shard_map.90.rest_0_), channel_id=1, source_target_pairs={{0,8},{1,9},{2,10},{3,11},{4,12},{5,13},{6,14},{7,15},{8,0},{9,1},... | collective-permute-start | bytes 393224 | tf_op jit(solution)/shard_map/ppermute | solution.py:345
  51.0 1.2 %shard_map.93 = bf16[512,256]{1,0:T(8,128)(2,1)} custom-call(s32[1]{0:T(128)} %bitcast.me_ref, s32[1,512]{1,0:T(1,128)S(1)} %get-tuple-element.56.slots_ref, bf16[512,256]{1,0:T(8,128)(2,1)S(1)} %get-tuple-element.69.mid_ref, bf16[192,256]{1,0:T(8,128)(2,1)S(1)} %get-tuple-element.71.rest_0_, bf16[192,256]{1,0:T(8,128)(2,1)S(1)} %collective-permute-done.14.rest_1_, ...), custom_call_target="tpu_custom_call" | custom-call | flops 1000000000 | bytes 1048576 | tf_op jit(solution)/shard_map/pallas_call | solution.py:32
  52.2 2.0 %collective-permute-done.13.rest_3_ = bf16[1,256,256]{2,1,0:T(8,128)(2,1)S(1)} collective-permute-done((bf16[1,256,256]{2,1,0:T(8,128)(2,1)S(1)}, bf16[1,256,256]{2,1,0:T(8,128)(2,1)S(1)}, u32[]{:S(2)}, u32[]{:S(2)}) %collective-permute-start.13) | collective-permute-done | bytes 131104 | tf_op jit(solution)/shard_map/ppermute | solution.py:345
  54.2 5.4 %collective-permute-done.12.rest_2_ = bf16[1,256,256]{2,1,0:T(8,128)(2,1)S(1)} collective-permute-done((bf16[1,256,256]{2,1,0:T(8,128)(2,1)S(1)}, bf16[1,256,256]{2,1,0:T(8,128)(2,1)S(1)}, u32[]{:S(2)}, u32[]{:S(2)}) %collective-permute-start.12) | collective-permute-done | bytes 131104 | tf_op jit(solution)/shard_map/ppermute | solution.py:345
  59.7 1.7 %collective-permute-start.19 = (bf16[1,256,256]{2,1,0:T(8,128)(2,1)S(1)}, bf16[1,256,256]{2,1,0:T(8,128)(2,1)S(1)}, u32[]{:S(2)}, u32[]{:S(2)}) collective-permute-start(bf16[1,256,256]{2,1,0:T(8,128)(2,1)S(1)} %shard_map.91.rest_0_), channel_id=1, source_target_pairs={{0,6},{1,7},{2,4},{3,5},{4,2},{5,3},{6,0},{7,1},{8,14},{9,15},{10,... | collective-permute-start | bytes 393224 | tf_op jit(solution)/shard_map/ppermute | solution.py:345
  61.4 1.5 %collective-permute-start.18 = (bf16[1,256,256]{2,1,0:T(8,128)(2,1)S(1)}, bf16[1,256,256]{2,1,0:T(8,128)(2,1)S(1)}, u32[]{:S(2)}, u32[]{:S(2)}) collective-permute-start(bf16[1,256,256]{2,1,0:T(8,128)(2,1)S(1)} %shard_map.91.rest_0_), channel_id=1, source_target_pairs={{0,4},{1,5},{2,6},{3,7},{4,0},{5,1},{6,2},{7,3},{8,12},{9,13},{10,... | collective-permute-start | bytes 393224 | tf_op jit(solution)/shard_map/ppermute | solution.py:345
  63.2 3.6 %collective-permute-done.19.rest_3_ = bf16[1,256,256]{2,1,0:T(8,128)(2,1)S(1)} collective-permute-done((bf16[1,256,256]{2,1,0:T(8,128)(2,1)S(1)}, bf16[1,256,256]{2,1,0:T(8,128)(2,1)S(1)}, u32[]{:S(2)}, u32[]{:S(2)}) %collective-permute-start.19) | collective-permute-done | bytes 131104 | tf_op jit(solution)/shard_map/ppermute | solution.py:345
  66.9 1.1 %collective-permute-done.18.rest_2_ = bf16[1,256,256]{2,1,0:T(8,128)(2,1)S(1)} collective-permute-done((bf16[1,256,256]{2,1,0:T(8,128)(2,1)S(1)}, bf16[1,256,256]{2,1,0:T(8,128)(2,1)S(1)}, u32[]{:S(2)}, u32[]{:S(2)}) %collective-permute-start.18) | collective-permute-done | bytes 131104 | tf_op jit(solution)/shard_map/ppermute | solution.py:345
  68.5 0.8 %collective-permute-done.22.rest_6_ = bf16[1,256,256]{2,1,0:T(8,128)(2,1)S(1)} collective-permute-done((bf16[1,256,256]{2,1,0:T(8,128)(2,1)S(1)}, bf16[1,256,256]{2,1,0:T(8,128)(2,1)S(1)}, u32[]{:S(2)}, u32[]{:S(2)}) %collective-permute-start.22) | collective-permute-done | bytes 131104 | tf_op jit(solution)/shard_map/ppermute | solution.py:345
  69.5 1.5 %shard_map.94 = (f32[2,256,768]{2,1,0:T(8,128)}, f32[2,256,256]{2,1,0:T(8,128)}) custom-call(s32[1]{0:T(128)} %bitcast.1.me_ref, bf16[1,256,256]{2,1,0:T(8,128)(2,1)S(1)} %shard_map.91.rest_0_, bf16[1,256,256]{2,1,0:T(8,128)(2,1)S(1)} %collective-permute-done.17.rest_1_, bf16[1,256,256]{2,1,0:T(8,128)(2,1)S(1)} %collective-permute-done.18.rest_2_, ...), custom_call_target="tpu_custom_call" | custom-call | flops 1000000000 | bytes 1048576 | tf_op jit(solution)/shard_map/pallas_call | solution.py:32
  (34 shorter events, 3.0 us)
Async XLA Ops:
  2.4 17.4 %collective-permute-start = (bf16[208,256]{1,0:T(8,128)(2,1)S(1)}, bf16[208,256]{1,0:T(8,128)(2,1)S(1)}, u32[]{:S(2)}, u32[]{:S(2)}) collective-permute-start(bf16[208,256]{1,0:T(8,128)(2,1)S(1)} %get-tuple-element.44), channel_id=1, source_target_pairs={{0,1},{1,0},{2,3},{3,2},{4,5},{5,4},{6,7},{7,6},{8,9},{9,8},{10,11... | collective-permute-start | bytes 319496 | tf_op jit(solution)/shard_map/ppermute | solution.py:345
  2.9 16.9 %collective-permute-start.1 = (bf16[208,256]{1,0:T(8,128)(2,1)S(1)}, bf16[208,256]{1,0:T(8,128)(2,1)S(1)}, u32[]{:S(2)}, u32[]{:S(2)}) collective-permute-start(bf16[208,256]{1,0:T(8,128)(2,1)S(1)} %get-tuple-element.45), channel_id=1, source_target_pairs={{0,2},{1,3},{2,0},{3,1},{4,6},{5,7},{6,4},{7,5},{8,10},{9,11},{10,... | collective-permute-start | bytes 319496 | tf_op jit(solution)/shard_map/ppermute | solution.py:345
  5.5 14.6 %collective-permute-start.2 = (bf16[208,256]{1,0:T(8,128)(2,1)S(1)}, bf16[208,256]{1,0:T(8,128)(2,1)S(1)}, u32[]{:S(2)}, u32[]{:S(2)}) collective-permute-start(bf16[208,256]{1,0:T(8,128)(2,1)S(1)} %get-tuple-element.46), channel_id=1, source_target_pairs={{0,3},{1,2},{2,1},{3,0},{4,7},{5,6},{6,5},{7,4},{8,11},{9,10},{10,... | collective-permute-start | bytes 319496 | tf_op jit(solution)/shard_map/ppermute | solution.py:345
  17.7 9.1 %collective-permute-start.3 = (bf16[192,256]{1,0:T(8,128)(2,1)S(1)}, bf16[192,256]{1,0:T(8,128)(2,1)S(1)}, u32[]{:S(2)}, u32[]{:S(2)}) collective-permute-start(bf16[192,256]{1,0:T(8,128)(2,1)S(1)} %get-tuple-element.58), channel_id=1, source_target_pairs={{0,1},{1,0},{2,3},{3,2},{4,5},{5,4},{6,7},{7,6},{8,9},{9,8},{10,11... | collective-permute-start | bytes 294920 | tf_op jit(solution)/shard_map/ppermute | solution.py:345
  17.9 9.0 %collective-permute-start.4 = (bf16[192,256]{1,0:T(8,128)(2,1)S(1)}, bf16[192,256]{1,0:T(8,128)(2,1)S(1)}, u32[]{:S(2)}, u32[]{:S(2)}) collective-permute-start(bf16[192,256]{1,0:T(8,128)(2,1)S(1)} %get-tuple-element.59), channel_id=1, source_target_pairs={{0,2},{1,3},{2,0},{3,1},{4,6},{5,7},{6,4},{7,5},{8,10},{9,11},{10,... | collective-permute-start | bytes 294920 | tf_op jit(solution)/shard_map/ppermute | solution.py:345
  19.9 7.0 %collective-permute-start.5 = (bf16[192,256]{1,0:T(8,128)(2,1)S(1)}, bf16[192,256]{1,0:T(8,128)(2,1)S(1)}, u32[]{:S(2)}, u32[]{:S(2)}) collective-permute-start(bf16[192,256]{1,0:T(8,128)(2,1)S(1)} %get-tuple-element.60), channel_id=1, source_target_pairs={{0,3},{1,2},{2,1},{3,0},{4,7},{5,6},{6,5},{7,4},{8,11},{9,10},{10,... | collective-permute-start | bytes 294920 | tf_op jit(solution)/shard_map/ppermute | solution.py:345
  19.9 14.6 %collective-permute-start.7 = (bf16[4,128,256]{2,1,0:T(8,128)(2,1)S(1)}, bf16[4,128,256]{2,1,0:T(8,128)(2,1)S(1)}, u32[]{:S(2)}, u32[]{:S(2)}) collective-permute-start(bf16[4,128,256]{2,1,0:T(8,128)(2,1)S(1)} %get-tuple-element.64), channel_id=1, source_target_pairs={{0,1},{1,0},{2,3},{3,2},{4,5},{5,4},{6,7},{7,6},{8,9},{9,8},{10,11... | collective-permute-start | bytes 786440 | tf_op jit(solution)/shard_map/ppermute | solution.py:345
  34.0 1.6 %collective-permute-start.6 = (bf16[4,128,256]{2,1,0:T(8,128)(2,1)S(1)}, bf16[4,128,256]{2,1,0:T(8,128)(2,1)S(1)}, u32[]{:S(2)}, u32[]{:S(2)}) collective-permute-start(bf16[4,128,256]{2,1,0:T(8,128)(2,1)S(1)} %get-tuple-element.62), channel_id=1, source_target_pairs={{0,1},{1,0},{2,3},{3,2},{4,5},{5,4},{6,7},{7,6},{8,9},{9,8},{10,11... | collective-permute-start | bytes 786440 | tf_op jit(solution)/shard_map/ppermute | solution.py:345
  35.7 6.4 %collective-permute-start.8 = (bf16[1,256,256]{2,1,0:T(8,128)(2,1)S(1)}, bf16[1,256,256]{2,1,0:T(8,128)(2,1)S(1)}, u32[]{:S(2)}, u32[]{:S(2)}) collective-permute-start(bf16[1,256,256]{2,1,0:T(8,128)(2,1)S(1)} %get-tuple-element.66), channel_id=1, source_target_pairs={{0,2},{1,3},{2,0},{3,1},{4,6},{5,7},{6,4},{7,5},{8,10},{9,11},{10,... | collective-permute-start | bytes 393224 | tf_op jit(solution)/shard_map/ppermute | solution.py:345
  37.7 7.4 %collective-permute-start.9 = (bf16[1,256,256]{2,1,0:T(8,128)(2,1)S(1)}, bf16[1,256,256]{2,1,0:T(8,128)(2,1)S(1)}, u32[]{:S(2)}, u32[]{:S(2)}) collective-permute-start(bf16[1,256,256]{2,1,0:T(8,128)(2,1)S(1)} %get-tuple-element.67), channel_id=1, source_target_pairs={{0,4},{1,5},{2,6},{3,7},{4,0},{5,1},{6,2},{7,3},{8,12},{9,13},{10,... | collective-permute-start | bytes 393224 | tf_op jit(solution)/shard_map/ppermute | solution.py:345
  39.2 7.2 %collective-permute-start.10 = (bf16[1,256,256]{2,1,0:T(8,128)(2,1)S(1)}, bf16[1,256,256]{2,1,0:T(8,128)(2,1)S(1)}, u32[]{:S(2)}, u32[]{:S(2)}) collective-permute-start(bf16[1,256,256]{2,1,0:T(8,128)(2,1)S(1)} %get-tuple-element.68), channel_id=1, source_target_pairs={{0,6},{1,7},{2,4},{3,5},{4,2},{5,3},{6,0},{7,1},{8,14},{9,15},{10,... | collective-permute-start | bytes 393224 | tf_op jit(solution)/shard_map/ppermute | solution.py:345
  40.1 10.1 %collective-permute-start.14 = (bf16[192,256]{1,0:T(8,128)(2,1)S(1)}, bf16[192,256]{1,0:T(8,128)(2,1)S(1)}, u32[]{:S(2)}, u32[]{:S(2)}) collective-permute-start(bf16[192,256]{1,0:T(8,128)(2,1)S(1)} %get-tuple-element.72), channel_id=1, source_target_pairs={{0,1},{1,0},{2,3},{3,2},{4,5},{5,4},{6,7},{7,6},{8,9},{9,8},{10,11... | collective-permute-start | bytes 294920 | tf_op jit(solution)/shard_map/ppermute | solution.py:345
  40.2 10.8 %collective-permute-start.15 = (bf16[192,256]{1,0:T(8,128)(2,1)S(1)}, bf16[192,256]{1,0:T(8,128)(2,1)S(1)}, u32[]{:S(2)}, u32[]{:S(2)}) collective-permute-start(bf16[192,256]{1,0:T(8,128)(2,1)S(1)} %get-tuple-element.73), channel_id=1, source_target_pairs={{0,2},{1,3},{2,0},{3,1},{4,6},{5,7},{6,4},{7,5},{8,10},{9,11},{10,... | collective-permute-start | bytes 294920 | tf_op jit(solution)/shard_map/ppermute | solution.py:345
  42.2 8.8 %collective-permute-start.16 = (bf16[192,256]{1,0:T(8,128)(2,1)S(1)}, bf16[192,256]{1,0:T(8,128)(2,1)S(1)}, u32[]{:S(2)}, u32[]{:S(2)}) collective-permute-start(bf16[192,256]{1,0:T(8,128)(2,1)S(1)} %get-tuple-element.74), channel_id=1, source_target_pairs={{0,3},{1,2},{2,1},{3,0},{4,7},{5,6},{6,5},{7,4},{8,11},{9,10},{10,... | collective-permute-start | bytes 294920 | tf_op jit(solution)/shard_map/ppermute | solution.py:345
  46.5 7.7 %collective-permute-start.13 = (bf16[1,256,256]{2,1,0:T(8,128)(2,1)S(1)}, bf16[1,256,256]{2,1,0:T(8,128)(2,1)S(1)}, u32[]{:S(2)}, u32[]{:S(2)}) collective-permute-start(bf16[1,256,256]{2,1,0:T(8,128)(2,1)S(1)} %shard_map.90.rest_0_), channel_id=1, source_target_pairs={{0,24},{1,25},{2,26},{3,27},{4,28},{5,29},{6,30},{7,31},{8,16},{9,... | collective-permute-start | bytes 393224 | tf_op jit(solution)/shard_map/ppermute | solution.py:345
  50.2 9.4 %collective-permute-start.12 = (bf16[1,256,256]{2,1,0:T(8,128)(2,1)S(1)}, bf16[1,256,256]{2,1,0:T(8,128)(2,1)S(1)}, u32[]{:S(2)}, u32[]{:S(2)}) collective-permute-start(bf16[1,256,256]{2,1,0:T(8,128)(2,1)S(1)} %shard_map.90.rest_0_), channel_id=1, source_target_pairs={{0,16},{1,17},{2,18},{3,19},{4,20},{5,21},{6,22},{7,23},{8,24},{9,... | collective-permute-start | bytes 393224 | tf_op jit(solution)/shard_map/ppermute | solution.py:345
  50.2 9.4 %collective-permute-start.11 = (bf16[1,256,256]{2,1,0:T(8,128)(2,1)S(1)}, bf16[1,256,256]{2,1,0:T(8,128)(2,1)S(1)}, u32[]{:S(2)}, u32[]{:S(2)}) collective-permute-start(bf16[1,256,256]{2,1,0:T(8,128)(2,1)S(1)} %shard_map.90.rest_0_), channel_id=1, source_target_pairs={{0,8},{1,9},{2,10},{3,11},{4,12},{5,13},{6,14},{7,15},{8,0},{9,1},... | collective-permute-start | bytes 393224 | tf_op jit(solution)/shard_map/ppermute | solution.py:345
  59.7 7.2 %collective-permute-start.19 = (bf16[1,256,256]{2,1,0:T(8,128)(2,1)S(1)}, bf16[1,256,256]{2,1,0:T(8,128)(2,1)S(1)}, u32[]{:S(2)}, u32[]{:S(2)}) collective-permute-start(bf16[1,256,256]{2,1,0:T(8,128)(2,1)S(1)} %shard_map.91.rest_0_), channel_id=1, source_target_pairs={{0,6},{1,7},{2,4},{3,5},{4,2},{5,3},{6,0},{7,1},{8,14},{9,15},{10,... | collective-permute-start | bytes 393224 | tf_op jit(solution)/shard_map/ppermute | solution.py:345
  61.4 6.5 %collective-permute-start.18 = (bf16[1,256,256]{2,1,0:T(8,128)(2,1)S(1)}, bf16[1,256,256]{2,1,0:T(8,128)(2,1)S(1)}, u32[]{:S(2)}, u32[]{:S(2)}) collective-permute-start(bf16[1,256,256]{2,1,0:T(8,128)(2,1)S(1)} %shard_map.91.rest_0_), channel_id=1, source_target_pairs={{0,4},{1,5},{2,6},{3,7},{4,0},{5,1},{6,2},{7,3},{8,12},{9,13},{10,... | collective-permute-start | bytes 393224 | tf_op jit(solution)/shard_map/ppermute | solution.py:345
  62.9 5.1 %collective-permute-start.17 = (bf16[1,256,256]{2,1,0:T(8,128)(2,1)S(1)}, bf16[1,256,256]{2,1,0:T(8,128)(2,1)S(1)}, u32[]{:S(2)}, u32[]{:S(2)}) collective-permute-start(bf16[1,256,256]{2,1,0:T(8,128)(2,1)S(1)} %shard_map.91.rest_0_), channel_id=1, source_target_pairs={{0,2},{1,3},{2,0},{3,1},{4,6},{5,7},{6,4},{7,5},{8,10},{9,11},{10,... | collective-permute-start | bytes 393224 | tf_op jit(solution)/shard_map/ppermute | solution.py:345
  63.2 5.2 %collective-permute-start.20 = (bf16[1,256,256]{2,1,0:T(8,128)(2,1)S(1)}, bf16[1,256,256]{2,1,0:T(8,128)(2,1)S(1)}, u32[]{:S(2)}, u32[]{:S(2)}) collective-permute-start(bf16[1,256,256]{2,1,0:T(8,128)(2,1)S(1)} %shard_map.91.rest_0_), channel_id=1, source_target_pairs={{0,1},{1,0},{2,3},{3,2},{4,5},{5,4},{6,7},{7,6},{8,9},{9,8},{10,11... | collective-permute-start | bytes 393224 | tf_op jit(solution)/shard_map/ppermute | solution.py:345
  66.9 1.6 %collective-permute-start.23 = (bf16[1,256,256]{2,1,0:T(8,128)(2,1)S(1)}, bf16[1,256,256]{2,1,0:T(8,128)(2,1)S(1)}, u32[]{:S(2)}, u32[]{:S(2)}) collective-permute-start(bf16[1,256,256]{2,1,0:T(8,128)(2,1)S(1)} %collective-permute-done.19.rest_3_), channel_id=1, source_target_pairs={{0,1},{1,0},{2,3},{3,2},{4,5},{5,4},{6,7},{7,6},{8,9},{9,8},{10,11... | collective-permute-start | bytes 393224 | tf_op jit(solution)/shard_map/ppermute | solution.py:345
  68.0 1.3 %collective-permute-start.22 = (bf16[1,256,256]{2,1,0:T(8,128)(2,1)S(1)}, bf16[1,256,256]{2,1,0:T(8,128)(2,1)S(1)}, u32[]{:S(2)}, u32[]{:S(2)}) collective-permute-start(bf16[1,256,256]{2,1,0:T(8,128)(2,1)S(1)} %collective-permute-done.18.rest_2_), channel_id=1, source_target_pairs={{0,1},{1,0},{2,3},{3,2},{4,5},{5,4},{6,7},{7,6},{8,9},{9,8},{10,11... | collective-permute-start | bytes 393224 | tf_op jit(solution)/shard_map/ppermute | solution.py:345
  68.0 1.5 %collective-permute-start.21 = (bf16[1,256,256]{2,1,0:T(8,128)(2,1)S(1)}, bf16[1,256,256]{2,1,0:T(8,128)(2,1)S(1)}, u32[]{:S(2)}, u32[]{:S(2)}) collective-permute-start(bf16[1,256,256]{2,1,0:T(8,128)(2,1)S(1)} %collective-permute-done.17.rest_1_), channel_id=1, source_target_pairs={{0,1},{1,0},{2,3},{3,2},{4,5},{5,4},{6,7},{7,6},{8,9},{9,8},{10,11... | collective-permute-start | bytes 393224 | tf_op jit(solution)/shard_map/ppermute | solution.py:345

commit v6 on v5

--- a/solution.py
+++ b/solution.py
@@ -68,7 +68,7 @@
 
 def route_kernel(group, cap, me_ref, tz_hbm, rows_hbm, h_hbm, g_hbm, qkv_hbm, out_hbm, *rest):
     slots_ref, send_refs = rest[0], rest[1 : 1 + group]
-    tz_ref, rows_ref, sems = rest[5 + group :]
+    tz_ref, rows_ref, earlier_ref, sems = rest[5 + group :]
     sources = (tz_hbm, rows_hbm, h_hbm, g_hbm, qkv_hbm, out_hbm)
     targets = (tz_ref, rows_ref) + tuple(rest[1 + group : 5 + group])
     copies = [
@@ -76,9 +76,12 @@
     ]
     for copy in copies:
         copy.start()
+    n, channels = rows_ref.shape
+    earlier_ref[...] = jnp.where(
+        lax.broadcasted_iota(i32, (n, n), 0) < lax.broadcasted_iota(i32, (n, n), 1), 1.0, 0.0
+    ).astype(bf16)
     copies[0].wait()
     copies[1].wait()
-    n, channels = rows_ref.shape
     here = me_ref[0] % group
     target = tz_ref[...]
     partner = (target // n % group) ^ here
@@ -86,10 +89,7 @@
     lanes = max(16, group)
     which = lax.broadcasted_iota(i32, (lanes, n), 0)
     mine = jnp.where(which == partner, 1.0, 0.0)
-    earlier = jnp.where(
-        lax.broadcasted_iota(i32, (n, n), 0) < lax.broadcasted_iota(i32, (n, n), 1), 1.0, 0.0
-    ).astype(bf16)
-    before = dg(mine.astype(bf16), earlier, 1, 0)
+    before = dg(mine.astype(bf16), earlier_ref[...], 1, 0)
     rank = jnp.sum(mine * before, axis=0, keepdims=True).astype(i32)
     slots = partner * cap + rank
     slots_ref[...] = slots
@@ -109,9 +109,12 @@
         copy.wait()
 
 
-def two_terms(x):
-    high = x.astype(bf16)
-    return jnp.concatenate([high, (x - high.astype(f32)).astype(bf16)], axis=0)
+def three_terms(x):
+    parts = []
+    for _ in range(3):
+        parts.append(x.astype(bf16))
+        x = x - parts[-1].astype(f32)
+    return jnp.concatenate(parts, axis=0)
 
 
 class Heads:
@@ -130,7 +133,7 @@
     def scores(self, head):
         k = self.rows(self.proj, 1, head)
         q = self.rows(self.proj, 0, head).astype(f32) * (self.size**-0.5 * LOG2E)
-        self.held["s", head] = dg(jnp.concatenate([k, k], axis=0), two_terms(q), 0, 0)
+        self.held["s", head] = dg(jnp.concatenate([k] * 3, axis=0), three_terms(q), 0, 0)
 
     def softmax(self, head):
         scores = self.held.pop(("s", head))
@@ -152,9 +155,9 @@
         inverse = self.inv[head : head + 1, :]
         centre = jnp.sum(self.rows(self.att, 0, head) * o, axis=0, keepdims=True) * inverse
         v = self.rows(self.proj, 2, head)
-        o = two_terms(o * inverse)
-        self.held["p", head] = dg(jnp.concatenate([v, v], axis=0), o, 0, 0) - centre
-        self.held["o", head] = o
+        o = three_terms(o * inverse)
+        self.held["p", head] = dg(jnp.concatenate([v] * 3, axis=0), o, 0, 0) - centre
+        self.held["o", head] = o[0 : 2 * self.size]
 
     def score_grad(self, head):
         slot = head % self.grads.shape[0]
@@ -386,6 +389,7 @@
         [
             pltpu.VMEM((1, n), i32),
             pltpu.VMEM((n, channels), bf16),
+            pltpu.VMEM((n, n), bf16),
             pltpu.SemaphoreType.DMA((6,)),
         ],
         us=2,

time: 71.3 us -> 71.2 us (level)
  transfers between devices with their start and end apart: 24 -> 24, of which waited for: 10 -> 9; matrix products, arithmetic and copies ran while one was open for 0% -> 0% of each run, Pallas kernels for 39% -> 39%
where the time goes in v6:
time: 71.2 us; the launch traced here: 71 us
  Pallas kernels  31.4 us (44%)
  starting transfers between devices  20.1 us (28%)
  waiting for transfers between devices  18.7 us (26%)
  between operations  0.92 us (1%)
    pallas_call x10, Pallas kernels, call(): pl.pallas_call(body, out_shape=tuple(out_shape), in_specs=[pl.BlockSpec(m...  31.4 us
    ppermute x24, starting transfers between devices, swap(): return lax.ppermute(x, AXES, [(d, d ^ mask) for d in range(devices)])  20.1 us
    ppermute x24, waiting for transfers between devices, swap(): return lax.ppermute(x, AXES, [(d, d ^ mask) for d in range(devices)])  18.7 us
  transfers between devices with their start and end apart: 24, of which 9 were waited for; matrix products, arithmetic and copies ran while one was open for 0% of the time, Pallas kernels for 39%

profile of v6, /device:TPU:0, one launch (start us, length us, event | category | flops | bytes accessed | tf_op | source)
XLA Modules:
  0.0 71.0 jit_solution(1542559294171958175)
XLA Ops:
  0.6 1.8 %shard_map.85 = (s32[1,512]{1,0:T(1,128)S(1)}, bf16[208,256]{1,0:T(8,128)(2,1)S(1)}, bf16[208,256]{1,0:T(8,128)(2,1)S(1)}, bf16[208,256]{1,0:T(8,128)(2,1)S(1)},...) custom-call(s32[1]{0:T(128)} %bitcast.me_ref, ...), custom_call_target="tpu_custom_call" | custom-call | flops 2000000000 | bytes 1048576 | tf_op jit(solution)/shard_map/pallas_call | solution.py:32
  2.9 2.6 %collective-permute-start.1 = (bf16[208,256]{1,0:T(8,128)(2,1)S(1)}, bf16[208,256]{1,0:T(8,128)(2,1)S(1)}, u32[]{:S(2)}, u32[]{:S(2)}) collective-permute-start(bf16[208,256]{1,0:T(8,128)(2,1)S(1)} %get-tuple-element.45), channel_id=1, source_target_pairs={{0,2},{1,3},{2,0},{3,1},{4,6},{5,7},{6,4},{7,5},{8,10},{9,11},{10,... | collective-permute-start | bytes 319496 | tf_op jit(solution)/shard_map/ppermute | solution.py:348
  5.6 12.2 %shard_map.87 = (bf16[512,256]{1,0:T(8,128)(2,1)S(1)}, bf16[4,128,256]{2,1,0:T(8,128)(2,1)S(1)}, bf16[4,128,256]{2,1,0:T(8,128)(2,1)S(1)}, bf16[192,256]{1,0:T(8...) custom-call(s32[1]{0:T(128)} %bitcast.1.me_ref, ...), custom_call_target="tpu_custom_call" | custom-call | flops 16000000000 | bytes 1048576 | tf_op jit(solution)/shard_map/pallas_call | solution.py:32
  18.0 1.9 %collective-permute-start.4 = (bf16[192,256]{1,0:T(8,128)(2,1)S(1)}, bf16[192,256]{1,0:T(8,128)(2,1)S(1)}, u32[]{:S(2)}, u32[]{:S(2)}) collective-permute-start(bf16[192,256]{1,0:T(8,128)(2,1)S(1)} %get-tuple-element.59), channel_id=1, source_target_pairs={{0,2},{1,3},{2,0},{3,1},{4,6},{5,7},{6,4},{7,5},{8,10},{9,11},{10,... | collective-permute-start | bytes 294920 | tf_op jit(solution)/shard_map/ppermute | solution.py:348
  20.2 6.7 %shard_map.86 = (bf16[512,768]{1,0:T(8,128)(2,1)S(1)}, bf16[256,512]{1,0:T(8,128)(2,1)S(1)}, bf16[768,512]{1,0:T(8,128)(2,1)S(1)}, bf16[16,512,512]{2,1,0:T(8,12...) custom-call(s32[1]{0:T(128)} %bitcast.me_ref, ...), custom_call_target="tpu_custom_call" | custom-call | flops 7000000000 | bytes 1048576 | tf_op jit(solution)/shard_map/pallas_call | solution.py:32
  26.9 6.9 %shard_map.88 = (bf16[768,512]{1,0:T(8,128)(2,1)S(1)}, bf16[4,128,256]{2,1,0:T(8,128)(2,1)S(1)}, bf16[4,128,256]{2,1,0:T(8,128)(2,1)S(1)}) custom-call(s32[1]{0:T(128)} %bitcast.1.me_ref, bf16[2,256,256]{2,1,0:T(8,128)(2,1)S(1)} %get-tuple-element.41.out_ref, bf16[512,768]{1,0:T(8,128)(2,1)S(1)} %get-tuple-element.47.place_ref, ...), custom_call_target="tpu_custom_call" | custom-call | flops 8999999488 | bytes 1048576 | tf_op jit(solution)/shard_map/pallas_call | solution.py:32
  34.2 1.2 %collective-permute-done.6.rest_1_ = bf16[4,128,256]{2,1,0:T(8,128)(2,1)S(1)} collective-permute-done((bf16[4,128,256]{2,1,0:T(8,128)(2,1)S(1)}, bf16[4,128,256]{2,1,0:T(8,128)(2,1)S(1)}, u32[]{:S(2)}, u32[]{:S(2)}) %collective-permute-start.6) | collective-permute-done | bytes 262176 | tf_op jit(solution)/shard_map/ppermute | solution.py:348
  35.5 2.0 %collective-permute-start.8 = (bf16[1,256,256]{2,1,0:T(8,128)(2,1)S(1)}, bf16[1,256,256]{2,1,0:T(8,128)(2,1)S(1)}, u32[]{:S(2)}, u32[]{:S(2)}) collective-permute-start(bf16[1,256,256]{2,1,0:T(8,128)(2,1)S(1)} %get-tuple-element.66), channel_id=1, source_target_pairs={{0,2},{1,3},{2,0},{3,1},{4,6},{5,7},{6,4},{7,5},{8,10},{9,11},{10,... | collective-permute-start | bytes 393224 | tf_op jit(solution)/shard_map/ppermute | solution.py:348
  37.5 1.5 %collective-permute-start.9 = (bf16[1,256,256]{2,1,0:T(8,128)(2,1)S(1)}, bf16[1,256,256]{2,1,0:T(8,128)(2,1)S(1)}, u32[]{:S(2)}, u32[]{:S(2)}) collective-permute-start(bf16[1,256,256]{2,1,0:T(8,128)(2,1)S(1)} %get-tuple-element.67), channel_id=1, source_target_pairs={{0,4},{1,5},{2,6},{3,7},{4,0},{5,1},{6,2},{7,3},{8,12},{9,13},{10,... | collective-permute-start | bytes 393224 | tf_op jit(solution)/shard_map/ppermute | solution.py:348
  39.1 0.8 %shard_map.92 = (bf16[192,256]{1,0:T(8,128)(2,1)S(1)}, bf16[192,256]{1,0:T(8,128)(2,1)S(1)}, bf16[192,256]{1,0:T(8,128)(2,1)S(1)}, bf16[192,256]{1,0:T(8,128)(2,1)S(1)}) custom-call(s32[1]{0:T(128)} %bitcast.me_ref, bf16[2,256,768]{2,1,0:T(8,128)(2,1)S(1)} %get-tuple-element.42.qkv_ref, bf16[768,512]{1,0:T(8,128)(2,1)S(1)} %get-tuple-element.70.delta, ...), custom_call_target="tpu_custom_call" | custom-call | flops 2000000000 | bytes 1048576 | tf_op jit(solution)/shard_map/pallas_call | solution.py:32
  40.0 2.0 %collective-permute-start.15 = (bf16[192,256]{1,0:T(8,128)(2,1)S(1)}, bf16[192,256]{1,0:T(8,128)(2,1)S(1)}, u32[]{:S(2)}, u32[]{:S(2)}) collective-permute-start(bf16[192,256]{1,0:T(8,128)(2,1)S(1)} %get-tuple-element.73), channel_id=1, source_target_pairs={{0,2},{1,3},{2,0},{3,1},{4,6},{5,7},{6,4},{7,5},{8,10},{9,11},{10,... | collective-permute-start | bytes 294920 | tf_op jit(solution)/shard_map/ppermute | solution.py:348
  42.0 2.8 %collective-permute-done.9.rest_2_ = bf16[1,256,256]{2,1,0:T(8,128)(2,1)S(1)} collective-permute-done((bf16[1,256,256]{2,1,0:T(8,128)(2,1)S(1)}, bf16[1,256,256]{2,1,0:T(8,128)(2,1)S(1)}, u32[]{:S(2)}, u32[]{:S(2)}) %collective-permute-start.9) | collective-permute-done | bytes 131104 | tf_op jit(solution)/shard_map/ppermute | solution.py:348
  44.9 1.4 %collective-permute-done.10.rest_3_ = bf16[1,256,256]{2,1,0:T(8,128)(2,1)S(1)} collective-permute-done((bf16[1,256,256]{2,1,0:T(8,128)(2,1)S(1)}, bf16[1,256,256]{2,1,0:T(8,128)(2,1)S(1)}, u32[]{:S(2)}, u32[]{:S(2)}) %collective-permute-start.10) | collective-permute-done | bytes 131104 | tf_op jit(solution)/shard_map/ppermute | solution.py:348
  46.3 3.7 %collective-permute-start.13 = (bf16[1,256,256]{2,1,0:T(8,128)(2,1)S(1)}, bf16[1,256,256]{2,1,0:T(8,128)(2,1)S(1)}, u32[]{:S(2)}, u32[]{:S(2)}) collective-permute-start(bf16[1,256,256]{2,1,0:T(8,128)(2,1)S(1)} %shard_map.90.rest_0_), channel_id=1, source_target_pairs={{0,24},{1,25},{2,26},{3,27},{4,28},{5,29},{6,30},{7,31},{8,16},{9,... | collective-permute-start | bytes 393224 | tf_op jit(solution)/shard_map/ppermute | solution.py:348
  50.0 0.8 %collective-permute-start.11 = (bf16[1,256,256]{2,1,0:T(8,128)(2,1)S(1)}, bf16[1,256,256]{2,1,0:T(8,128)(2,1)S(1)}, u32[]{:S(2)}, u32[]{:S(2)}) collective-permute-start(bf16[1,256,256]{2,1,0:T(8,128)(2,1)S(1)} %shard_map.90.rest_0_), channel_id=1, source_target_pairs={{0,8},{1,9},{2,10},{3,11},{4,12},{5,13},{6,14},{7,15},{8,0},{9,1},... | collective-permute-start | bytes 393224 | tf_op jit(solution)/shard_map/ppermute | solution.py:348
  50.8 1.2 %shard_map.93 = bf16[512,256]{1,0:T(8,128)(2,1)} custom-call(s32[1]{0:T(128)} %bitcast.me_ref, s32[1,512]{1,0:T(1,128)S(1)} %get-tuple-element.56.slots_ref, bf16[512,256]{1,0:T(8,128)(2,1)S(1)} %get-tuple-element.69.mid_ref, bf16[192,256]{1,0:T(8,128)(2,1)S(1)} %get-tuple-element.71.rest_0_, bf16[192,256]{1,0:T(8,128)(2,1)S(1)} %collective-permute-done.14.rest_1_, ...), custom_call_target="tpu_custom_call" | custom-call | flops 1000000000 | bytes 1048576 | tf_op jit(solution)/shard_map/pallas_call | solution.py:32
  52.0 2.1 %collective-permute-done.13.rest_3_ = bf16[1,256,256]{2,1,0:T(8,128)(2,1)S(1)} collective-permute-done((bf16[1,256,256]{2,1,0:T(8,128)(2,1)S(1)}, bf16[1,256,256]{2,1,0:T(8,128)(2,1)S(1)}, u32[]{:S(2)}, u32[]{:S(2)}) %collective-permute-start.13) | collective-permute-done | bytes 131104 | tf_op jit(solution)/shard_map/ppermute | solution.py:348
  54.1 5.4 %collective-permute-done.12.rest_2_ = bf16[1,256,256]{2,1,0:T(8,128)(2,1)S(1)} collective-permute-done((bf16[1,256,256]{2,1,0:T(8,128)(2,1)S(1)}, bf16[1,256,256]{2,1,0:T(8,128)(2,1)S(1)}, u32[]{:S(2)}, u32[]{:S(2)}) %collective-permute-start.12) | collective-permute-done | bytes 131104 | tf_op jit(solution)/shard_map/ppermute | solution.py:348
  59.5 1.7 %collective-permute-start.19 = (bf16[1,256,256]{2,1,0:T(8,128)(2,1)S(1)}, bf16[1,256,256]{2,1,0:T(8,128)(2,1)S(1)}, u32[]{:S(2)}, u32[]{:S(2)}) collective-permute-start(bf16[1,256,256]{2,1,0:T(8,128)(2,1)S(1)} %shard_map.91.rest_0_), channel_id=1, source_target_pairs={{0,6},{1,7},{2,4},{3,5},{4,2},{5,3},{6,0},{7,1},{8,14},{9,15},{10,... | collective-permute-start | bytes 393224 | tf_op jit(solution)/shard_map/ppermute | solution.py:348
  61.2 1.5 %collective-permute-start.18 = (bf16[1,256,256]{2,1,0:T(8,128)(2,1)S(1)}, bf16[1,256,256]{2,1,0:T(8,128)(2,1)S(1)}, u32[]{:S(2)}, u32[]{:S(2)}) collective-permute-start(bf16[1,256,256]{2,1,0:T(8,128)(2,1)S(1)} %shard_map.91.rest_0_), channel_id=1, source_target_pairs={{0,4},{1,5},{2,6},{3,7},{4,0},{5,1},{6,2},{7,3},{8,12},{9,13},{10,... | collective-permute-start | bytes 393224 | tf_op jit(solution)/shard_map/ppermute | solution.py:348
  63.1 3.5 %collective-permute-done.19.rest_3_ = bf16[1,256,256]{2,1,0:T(8,128)(2,1)S(1)} collective-permute-done((bf16[1,256,256]{2,1,0:T(8,128)(2,1)S(1)}, bf16[1,256,256]{2,1,0:T(8,128)(2,1)S(1)}, u32[]{:S(2)}, u32[]{:S(2)}) %collective-permute-start.19) | collective-permute-done | bytes 131104 | tf_op jit(solution)/shard_map/ppermute | solution.py:348
  66.6 1.2 %collective-permute-done.18.rest_2_ = bf16[1,256,256]{2,1,0:T(8,128)(2,1)S(1)} collective-permute-done((bf16[1,256,256]{2,1,0:T(8,128)(2,1)S(1)}, bf16[1,256,256]{2,1,0:T(8,128)(2,1)S(1)}, u32[]{:S(2)}, u32[]{:S(2)}) %collective-permute-start.18) | collective-permute-done | bytes 131104 | tf_op jit(solution)/shard_map/ppermute | solution.py:348
  68.3 0.8 %collective-permute-done.22.rest_6_ = bf16[1,256,256]{2,1,0:T(8,128)(2,1)S(1)} collective-permute-done((bf16[1,256,256]{2,1,0:T(8,128)(2,1)S(1)}, bf16[1,256,256]{2,1,0:T(8,128)(2,1)S(1)}, u32[]{:S(2)}, u32[]{:S(2)}) %collective-permute-start.22) | collective-permute-done | bytes 131104 | tf_op jit(solution)/shard_map/ppermute | solution.py:348
  69.4 1.5 %shard_map.94 = (f32[2,256,768]{2,1,0:T(8,128)}, f32[2,256,256]{2,1,0:T(8,128)}) custom-call(s32[1]{0:T(128)} %bitcast.1.me_ref, bf16[1,256,256]{2,1,0:T(8,128)(2,1)S(1)} %shard_map.91.rest_0_, bf16[1,256,256]{2,1,0:T(8,128)(2,1)S(1)} %collective-permute-done.17.rest_1_, bf16[1,256,256]{2,1,0:T(8,128)(2,1)S(1)} %collective-permute-done.18.rest_2_, ...), custom_call_target="tpu_custom_call" | custom-call | flops 1000000000 | bytes 1048576 | tf_op jit(solution)/shard_map/pallas_call | solution.py:32
  (34 shorter events, 3.0 us)
Async XLA Ops:
  2.4 17.5 %collective-permute-start = (bf16[208,256]{1,0:T(8,128)(2,1)S(1)}, bf16[208,256]{1,0:T(8,128)(2,1)S(1)}, u32[]{:S(2)}, u32[]{:S(2)}) collective-permute-start(bf16[208,256]{1,0:T(8,128)(2,1)S(1)} %get-tuple-element.44), channel_id=1, source_target_pairs={{0,1},{1,0},{2,3},{3,2},{4,5},{5,4},{6,7},{7,6},{8,9},{9,8},{10,11... | collective-permute-start | bytes 319496 | tf_op jit(solution)/shard_map/ppermute | solution.py:348
  2.9 17.0 %collective-permute-start.1 = (bf16[208,256]{1,0:T(8,128)(2,1)S(1)}, bf16[208,256]{1,0:T(8,128)(2,1)S(1)}, u32[]{:S(2)}, u32[]{:S(2)}) collective-permute-start(bf16[208,256]{1,0:T(8,128)(2,1)S(1)} %get-tuple-element.45), channel_id=1, source_target_pairs={{0,2},{1,3},{2,0},{3,1},{4,6},{5,7},{6,4},{7,5},{8,10},{9,11},{10,... | collective-permute-start | bytes 319496 | tf_op jit(solution)/shard_map/ppermute | solution.py:348
  5.5 14.7 %collective-permute-start.2 = (bf16[208,256]{1,0:T(8,128)(2,1)S(1)}, bf16[208,256]{1,0:T(8,128)(2,1)S(1)}, u32[]{:S(2)}, u32[]{:S(2)}) collective-permute-start(bf16[208,256]{1,0:T(8,128)(2,1)S(1)} %get-tuple-element.46), channel_id=1, source_target_pairs={{0,3},{1,2},{2,1},{3,0},{4,7},{5,6},{6,5},{7,4},{8,11},{9,10},{10,... | collective-permute-start | bytes 319496 | tf_op jit(solution)/shard_map/ppermute | solution.py:348
  17.8 9.1 %collective-permute-start.3 = (bf16[192,256]{1,0:T(8,128)(2,1)S(1)}, bf16[192,256]{1,0:T(8,128)(2,1)S(1)}, u32[]{:S(2)}, u32[]{:S(2)}) collective-permute-start(bf16[192,256]{1,0:T(8,128)(2,1)S(1)} %get-tuple-element.58), channel_id=1, source_target_pairs={{0,1},{1,0},{2,3},{3,2},{4,5},{5,4},{6,7},{7,6},{8,9},{9,8},{10,11... | collective-permute-start | bytes 294920 | tf_op jit(solution)/shard_map/ppermute | solution.py:348
  18.0 8.9 %collective-permute-start.4 = (bf16[192,256]{1,0:T(8,128)(2,1)S(1)}, bf16[192,256]{1,0:T(8,128)(2,1)S(1)}, u32[]{:S(2)}, u32[]{:S(2)}) collective-permute-start(bf16[192,256]{1,0:T(8,128)(2,1)S(1)} %get-tuple-element.59), channel_id=1, source_target_pairs={{0,2},{1,3},{2,0},{3,1},{4,6},{5,7},{6,4},{7,5},{8,10},{9,11},{10,... | collective-permute-start | bytes 294920 | tf_op jit(solution)/shard_map/ppermute | solution.py:348
  19.9 7.0 %collective-permute-start.5 = (bf16[192,256]{1,0:T(8,128)(2,1)S(1)}, bf16[192,256]{1,0:T(8,128)(2,1)S(1)}, u32[]{:S(2)}, u32[]{:S(2)}) collective-permute-start(bf16[192,256]{1,0:T(8,128)(2,1)S(1)} %get-tuple-element.60), channel_id=1, source_target_pairs={{0,3},{1,2},{2,1},{3,0},{4,7},{5,6},{6,5},{7,4},{8,11},{9,10},{10,... | collective-permute-start | bytes 294920 | tf_op jit(solution)/shard_map/ppermute | solution.py:348
  19.9 14.3 %collective-permute-start.7 = (bf16[4,128,256]{2,1,0:T(8,128)(2,1)S(1)}, bf16[4,128,256]{2,1,0:T(8,128)(2,1)S(1)}, u32[]{:S(2)}, u32[]{:S(2)}) collective-permute-start(bf16[4,128,256]{2,1,0:T(8,128)(2,1)S(1)} %get-tuple-element.64), channel_id=1, source_target_pairs={{0,1},{1,0},{2,3},{3,2},{4,5},{5,4},{6,7},{7,6},{8,9},{9,8},{10,11... | collective-permute-start | bytes 786440 | tf_op jit(solution)/shard_map/ppermute | solution.py:348
  33.8 1.6 %collective-permute-start.6 = (bf16[4,128,256]{2,1,0:T(8,128)(2,1)S(1)}, bf16[4,128,256]{2,1,0:T(8,128)(2,1)S(1)}, u32[]{:S(2)}, u32[]{:S(2)}) collective-permute-start(bf16[4,128,256]{2,1,0:T(8,128)(2,1)S(1)} %get-tuple-element.62), channel_id=1, source_target_pairs={{0,1},{1,0},{2,3},{3,2},{4,5},{5,4},{6,7},{7,6},{8,9},{9,8},{10,11... | collective-permute-start | bytes 786440 | tf_op jit(solution)/shard_map/ppermute | solution.py:348
  35.5 6.4 %collective-permute-start.8 = (bf16[1,256,256]{2,1,0:T(8,128)(2,1)S(1)}, bf16[1,256,256]{2,1,0:T(8,128)(2,1)S(1)}, u32[]{:S(2)}, u32[]{:S(2)}) collective-permute-start(bf16[1,256,256]{2,1,0:T(8,128)(2,1)S(1)} %get-tuple-element.66), channel_id=1, source_target_pairs={{0,2},{1,3},{2,0},{3,1},{4,6},{5,7},{6,4},{7,5},{8,10},{9,11},{10,... | collective-permute-start | bytes 393224 | tf_op jit(solution)/shard_map/ppermute | solution.py:348
  37.5 7.4 %collective-permute-start.9 = (bf16[1,256,256]{2,1,0:T(8,128)(2,1)S(1)}, bf16[1,256,256]{2,1,0:T(8,128)(2,1)S(1)}, u32[]{:S(2)}, u32[]{:S(2)}) collective-permute-start(bf16[1,256,256]{2,1,0:T(8,128)(2,1)S(1)} %get-tuple-element.67), channel_id=1, source_target_pairs={{0,4},{1,5},{2,6},{3,7},{4,0},{5,1},{6,2},{7,3},{8,12},{9,13},{10,... | collective-permute-start | bytes 393224 | tf_op jit(solution)/shard_map/ppermute | solution.py:348
  39.0 7.2 %collective-permute-start.10 = (bf16[1,256,256]{2,1,0:T(8,128)(2,1)S(1)}, bf16[1,256,256]{2,1,0:T(8,128)(2,1)S(1)}, u32[]{:S(2)}, u32[]{:S(2)}) collective-permute-start(bf16[1,256,256]{2,1,0:T(8,128)(2,1)S(1)} %get-tuple-element.68), channel_id=1, source_target_pairs={{0,6},{1,7},{2,4},{3,5},{4,2},{5,3},{6,0},{7,1},{8,14},{9,15},{10,... | collective-permute-start | bytes 393224 | tf_op jit(solution)/shard_map/ppermute | solution.py:348
  39.9 10.1 %collective-permute-start.14 = (bf16[192,256]{1,0:T(8,128)(2,1)S(1)}, bf16[192,256]{1,0:T(8,128)(2,1)S(1)}, u32[]{:S(2)}, u32[]{:S(2)}) collective-permute-start(bf16[192,256]{1,0:T(8,128)(2,1)S(1)} %get-tuple-element.72), channel_id=1, source_target_pairs={{0,1},{1,0},{2,3},{3,2},{4,5},{5,4},{6,7},{7,6},{8,9},{9,8},{10,11... | collective-permute-start | bytes 294920 | tf_op jit(solution)/shard_map/ppermute | solution.py:348
  40.0 10.8 %collective-permute-start.15 = (bf16[192,256]{1,0:T(8,128)(2,1)S(1)}, bf16[192,256]{1,0:T(8,128)(2,1)S(1)}, u32[]{:S(2)}, u32[]{:S(2)}) collective-permute-start(bf16[192,256]{1,0:T(8,128)(2,1)S(1)} %get-tuple-element.73), channel_id=1, source_target_pairs={{0,2},{1,3},{2,0},{3,1},{4,6},{5,7},{6,4},{7,5},{8,10},{9,11},{10,... | collective-permute-start | bytes 294920 | tf_op jit(solution)/shard_map/ppermute | solution.py:348
  42.0 8.8 %collective-permute-start.16 = (bf16[192,256]{1,0:T(8,128)(2,1)S(1)}, bf16[192,256]{1,0:T(8,128)(2,1)S(1)}, u32[]{:S(2)}, u32[]{:S(2)}) collective-permute-start(bf16[192,256]{1,0:T(8,128)(2,1)S(1)} %get-tuple-element.74), channel_id=1, source_target_pairs={{0,3},{1,2},{2,1},{3,0},{4,7},{5,6},{6,5},{7,4},{8,11},{9,10},{10,... | collective-permute-start | bytes 294920 | tf_op jit(solution)/shard_map/ppermute | solution.py:348
  46.3 7.7 %collective-permute-start.13 = (bf16[1,256,256]{2,1,0:T(8,128)(2,1)S(1)}, bf16[1,256,256]{2,1,0:T(8,128)(2,1)S(1)}, u32[]{:S(2)}, u32[]{:S(2)}) collective-permute-start(bf16[1,256,256]{2,1,0:T(8,128)(2,1)S(1)} %shard_map.90.rest_0_), channel_id=1, source_target_pairs={{0,24},{1,25},{2,26},{3,27},{4,28},{5,29},{6,30},{7,31},{8,16},{9,... | collective-permute-start | bytes 393224 | tf_op jit(solution)/shard_map/ppermute | solution.py:348
  50.0 9.4 %collective-permute-start.12 = (bf16[1,256,256]{2,1,0:T(8,128)(2,1)S(1)}, bf16[1,256,256]{2,1,0:T(8,128)(2,1)S(1)}, u32[]{:S(2)}, u32[]{:S(2)}) collective-permute-start(bf16[1,256,256]{2,1,0:T(8,128)(2,1)S(1)} %shard_map.90.rest_0_), channel_id=1, source_target_pairs={{0,16},{1,17},{2,18},{3,19},{4,20},{5,21},{6,22},{7,23},{8,24},{9,... | collective-permute-start | bytes 393224 | tf_op jit(solution)/shard_map/ppermute | solution.py:348
  50.0 9.4 %collective-permute-start.11 = (bf16[1,256,256]{2,1,0:T(8,128)(2,1)S(1)}, bf16[1,256,256]{2,1,0:T(8,128)(2,1)S(1)}, u32[]{:S(2)}, u32[]{:S(2)}) collective-permute-start(bf16[1,256,256]{2,1,0:T(8,128)(2,1)S(1)} %shard_map.90.rest_0_), channel_id=1, source_target_pairs={{0,8},{1,9},{2,10},{3,11},{4,12},{5,13},{6,14},{7,15},{8,0},{9,1},... | collective-permute-start | bytes 393224 | tf_op jit(solution)/shard_map/ppermute | solution.py:348
  59.5 7.1 %collective-permute-start.19 = (bf16[1,256,256]{2,1,0:T(8,128)(2,1)S(1)}, bf16[1,256,256]{2,1,0:T(8,128)(2,1)S(1)}, u32[]{:S(2)}, u32[]{:S(2)}) collective-permute-start(bf16[1,256,256]{2,1,0:T(8,128)(2,1)S(1)} %shard_map.91.rest_0_), channel_id=1, source_target_pairs={{0,6},{1,7},{2,4},{3,5},{4,2},{5,3},{6,0},{7,1},{8,14},{9,15},{10,... | collective-permute-start | bytes 393224 | tf_op jit(solution)/shard_map/ppermute | solution.py:348
  61.2 6.6 %collective-permute-start.18 = (bf16[1,256,256]{2,1,0:T(8,128)(2,1)S(1)}, bf16[1,256,256]{2,1,0:T(8,128)(2,1)S(1)}, u32[]{:S(2)}, u32[]{:S(2)}) collective-permute-start(bf16[1,256,256]{2,1,0:T(8,128)(2,1)S(1)} %shard_map.91.rest_0_), channel_id=1, source_target_pairs={{0,4},{1,5},{2,6},{3,7},{4,0},{5,1},{6,2},{7,3},{8,12},{9,13},{10,... | collective-permute-start | bytes 393224 | tf_op jit(solution)/shard_map/ppermute | solution.py:348
  62.7 5.1 %collective-permute-start.17 = (bf16[1,256,256]{2,1,0:T(8,128)(2,1)S(1)}, bf16[1,256,256]{2,1,0:T(8,128)(2,1)S(1)}, u32[]{:S(2)}, u32[]{:S(2)}) collective-permute-start(bf16[1,256,256]{2,1,0:T(8,128)(2,1)S(1)} %shard_map.91.rest_0_), channel_id=1, source_target_pairs={{0,2},{1,3},{2,0},{3,1},{4,6},{5,7},{6,4},{7,5},{8,10},{9,11},{10,... | collective-permute-start | bytes 393224 | tf_op jit(solution)/shard_map/ppermute | solution.py:348
  63.1 5.2 %collective-permute-start.20 = (bf16[1,256,256]{2,1,0:T(8,128)(2,1)S(1)}, bf16[1,256,256]{2,1,0:T(8,128)(2,1)S(1)}, u32[]{:S(2)}, u32[]{:S(2)}) collective-permute-start(bf16[1,256,256]{2,1,0:T(8,128)(2,1)S(1)} %shard_map.91.rest_0_), channel_id=1, source_target_pairs={{0,1},{1,0},{2,3},{3,2},{4,5},{5,4},{6,7},{7,6},{8,9},{9,8},{10,11... | collective-permute-start | bytes 393224 | tf_op jit(solution)/shard_map/ppermute | solution.py:348
  66.6 1.7 %collective-permute-start.23 = (bf16[1,256,256]{2,1,0:T(8,128)(2,1)S(1)}, bf16[1,256,256]{2,1,0:T(8,128)(2,1)S(1)}, u32[]{:S(2)}, u32[]{:S(2)}) collective-permute-start(bf16[1,256,256]{2,1,0:T(8,128)(2,1)S(1)} %collective-permute-done.19.rest_3_), channel_id=1, source_target_pairs={{0,1},{1,0},{2,3},{3,2},{4,5},{5,4},{6,7},{7,6},{8,9},{9,8},{10,11... | collective-permute-start | bytes 393224 | tf_op jit(solution)/shard_map/ppermute | solution.py:348
  67.8 1.3 %collective-permute-start.22 = (bf16[1,256,256]{2,1,0:T(8,128)(2,1)S(1)}, bf16[1,256,256]{2,1,0:T(8,128)(2,1)S(1)}, u32[]{:S(2)}, u32[]{:S(2)}) collective-permute-start(bf16[1,256,256]{2,1,0:T(8,128)(2,1)S(1)} %collective-permute-done.18.rest_2_), channel_id=1, source_target_pairs={{0,1},{1,0},{2,3},{3,2},{4,5},{5,4},{6,7},{7,6},{8,9},{9,8},{10,11... | collective-permute-start | bytes 393224 | tf_op jit(solution)/shard_map/ppermute | solution.py:348
  67.8 1.5 %collective-permute-start.21 = (bf16[1,256,256]{2,1,0:T(8,128)(2,1)S(1)}, bf16[1,256,256]{2,1,0:T(8,128)(2,1)S(1)}, u32[]{:S(2)}, u32[]{:S(2)}) collective-permute-start(bf16[1,256,256]{2,1,0:T(8,128)(2,1)S(1)} %collective-permute-done.17.rest_1_), channel_id=1, source_target_pairs={{0,1},{1,0},{2,3},{3,2},{4,5},{5,4},{6,7},{7,6},{8,9},{9,8},{10,11... | collective-permute-start | bytes 393224 | tf_op jit(solution)/shard_map/ppermute | solution.py:348

commit v7 on v6

--- a/solution.py
+++ b/solution.py
@@ -371,7 +371,7 @@
     low = rank % blocks
     place = ((low & 1) << 2 | (low >> 1)).reshape(1)
     bits = devices.bit_length() - 1
-    whole_stages = [tuple(range(b, min(b + 2, bits))) for b in range(3, bits, 2)]
+    whole_stages = [(b,) for b in reversed(range(3, bits))]
 
     size_rows = shape((n, channels), bf16)
     size_send = shape((cap, channels), bf16)

time: 71.2 us -> 70.2 us (0.986)
  starting transfers between devices: 20.1 us -> 18.7 us
    ppermute x24 -> x23, starting transfers between devices: 20.1 us -> 18.7 us  [swap(): return lax.ppermute(x, AXES, [(d, d ^ mask) for d in range(devices)])]
    ppermute x24 -> x23, waiting for transfers between devices: 18.7 us -> 19 us  [swap(): return lax.ppermute(x, AXES, [(d, d ^ mask) for d in range(devices)])]
    pallas_call x10 -> x11, Pallas kernels: 31.4 us -> 31.4 us  [call(): pl.pallas_call(body, out_shape=tuple(out_shape), in_specs=[pl.BlockSpec(m...]
  transfers between devices with their start and end apart: 24 -> 23, of which waited for: 9 -> 12; matrix products, arithmetic and copies ran while one was open for 0% -> 0% of each run, Pallas kernels for 39% -> 40%
where the time goes in v7:
time: 70.2 us; the launch traced here: 70 us
  Pallas kernels  31.4 us (45%)
  waiting for transfers between devices  19 us (27%)
  starting transfers between devices  18.7 us (27%)
  between operations  0.92 us (1%)
    pallas_call x11, Pallas kernels, call(): pl.pallas_call(body, out_shape=tuple(out_shape), in_specs=[pl.BlockSpec(m...  31.4 us
    ppermute x23, waiting for transfers between devices, swap(): return lax.ppermute(x, AXES, [(d, d ^ mask) for d in range(devices)])  19 us
    ppermute x23, starting transfers between devices, swap(): return lax.ppermute(x, AXES, [(d, d ^ mask) for d in range(devices)])  18.7 us
  transfers between devices with their start and end apart: 23, of which 12 were waited for; matrix products, arithmetic and copies ran while one was open for 0% of the time, Pallas kernels for 40%

profile of v7, /device:TPU:0, one launch (start us, length us, event | category | flops | bytes accessed | tf_op | source)
XLA Modules:
  0.0 70.0 jit_solution(11793420182398350481)
XLA Ops:
  0.6 1.8 %shard_map.85 = (s32[1,512]{1,0:T(1,128)S(1)}, bf16[208,256]{1,0:T(8,128)(2,1)S(1)}, bf16[208,256]{1,0:T(8,128)(2,1)S(1)}, bf16[208,256]{1,0:T(8,128)(2,1)S(1)},...) custom-call(s32[1]{0:T(128)} %bitcast.me_ref, ...), custom_call_target="tpu_custom_call" | custom-call | flops 2000000000 | bytes 1048576 | tf_op jit(solution)/shard_map/pallas_call | solution.py:32
  2.9 2.6 %collective-permute-start.1 = (bf16[208,256]{1,0:T(8,128)(2,1)S(1)}, bf16[208,256]{1,0:T(8,128)(2,1)S(1)}, u32[]{:S(2)}, u32[]{:S(2)}) collective-permute-start(bf16[208,256]{1,0:T(8,128)(2,1)S(1)} %get-tuple-element.45), channel_id=1, source_target_pairs={{0,2},{1,3},{2,0},{3,1},{4,6},{5,7},{6,4},{7,5},{8,10},{9,11},{10,... | collective-permute-start | bytes 319496 | tf_op jit(solution)/shard_map/ppermute | solution.py:348
  5.6 12.2 %shard_map.87 = (bf16[512,256]{1,0:T(8,128)(2,1)S(1)}, bf16[4,128,256]{2,1,0:T(8,128)(2,1)S(1)}, bf16[4,128,256]{2,1,0:T(8,128)(2,1)S(1)}, bf16[192,256]{1,0:T(8...) custom-call(s32[1]{0:T(128)} %bitcast.1.me_ref, ...), custom_call_target="tpu_custom_call" | custom-call | flops 16000000000 | bytes 1048576 | tf_op jit(solution)/shard_map/pallas_call | solution.py:32
  18.0 1.9 %collective-permute-start.4 = (bf16[192,256]{1,0:T(8,128)(2,1)S(1)}, bf16[192,256]{1,0:T(8,128)(2,1)S(1)}, u32[]{:S(2)}, u32[]{:S(2)}) collective-permute-start(bf16[192,256]{1,0:T(8,128)(2,1)S(1)} %get-tuple-element.59), channel_id=1, source_target_pairs={{0,2},{1,3},{2,0},{3,1},{4,6},{5,7},{6,4},{7,5},{8,10},{9,11},{10,... | collective-permute-start | bytes 294920 | tf_op jit(solution)/shard_map/ppermute | solution.py:348
  20.2 6.7 %shard_map.86 = (bf16[512,768]{1,0:T(8,128)(2,1)S(1)}, bf16[256,512]{1,0:T(8,128)(2,1)S(1)}, bf16[768,512]{1,0:T(8,128)(2,1)S(1)}, bf16[16,512,512]{2,1,0:T(8,12...) custom-call(s32[1]{0:T(128)} %bitcast.me_ref, ...), custom_call_target="tpu_custom_call" | custom-call | flops 7000000000 | bytes 1048576 | tf_op jit(solution)/shard_map/pallas_call | solution.py:32
  26.9 6.9 %shard_map.88 = (bf16[768,512]{1,0:T(8,128)(2,1)S(1)}, bf16[4,128,256]{2,1,0:T(8,128)(2,1)S(1)}, bf16[4,128,256]{2,1,0:T(8,128)(2,1)S(1)}) custom-call(s32[1]{0:T(128)} %bitcast.1.me_ref, bf16[2,256,256]{2,1,0:T(8,128)(2,1)S(1)} %get-tuple-element.41.out_ref, bf16[512,768]{1,0:T(8,128)(2,1)S(1)} %get-tuple-element.47.place_ref, ...), custom_call_target="tpu_custom_call" | custom-call | flops 8999999488 | bytes 1048576 | tf_op jit(solution)/shard_map/pallas_call | solution.py:32
  34.2 1.2 %collective-permute-done.6.rest_1_ = bf16[4,128,256]{2,1,0:T(8,128)(2,1)S(1)} collective-permute-done((bf16[4,128,256]{2,1,0:T(8,128)(2,1)S(1)}, bf16[4,128,256]{2,1,0:T(8,128)(2,1)S(1)}, u32[]{:S(2)}, u32[]{:S(2)}) %collective-permute-start.6) | collective-permute-done | bytes 262176 | tf_op jit(solution)/shard_map/ppermute | solution.py:348
  35.5 2.0 %collective-permute-start.8 = (bf16[1,256,256]{2,1,0:T(8,128)(2,1)S(1)}, bf16[1,256,256]{2,1,0:T(8,128)(2,1)S(1)}, u32[]{:S(2)}, u32[]{:S(2)}) collective-permute-start(bf16[1,256,256]{2,1,0:T(8,128)(2,1)S(1)} %get-tuple-element.66), channel_id=1, source_target_pairs={{0,2},{1,3},{2,0},{3,1},{4,6},{5,7},{6,4},{7,5},{8,10},{9,11},{10,... | collective-permute-start | bytes 393224 | tf_op jit(solution)/shard_map/ppermute | solution.py:348
  37.5 1.5 %collective-permute-start.9 = (bf16[1,256,256]{2,1,0:T(8,128)(2,1)S(1)}, bf16[1,256,256]{2,1,0:T(8,128)(2,1)S(1)}, u32[]{:S(2)}, u32[]{:S(2)}) collective-permute-start(bf16[1,256,256]{2,1,0:T(8,128)(2,1)S(1)} %get-tuple-element.67), channel_id=1, source_target_pairs={{0,4},{1,5},{2,6},{3,7},{4,0},{5,1},{6,2},{7,3},{8,12},{9,13},{10,... | collective-permute-start | bytes 393224 | tf_op jit(solution)/shard_map/ppermute | solution.py:348
  39.1 2.4 %collective-permute-done.8.rest_1_ = bf16[1,256,256]{2,1,0:T(8,128)(2,1)S(1)} collective-permute-done((bf16[1,256,256]{2,1,0:T(8,128)(2,1)S(1)}, bf16[1,256,256]{2,1,0:T(8,128)(2,1)S(1)}, u32[]{:S(2)}, u32[]{:S(2)}) %collective-permute-start.8) | collective-permute-done | bytes 131104 | tf_op jit(solution)/shard_map/ppermute | solution.py:348
  41.5 4.1 %collective-permute-done.9.rest_2_ = bf16[1,256,256]{2,1,0:T(8,128)(2,1)S(1)} collective-permute-done((bf16[1,256,256]{2,1,0:T(8,128)(2,1)S(1)}, bf16[1,256,256]{2,1,0:T(8,128)(2,1)S(1)}, u32[]{:S(2)}, u32[]{:S(2)}) %collective-permute-start.9) | collective-permute-done | bytes 131104 | tf_op jit(solution)/shard_map/ppermute | solution.py:348
  45.7 2.7 %collective-permute-start.11 = (bf16[1,256,256]{2,1,0:T(8,128)(2,1)S(1)}, bf16[1,256,256]{2,1,0:T(8,128)(2,1)S(1)}, u32[]{:S(2)}, u32[]{:S(2)}) collective-permute-start(bf16[1,256,256]{2,1,0:T(8,128)(2,1)S(1)} %shard_map.90.rest_0_), channel_id=1, source_target_pairs={{0,16},{1,17},{2,18},{3,19},{4,20},{5,21},{6,22},{7,23},{8,24},{9,... | collective-permute-start | bytes 393224 | tf_op jit(solution)/shard_map/ppermute | solution.py:348
  48.3 0.8 %shard_map.93 = (bf16[192,256]{1,0:T(8,128)(2,1)S(1)}, bf16[192,256]{1,0:T(8,128)(2,1)S(1)}, bf16[192,256]{1,0:T(8,128)(2,1)S(1)}, bf16[192,256]{1,0:T(8,128)(2,1)S(1)}) custom-call(s32[1]{0:T(128)} %bitcast.me_ref, bf16[2,256,768]{2,1,0:T(8,128)(2,1)S(1)} %get-tuple-element.42.qkv_ref, bf16[768,512]{1,0:T(8,128)(2,1)S(1)} %get-tuple-element.70.delta, ...), custom_call_target="tpu_custom_call" | custom-call | flops 2000000000 | bytes 1048576 | tf_op jit(solution)/shard_map/pallas_call | solution.py:32
  49.2 1.3 %collective-permute-start.14 = (bf16[192,256]{1,0:T(8,128)(2,1)S(1)}, bf16[192,256]{1,0:T(8,128)(2,1)S(1)}, u32[]{:S(2)}, u32[]{:S(2)}) collective-permute-start(bf16[192,256]{1,0:T(8,128)(2,1)S(1)} %get-tuple-element.73), channel_id=1, source_target_pairs={{0,2},{1,3},{2,0},{3,1},{4,6},{5,7},{6,4},{7,5},{8,10},{9,11},{10,... | collective-permute-start | bytes 294920 | tf_op jit(solution)/shard_map/ppermute | solution.py:348
  51.1 2.6 %collective-permute-done.11.rest_1_ = bf16[1,256,256]{2,1,0:T(8,128)(2,1)S(1)} collective-permute-done((bf16[1,256,256]{2,1,0:T(8,128)(2,1)S(1)}, bf16[1,256,256]{2,1,0:T(8,128)(2,1)S(1)}, u32[]{:S(2)}, u32[]{:S(2)}) %collective-permute-start.11) | collective-permute-done | bytes 131104 | tf_op jit(solution)/shard_map/ppermute | solution.py:348
  54.9 1.2 %collective-permute-done.15.rest_3_ = bf16[192,256]{1,0:T(8,128)(2,1)S(1)} collective-permute-done((bf16[192,256]{1,0:T(8,128)(2,1)S(1)}, bf16[192,256]{1,0:T(8,128)(2,1)S(1)}, u32[]{:S(2)}, u32[]{:S(2)}) %collective-permute-start.15) | collective-permute-done | bytes 98336 | tf_op jit(solution)/shard_map/ppermute | solution.py:348
  56.1 1.2 %shard_map.94 = bf16[512,256]{1,0:T(8,128)(2,1)} custom-call(s32[1]{0:T(128)} %bitcast.me_ref, s32[1,512]{1,0:T(1,128)S(1)} %get-tuple-element.56.slots_ref, bf16[512,256]{1,0:T(8,128)(2,1)S(1)} %get-tuple-element.69.mid_ref, bf16[192,256]{1,0:T(8,128)(2,1)S(1)} %get-tuple-element.71.rest_0_, bf16[192,256]{1,0:T(8,128)(2,1)S(1)} %collective-permute-done.13.rest_1_, ...), custom_call_target="tpu_custom_call" | custom-call | flops 1000000000 | bytes 1048576 | tf_op jit(solution)/shard_map/pallas_call | solution.py:32
  57.3 1.5 %collective-permute-done.12.rest_1_ = bf16[1,256,256]{2,1,0:T(8,128)(2,1)S(1)} collective-permute-done((bf16[1,256,256]{2,1,0:T(8,128)(2,1)S(1)}, bf16[1,256,256]{2,1,0:T(8,128)(2,1)S(1)}, u32[]{:S(2)}, u32[]{:S(2)}) %collective-permute-start.12) | collective-permute-done | bytes 131104 | tf_op jit(solution)/shard_map/ppermute | solution.py:348
  58.8 1.7 %collective-permute-start.18 = (bf16[1,256,256]{2,1,0:T(8,128)(2,1)S(1)}, bf16[1,256,256]{2,1,0:T(8,128)(2,1)S(1)}, u32[]{:S(2)}, u32[]{:S(2)}) collective-permute-start(bf16[1,256,256]{2,1,0:T(8,128)(2,1)S(1)} %shard_map.92.rest_0_), channel_id=1, source_target_pairs={{0,6},{1,7},{2,4},{3,5},{4,2},{5,3},{6,0},{7,1},{8,14},{9,15},{10,... | collective-permute-start | bytes 393224 | tf_op jit(solution)/shard_map/ppermute | solution.py:348
  60.5 1.5 %collective-permute-start.17 = (bf16[1,256,256]{2,1,0:T(8,128)(2,1)S(1)}, bf16[1,256,256]{2,1,0:T(8,128)(2,1)S(1)}, u32[]{:S(2)}, u32[]{:S(2)}) collective-permute-start(bf16[1,256,256]{2,1,0:T(8,128)(2,1)S(1)} %shard_map.92.rest_0_), channel_id=1, source_target_pairs={{0,4},{1,5},{2,6},{3,7},{4,0},{5,1},{6,2},{7,3},{8,12},{9,13},{10,... | collective-permute-start | bytes 393224 | tf_op jit(solution)/shard_map/ppermute | solution.py:348
  62.3 3.2 %collective-permute-done.18.rest_3_ = bf16[1,256,256]{2,1,0:T(8,128)(2,1)S(1)} collective-permute-done((bf16[1,256,256]{2,1,0:T(8,128)(2,1)S(1)}, bf16[1,256,256]{2,1,0:T(8,128)(2,1)S(1)}, u32[]{:S(2)}, u32[]{:S(2)}) %collective-permute-start.18) | collective-permute-done | bytes 131104 | tf_op jit(solution)/shard_map/ppermute | solution.py:348
  65.5 1.2 %collective-permute-done.17.rest_2_ = bf16[1,256,256]{2,1,0:T(8,128)(2,1)S(1)} collective-permute-done((bf16[1,256,256]{2,1,0:T(8,128)(2,1)S(1)}, bf16[1,256,256]{2,1,0:T(8,128)(2,1)S(1)}, u32[]{:S(2)}, u32[]{:S(2)}) %collective-permute-start.17) | collective-permute-done | bytes 131104 | tf_op jit(solution)/shard_map/ppermute | solution.py:348
  67.3 0.8 %collective-permute-done.21.rest_6_ = bf16[1,256,256]{2,1,0:T(8,128)(2,1)S(1)} collective-permute-done((bf16[1,256,256]{2,1,0:T(8,128)(2,1)S(1)}, bf16[1,256,256]{2,1,0:T(8,128)(2,1)S(1)}, u32[]{:S(2)}, u32[]{:S(2)}) %collective-permute-start.21) | collective-permute-done | bytes 131104 | tf_op jit(solution)/shard_map/ppermute | solution.py:348
  68.3 1.5 %shard_map.95 = (f32[2,256,768]{2,1,0:T(8,128)}, f32[2,256,256]{2,1,0:T(8,128)}) custom-call(s32[1]{0:T(128)} %bitcast.1.me_ref, bf16[1,256,256]{2,1,0:T(8,128)(2,1)S(1)} %shard_map.92.rest_0_, bf16[1,256,256]{2,1,0:T(8,128)(2,1)S(1)} %collective-permute-done.16.rest_1_, bf16[1,256,256]{2,1,0:T(8,128)(2,1)S(1)} %collective-permute-done.17.rest_2_, ...), custom_call_target="tpu_custom_call" | custom-call | flops 1000000000 | bytes 1048576 | tf_op jit(solution)/shard_map/pallas_call | solution.py:32
  (33 shorter events, 4.6 us)
Async XLA Ops:
  2.4 17.5 %collective-permute-start = (bf16[208,256]{1,0:T(8,128)(2,1)S(1)}, bf16[208,256]{1,0:T(8,128)(2,1)S(1)}, u32[]{:S(2)}, u32[]{:S(2)}) collective-permute-start(bf16[208,256]{1,0:T(8,128)(2,1)S(1)} %get-tuple-element.44), channel_id=1, source_target_pairs={{0,1},{1,0},{2,3},{3,2},{4,5},{5,4},{6,7},{7,6},{8,9},{9,8},{10,11... | collective-permute-start | bytes 319496 | tf_op jit(solution)/shard_map/ppermute | solution.py:348
  2.9 17.0 %collective-permute-start.1 = (bf16[208,256]{1,0:T(8,128)(2,1)S(1)}, bf16[208,256]{1,0:T(8,128)(2,1)S(1)}, u32[]{:S(2)}, u32[]{:S(2)}) collective-permute-start(bf16[208,256]{1,0:T(8,128)(2,1)S(1)} %get-tuple-element.45), channel_id=1, source_target_pairs={{0,2},{1,3},{2,0},{3,1},{4,6},{5,7},{6,4},{7,5},{8,10},{9,11},{10,... | collective-permute-start | bytes 319496 | tf_op jit(solution)/shard_map/ppermute | solution.py:348
  5.5 14.7 %collective-permute-start.2 = (bf16[208,256]{1,0:T(8,128)(2,1)S(1)}, bf16[208,256]{1,0:T(8,128)(2,1)S(1)}, u32[]{:S(2)}, u32[]{:S(2)}) collective-permute-start(bf16[208,256]{1,0:T(8,128)(2,1)S(1)} %get-tuple-element.46), channel_id=1, source_target_pairs={{0,3},{1,2},{2,1},{3,0},{4,7},{5,6},{6,5},{7,4},{8,11},{9,10},{10,... | collective-permute-start | bytes 319496 | tf_op jit(solution)/shard_map/ppermute | solution.py:348
  17.8 9.1 %collective-permute-start.3 = (bf16[192,256]{1,0:T(8,128)(2,1)S(1)}, bf16[192,256]{1,0:T(8,128)(2,1)S(1)}, u32[]{:S(2)}, u32[]{:S(2)}) collective-permute-start(bf16[192,256]{1,0:T(8,128)(2,1)S(1)} %get-tuple-element.58), channel_id=1, source_target_pairs={{0,1},{1,0},{2,3},{3,2},{4,5},{5,4},{6,7},{7,6},{8,9},{9,8},{10,11... | collective-permute-start | bytes 294920 | tf_op jit(solution)/shard_map/ppermute | solution.py:348
  18.0 8.9 %collective-permute-start.4 = (bf16[192,256]{1,0:T(8,128)(2,1)S(1)}, bf16[192,256]{1,0:T(8,128)(2,1)S(1)}, u32[]{:S(2)}, u32[]{:S(2)}) collective-permute-start(bf16[192,256]{1,0:T(8,128)(2,1)S(1)} %get-tuple-element.59), channel_id=1, source_target_pairs={{0,2},{1,3},{2,0},{3,1},{4,6},{5,7},{6,4},{7,5},{8,10},{9,11},{10,... | collective-permute-start | bytes 294920 | tf_op jit(solution)/shard_map/ppermute | solution.py:348
  19.9 7.0 %collective-permute-start.5 = (bf16[192,256]{1,0:T(8,128)(2,1)S(1)}, bf16[192,256]{1,0:T(8,128)(2,1)S(1)}, u32[]{:S(2)}, u32[]{:S(2)}) collective-permute-start(bf16[192,256]{1,0:T(8,128)(2,1)S(1)} %get-tuple-element.60), channel_id=1, source_target_pairs={{0,3},{1,2},{2,1},{3,0},{4,7},{5,6},{6,5},{7,4},{8,11},{9,10},{10,... | collective-permute-start | bytes 294920 | tf_op jit(solution)/shard_map/ppermute | solution.py:348
  19.9 14.3 %collective-permute-start.7 = (bf16[4,128,256]{2,1,0:T(8,128)(2,1)S(1)}, bf16[4,128,256]{2,1,0:T(8,128)(2,1)S(1)}, u32[]{:S(2)}, u32[]{:S(2)}) collective-permute-start(bf16[4,128,256]{2,1,0:T(8,128)(2,1)S(1)} %get-tuple-element.64), channel_id=1, source_target_pairs={{0,1},{1,0},{2,3},{3,2},{4,5},{5,4},{6,7},{7,6},{8,9},{9,8},{10,11... | collective-permute-start | bytes 786440 | tf_op jit(solution)/shard_map/ppermute | solution.py:348
  33.8 1.6 %collective-permute-start.6 = (bf16[4,128,256]{2,1,0:T(8,128)(2,1)S(1)}, bf16[4,128,256]{2,1,0:T(8,128)(2,1)S(1)}, u32[]{:S(2)}, u32[]{:S(2)}) collective-permute-start(bf16[4,128,256]{2,1,0:T(8,128)(2,1)S(1)} %get-tuple-element.62), channel_id=1, source_target_pairs={{0,1},{1,0},{2,3},{3,2},{4,5},{5,4},{6,7},{7,6},{8,9},{9,8},{10,11... | collective-permute-start | bytes 786440 | tf_op jit(solution)/shard_map/ppermute | solution.py:348
  35.5 5.9 %collective-permute-start.8 = (bf16[1,256,256]{2,1,0:T(8,128)(2,1)S(1)}, bf16[1,256,256]{2,1,0:T(8,128)(2,1)S(1)}, u32[]{:S(2)}, u32[]{:S(2)}) collective-permute-start(bf16[1,256,256]{2,1,0:T(8,128)(2,1)S(1)} %get-tuple-element.66), channel_id=1, source_target_pairs={{0,2},{1,3},{2,0},{3,1},{4,6},{5,7},{6,4},{7,5},{8,10},{9,11},{10,... | collective-permute-start | bytes 393224 | tf_op jit(solution)/shard_map/ppermute | solution.py:348
  37.5 8.1 %collective-permute-start.9 = (bf16[1,256,256]{2,1,0:T(8,128)(2,1)S(1)}, bf16[1,256,256]{2,1,0:T(8,128)(2,1)S(1)}, u32[]{:S(2)}, u32[]{:S(2)}) collective-permute-start(bf16[1,256,256]{2,1,0:T(8,128)(2,1)S(1)} %get-tuple-element.67), channel_id=1, source_target_pairs={{0,4},{1,5},{2,6},{3,7},{4,0},{5,1},{6,2},{7,3},{8,12},{9,13},{10,... | collective-permute-start | bytes 393224 | tf_op jit(solution)/shard_map/ppermute | solution.py:348
  39.0 6.5 %collective-permute-start.10 = (bf16[1,256,256]{2,1,0:T(8,128)(2,1)S(1)}, bf16[1,256,256]{2,1,0:T(8,128)(2,1)S(1)}, u32[]{:S(2)}, u32[]{:S(2)}) collective-permute-start(bf16[1,256,256]{2,1,0:T(8,128)(2,1)S(1)} %get-tuple-element.68), channel_id=1, source_target_pairs={{0,6},{1,7},{2,4},{3,5},{4,2},{5,3},{6,0},{7,1},{8,14},{9,15},{10,... | collective-permute-start | bytes 393224 | tf_op jit(solution)/shard_map/ppermute | solution.py:348
  45.7 8.0 %collective-permute-start.11 = (bf16[1,256,256]{2,1,0:T(8,128)(2,1)S(1)}, bf16[1,256,256]{2,1,0:T(8,128)(2,1)S(1)}, u32[]{:S(2)}, u32[]{:S(2)}) collective-permute-start(bf16[1,256,256]{2,1,0:T(8,128)(2,1)S(1)} %shard_map.90.rest_0_), channel_id=1, source_target_pairs={{0,16},{1,17},{2,18},{3,19},{4,20},{5,21},{6,22},{7,23},{8,24},{9,... | collective-permute-start | bytes 393224 | tf_op jit(solution)/shard_map/ppermute | solution.py:348
  49.1 5.4 %collective-permute-start.13 = (bf16[192,256]{1,0:T(8,128)(2,1)S(1)}, bf16[192,256]{1,0:T(8,128)(2,1)S(1)}, u32[]{:S(2)}, u32[]{:S(2)}) collective-permute-start(bf16[192,256]{1,0:T(8,128)(2,1)S(1)} %get-tuple-element.72), channel_id=1, source_target_pairs={{0,1},{1,0},{2,3},{3,2},{4,5},{5,4},{6,7},{7,6},{8,9},{9,8},{10,11... | collective-permute-start | bytes 294920 | tf_op jit(solution)/shard_map/ppermute | solution.py:348
  49.2 5.7 %collective-permute-start.14 = (bf16[192,256]{1,0:T(8,128)(2,1)S(1)}, bf16[192,256]{1,0:T(8,128)(2,1)S(1)}, u32[]{:S(2)}, u32[]{:S(2)}) collective-permute-start(bf16[192,256]{1,0:T(8,128)(2,1)S(1)} %get-tuple-element.73), channel_id=1, source_target_pairs={{0,2},{1,3},{2,0},{3,1},{4,6},{5,7},{6,4},{7,5},{8,10},{9,11},{10,... | collective-permute-start | bytes 294920 | tf_op jit(solution)/shard_map/ppermute | solution.py:348
  50.5 5.6 %collective-permute-start.15 = (bf16[192,256]{1,0:T(8,128)(2,1)S(1)}, bf16[192,256]{1,0:T(8,128)(2,1)S(1)}, u32[]{:S(2)}, u32[]{:S(2)}) collective-permute-start(bf16[192,256]{1,0:T(8,128)(2,1)S(1)} %get-tuple-element.74), channel_id=1, source_target_pairs={{0,3},{1,2},{2,1},{3,0},{4,7},{5,6},{6,5},{7,4},{8,11},{9,10},{10,... | collective-permute-start | bytes 294920 | tf_op jit(solution)/shard_map/ppermute | solution.py:348
  53.7 5.0 %collective-permute-start.12 = (bf16[1,256,256]{2,1,0:T(8,128)(2,1)S(1)}, bf16[1,256,256]{2,1,0:T(8,128)(2,1)S(1)}, u32[]{:S(2)}, u32[]{:S(2)}) collective-permute-start(bf16[1,256,256]{2,1,0:T(8,128)(2,1)S(1)} %shard_map.91.rest_0_), channel_id=1, source_target_pairs={{0,8},{1,9},{2,10},{3,11},{4,12},{5,13},{6,14},{7,15},{8,0},{9,1},... | collective-permute-start | bytes 393224 | tf_op jit(solution)/shard_map/ppermute | solution.py:348
  58.8 6.7 %collective-permute-start.18 = (bf16[1,256,256]{2,1,0:T(8,128)(2,1)S(1)}, bf16[1,256,256]{2,1,0:T(8,128)(2,1)S(1)}, u32[]{:S(2)}, u32[]{:S(2)}) collective-permute-start(bf16[1,256,256]{2,1,0:T(8,128)(2,1)S(1)} %shard_map.92.rest_0_), channel_id=1, source_target_pairs={{0,6},{1,7},{2,4},{3,5},{4,2},{5,3},{6,0},{7,1},{8,14},{9,15},{10,... | collective-permute-start | bytes 393224 | tf_op jit(solution)/shard_map/ppermute | solution.py:348
  60.5 6.3 %collective-permute-start.17 = (bf16[1,256,256]{2,1,0:T(8,128)(2,1)S(1)}, bf16[1,256,256]{2,1,0:T(8,128)(2,1)S(1)}, u32[]{:S(2)}, u32[]{:S(2)}) collective-permute-start(bf16[1,256,256]{2,1,0:T(8,128)(2,1)S(1)} %shard_map.92.rest_0_), channel_id=1, source_target_pairs={{0,4},{1,5},{2,6},{3,7},{4,0},{5,1},{6,2},{7,3},{8,12},{9,13},{10,... | collective-permute-start | bytes 393224 | tf_op jit(solution)/shard_map/ppermute | solution.py:348
  62.0 5.0 %collective-permute-start.16 = (bf16[1,256,256]{2,1,0:T(8,128)(2,1)S(1)}, bf16[1,256,256]{2,1,0:T(8,128)(2,1)S(1)}, u32[]{:S(2)}, u32[]{:S(2)}) collective-permute-start(bf16[1,256,256]{2,1,0:T(8,128)(2,1)S(1)} %shard_map.92.rest_0_), channel_id=1, source_target_pairs={{0,2},{1,3},{2,0},{3,1},{4,6},{5,7},{6,4},{7,5},{8,10},{9,11},{10,... | collective-permute-start | bytes 393224 | tf_op jit(solution)/shard_map/ppermute | solution.py:348
  62.3 5.0 %collective-permute-start.19 = (bf16[1,256,256]{2,1,0:T(8,128)(2,1)S(1)}, bf16[1,256,256]{2,1,0:T(8,128)(2,1)S(1)}, u32[]{:S(2)}, u32[]{:S(2)}) collective-permute-start(bf16[1,256,256]{2,1,0:T(8,128)(2,1)S(1)} %shard_map.92.rest_0_), channel_id=1, source_target_pairs={{0,1},{1,0},{2,3},{3,2},{4,5},{5,4},{6,7},{7,6},{8,9},{9,8},{10,11... | collective-permute-start | bytes 393224 | tf_op jit(solution)/shard_map/ppermute | solution.py:348
  65.5 1.8 %collective-permute-start.22 = (bf16[1,256,256]{2,1,0:T(8,128)(2,1)S(1)}, bf16[1,256,256]{2,1,0:T(8,128)(2,1)S(1)}, u32[]{:S(2)}, u32[]{:S(2)}) collective-permute-start(bf16[1,256,256]{2,1,0:T(8,128)(2,1)S(1)} %collective-permute-done.18.rest_3_), channel_id=1, source_target_pairs={{0,1},{1,0},{2,3},{3,2},{4,5},{5,4},{6,7},{7,6},{8,9},{9,8},{10,11... | collective-permute-start | bytes 393224 | tf_op jit(solution)/shard_map/ppermute | solution.py:348
  66.8 1.3 %collective-permute-start.21 = (bf16[1,256,256]{2,1,0:T(8,128)(2,1)S(1)}, bf16[1,256,256]{2,1,0:T(8,128)(2,1)S(1)}, u32[]{:S(2)}, u32[]{:S(2)}) collective-permute-start(bf16[1,256,256]{2,1,0:T(8,128)(2,1)S(1)} %collective-permute-done.17.rest_2_), channel_id=1, source_target_pairs={{0,1},{1,0},{2,3},{3,2},{4,5},{5,4},{6,7},{7,6},{8,9},{9,8},{10,11... | collective-permute-start | bytes 393224 | tf_op jit(solution)/shard_map/ppermute | solution.py:348
  67.0 1.3 %collective-permute-start.20 = (bf16[1,256,256]{2,1,0:T(8,128)(2,1)S(1)}, bf16[1,256,256]{2,1,0:T(8,128)(2,1)S(1)}, u32[]{:S(2)}, u32[]{:S(2)}) collective-permute-start(bf16[1,256,256]{2,1,0:T(8,128)(2,1)S(1)} %collective-permute-done.16.rest_1_), channel_id=1, source_target_pairs={{0,1},{1,0},{2,3},{3,2},{4,5},{5,4},{6,7},{7,6},{8,9},{9,8},{10,11... | collective-permute-start | bytes 393224 | tf_op jit(solution)/shard_map/ppermute | solution.py:348

commit v8 on v7

--- a/solution.py
+++ b/solution.py
@@ -455,10 +455,10 @@
     for stage in whole_stages:
         parts = [total] + [swap(total, m, devices) for m in stage_masks(stage)[1:]]
         (total,) = add_parts(me, [parts])
+    total, *backs = lax.optimization_barrier((total, *backs))
     (input_grad,) = call(
         partial(join_kernel, group, cap), [size_rows], [me, slots, mid, *backs]
     )
-    total, input_grad = lax.optimization_barrier((total, input_grad))
     parts = [total] + [swap(total, m, devices) for m in masks[1:]]
     parts = parts + [swap(x, 1, devices) for x in parts]
     qkv_grad, out_w_grad = call(

time: 70.2 us -> 75.2 us (1.071)
  waiting for transfers between devices: 19 us -> 24.1 us
    ppermute x23, waiting for transfers between devices: 19 us -> 24.1 us  [swap(): return lax.ppermute(x, AXES, [(d, d ^ mask) for d in range(devices)])]
  transfers between devices with their start and end apart: 23 -> 23, of which waited for: 12 -> 10; matrix products, arithmetic and copies ran while one was open for 0% -> 0% of each run, Pallas kernels for 40% -> 37%
where the time goes in v8:
time: 75.2 us; the launch traced here: 75.1 us
  Pallas kernels  31.4 us (42%)
  waiting for transfers between devices  24.1 us (32%)
  starting transfers between devices  18.7 us (25%)
  between operations  0.94 us (1%)
    pallas_call x11, Pallas kernels, call(): pl.pallas_call(body, out_shape=tuple(out_shape), in_specs=[pl.BlockSpec(m...  31.4 us
    ppermute x23, waiting for transfers between devices, swap(): return lax.ppermute(x, AXES, [(d, d ^ mask) for d in range(devices)])  24.1 us
    ppermute x23, starting transfers between devices, swap(): return lax.ppermute(x, AXES, [(d, d ^ mask) for d in range(devices)])  18.7 us
  transfers between devices with their start and end apart: 23, of which 10 were waited for; matrix products, arithmetic and copies ran while one was open for 0% of the time, Pallas kernels for 37%

profile of v8, /device:TPU:0, one launch (start us, length us, event | category | flops | bytes accessed | tf_op | source)
XLA Modules:
  0.0 75.1 jit_solution(17742300299647549080)
XLA Ops:
  0.6 1.8 %shard_map.85 = (s32[1,512]{1,0:T(1,128)S(1)}, bf16[208,256]{1,0:T(8,128)(2,1)S(1)}, bf16[208,256]{1,0:T(8,128)(2,1)S(1)}, bf16[208,256]{1,0:T(8,128)(2,1)S(1)},...) custom-call(s32[1]{0:T(128)} %bitcast.me_ref, ...), custom_call_target="tpu_custom_call" | custom-call | flops 2000000000 | bytes 1048576 | tf_op jit(solution)/shard_map/pallas_call | solution.py:32
  2.9 2.6 %collective-permute-start.1 = (bf16[208,256]{1,0:T(8,128)(2,1)S(1)}, bf16[208,256]{1,0:T(8,128)(2,1)S(1)}, u32[]{:S(2)}, u32[]{:S(2)}) collective-permute-start(bf16[208,256]{1,0:T(8,128)(2,1)S(1)} %get-tuple-element.52), channel_id=1, source_target_pairs={{0,2},{1,3},{2,0},{3,1},{4,6},{5,7},{6,4},{7,5},{8,10},{9,11},{10,... | collective-permute-start | bytes 319496 | tf_op jit(solution)/shard_map/ppermute | solution.py:348
  5.6 12.2 %shard_map.86 = (bf16[512,256]{1,0:T(8,128)(2,1)S(1)}, bf16[4,128,256]{2,1,0:T(8,128)(2,1)S(1)}, bf16[4,128,256]{2,1,0:T(8,128)(2,1)S(1)}, bf16[192,256]{1,0:T(8...) custom-call(s32[1]{0:T(128)} %bitcast.2.me_ref, ...), custom_call_target="tpu_custom_call" | custom-call | flops 16000000000 | bytes 1048576 | tf_op jit(solution)/shard_map/pallas_call | solution.py:32
  18.0 1.9 %collective-permute-start.4 = (bf16[192,256]{1,0:T(8,128)(2,1)S(1)}, bf16[192,256]{1,0:T(8,128)(2,1)S(1)}, u32[]{:S(2)}, u32[]{:S(2)}) collective-permute-start(bf16[192,256]{1,0:T(8,128)(2,1)S(1)} %get-tuple-element.63), channel_id=1, source_target_pairs={{0,2},{1,3},{2,0},{3,1},{4,6},{5,7},{6,4},{7,5},{8,10},{9,11},{10,... | collective-permute-start | bytes 294920 | tf_op jit(solution)/shard_map/ppermute | solution.py:348
  20.2 6.7 %shard_map.87 = (bf16[512,768]{1,0:T(8,128)(2,1)S(1)}, bf16[256,512]{1,0:T(8,128)(2,1)S(1)}, bf16[768,512]{1,0:T(8,128)(2,1)S(1)}, bf16[16,512,512]{2,1,0:T(8,12...) custom-call(s32[1]{0:T(128)} %bitcast.me_ref, ...), custom_call_target="tpu_custom_call" | custom-call | flops 7000000000 | bytes 1048576 | tf_op jit(solution)/shard_map/pallas_call | solution.py:32
  26.9 6.9 %shard_map.88 = (bf16[768,512]{1,0:T(8,128)(2,1)S(1)}, bf16[4,128,256]{2,1,0:T(8,128)(2,1)S(1)}, bf16[4,128,256]{2,1,0:T(8,128)(2,1)S(1)}) custom-call(s32[1]{0:T(128)} %bitcast.2.me_ref, bf16[2,256,256]{2,1,0:T(8,128)(2,1)S(1)} %get-tuple-element.48.out_ref, bf16[512,768]{1,0:T(8,128)(2,1)S(1)} %get-tuple-element.54.place_ref, ...), custom_call_target="tpu_custom_call" | custom-call | flops 8999999488 | bytes 1048576 | tf_op jit(solution)/shard_map/pallas_call | solution.py:32
  34.2 1.2 %collective-permute-done.6.rest_1_ = bf16[4,128,256]{2,1,0:T(8,128)(2,1)S(1)} collective-permute-done((bf16[4,128,256]{2,1,0:T(8,128)(2,1)S(1)}, bf16[4,128,256]{2,1,0:T(8,128)(2,1)S(1)}, u32[]{:S(2)}, u32[]{:S(2)}) %collective-permute-start.6) | collective-permute-done | bytes 262176 | tf_op jit(solution)/shard_map/ppermute | solution.py:348
  35.5 2.0 %collective-permute-start.8 = (bf16[1,256,256]{2,1,0:T(8,128)(2,1)S(1)}, bf16[1,256,256]{2,1,0:T(8,128)(2,1)S(1)}, u32[]{:S(2)}, u32[]{:S(2)}) collective-permute-start(bf16[1,256,256]{2,1,0:T(8,128)(2,1)S(1)} %get-tuple-element.70), channel_id=1, source_target_pairs={{0,2},{1,3},{2,0},{3,1},{4,6},{5,7},{6,4},{7,5},{8,10},{9,11},{10,... | collective-permute-start | bytes 393224 | tf_op jit(solution)/shard_map/ppermute | solution.py:348
  37.5 1.5 %collective-permute-start.9 = (bf16[1,256,256]{2,1,0:T(8,128)(2,1)S(1)}, bf16[1,256,256]{2,1,0:T(8,128)(2,1)S(1)}, u32[]{:S(2)}, u32[]{:S(2)}) collective-permute-start(bf16[1,256,256]{2,1,0:T(8,128)(2,1)S(1)} %get-tuple-element.71), channel_id=1, source_target_pairs={{0,4},{1,5},{2,6},{3,7},{4,0},{5,1},{6,2},{7,3},{8,12},{9,13},{10,... | collective-permute-start | bytes 393224 | tf_op jit(solution)/shard_map/ppermute | solution.py:348
  39.1 2.4 %collective-permute-done.8.rest_1_ = bf16[1,256,256]{2,1,0:T(8,128)(2,1)S(1)} collective-permute-done((bf16[1,256,256]{2,1,0:T(8,128)(2,1)S(1)}, bf16[1,256,256]{2,1,0:T(8,128)(2,1)S(1)}, u32[]{:S(2)}, u32[]{:S(2)}) %collective-permute-start.8) | collective-permute-done | bytes 131104 | tf_op jit(solution)/shard_map/ppermute | solution.py:348
  41.5 4.1 %collective-permute-done.9.rest_2_ = bf16[1,256,256]{2,1,0:T(8,128)(2,1)S(1)} collective-permute-done((bf16[1,256,256]{2,1,0:T(8,128)(2,1)S(1)}, bf16[1,256,256]{2,1,0:T(8,128)(2,1)S(1)}, u32[]{:S(2)}, u32[]{:S(2)}) %collective-permute-start.9) | collective-permute-done | bytes 131104 | tf_op jit(solution)/shard_map/ppermute | solution.py:348
  45.7 2.7 %collective-permute-start.11 = (bf16[1,256,256]{2,1,0:T(8,128)(2,1)S(1)}, bf16[1,256,256]{2,1,0:T(8,128)(2,1)S(1)}, u32[]{:S(2)}, u32[]{:S(2)}) collective-permute-start(bf16[1,256,256]{2,1,0:T(8,128)(2,1)S(1)} %shard_map.90.rest_0_), channel_id=1, source_target_pairs={{0,16},{1,17},{2,18},{3,19},{4,20},{5,21},{6,22},{7,23},{8,24},{9,... | collective-permute-start | bytes 393224 | tf_op jit(solution)/shard_map/ppermute | solution.py:348
  48.3 5.4 %collective-permute-done.11.rest_1_ = bf16[1,256,256]{2,1,0:T(8,128)(2,1)S(1)} collective-permute-done((bf16[1,256,256]{2,1,0:T(8,128)(2,1)S(1)}, bf16[1,256,256]{2,1,0:T(8,128)(2,1)S(1)}, u32[]{:S(2)}, u32[]{:S(2)}) %collective-permute-start.11) | collective-permute-done | bytes 131104 | tf_op jit(solution)/shard_map/ppermute | solution.py:348
  54.5 0.8 %shard_map.93 = (bf16[192,256]{1,0:T(8,128)(2,1)S(1)}, bf16[192,256]{1,0:T(8,128)(2,1)S(1)}, bf16[192,256]{1,0:T(8,128)(2,1)S(1)}, bf16[192,256]{1,0:T(8,128)(2,1)S(1)}) custom-call(s32[1]{0:T(128)} %bitcast.me_ref, bf16[2,256,768]{2,1,0:T(8,128)(2,1)S(1)} %get-tuple-element.47.qkv_ref, bf16[768,512]{1,0:T(8,128)(2,1)S(1)} %get-tuple-element.73.delta, ...), custom_call_target="tpu_custom_call" | custom-call | flops 2000000000 | bytes 1048576 | tf_op jit(solution)/shard_map/pallas_call | solution.py:32
  55.4 1.7 %collective-permute-start.14 = (bf16[192,256]{1,0:T(8,128)(2,1)S(1)}, bf16[192,256]{1,0:T(8,128)(2,1)S(1)}, u32[]{:S(2)}, u32[]{:S(2)}) collective-permute-start(bf16[192,256]{1,0:T(8,128)(2,1)S(1)} %get-tuple-element.76), channel_id=1, source_target_pairs={{0,2},{1,3},{2,0},{3,1},{4,6},{5,7},{6,4},{7,5},{8,10},{9,11},{10,... | collective-permute-start | bytes 294920 | tf_op jit(solution)/shard_map/ppermute | solution.py:348
  57.3 1.5 %collective-permute-done.12.rest_1_ = bf16[1,256,256]{2,1,0:T(8,128)(2,1)S(1)} collective-permute-done((bf16[1,256,256]{2,1,0:T(8,128)(2,1)S(1)}, bf16[1,256,256]{2,1,0:T(8,128)(2,1)S(1)}, u32[]{:S(2)}, u32[]{:S(2)}) %collective-permute-start.12) | collective-permute-done | bytes 131104 | tf_op jit(solution)/shard_map/ppermute | solution.py:348
  58.8 2.3 %collective-permute-done.14.rest_2_ = bf16[192,256]{1,0:T(8,128)(2,1)S(1)} collective-permute-done((bf16[192,256]{1,0:T(8,128)(2,1)S(1)}, bf16[192,256]{1,0:T(8,128)(2,1)S(1)}, u32[]{:S(2)}, u32[]{:S(2)}) %collective-permute-start.14) | collective-permute-done | bytes 98336 | tf_op jit(solution)/shard_map/ppermute | solution.py:348
  61.1 1.2 %collective-permute-done.15.rest_3_ = bf16[192,256]{1,0:T(8,128)(2,1)S(1)} collective-permute-done((bf16[192,256]{1,0:T(8,128)(2,1)S(1)}, bf16[192,256]{1,0:T(8,128)(2,1)S(1)}, u32[]{:S(2)}, u32[]{:S(2)}) %collective-permute-start.15) | collective-permute-done | bytes 98336 | tf_op jit(solution)/shard_map/ppermute | solution.py:348
  62.3 1.7 %collective-permute-start.18 = (bf16[1,256,256]{2,1,0:T(8,128)(2,1)S(1)}, bf16[1,256,256]{2,1,0:T(8,128)(2,1)S(1)}, u32[]{:S(2)}, u32[]{:S(2)}) collective-permute-start(bf16[1,256,256]{2,1,0:T(8,128)(2,1)S(1)} %shard_map.92.rest_0_), channel_id=1, source_target_pairs={{0,6},{1,7},{2,4},{3,5},{4,2},{5,3},{6,0},{7,1},{8,14},{9,15},{10,... | collective-permute-start | bytes 393224 | tf_op jit(solution)/shard_map/ppermute | solution.py:348
  63.9 1.4 %collective-permute-start.17 = (bf16[1,256,256]{2,1,0:T(8,128)(2,1)S(1)}, bf16[1,256,256]{2,1,0:T(8,128)(2,1)S(1)}, u32[]{:S(2)}, u32[]{:S(2)}) collective-permute-start(bf16[1,256,256]{2,1,0:T(8,128)(2,1)S(1)} %shard_map.92.rest_0_), channel_id=1, source_target_pairs={{0,4},{1,5},{2,6},{3,7},{4,0},{5,1},{6,2},{7,3},{8,12},{9,13},{10,... | collective-permute-start | bytes 393224 | tf_op jit(solution)/shard_map/ppermute | solution.py:348
  65.8 3.8 %collective-permute-done.18.rest_3_ = bf16[1,256,256]{2,1,0:T(8,128)(2,1)S(1)} collective-permute-done((bf16[1,256,256]{2,1,0:T(8,128)(2,1)S(1)}, bf16[1,256,256]{2,1,0:T(8,128)(2,1)S(1)}, u32[]{:S(2)}, u32[]{:S(2)}) %collective-permute-start.18) | collective-permute-done | bytes 131104 | tf_op jit(solution)/shard_map/ppermute | solution.py:348
  69.5 2.1 %collective-permute-done.17.rest_2_ = bf16[1,256,256]{2,1,0:T(8,128)(2,1)S(1)} collective-permute-done((bf16[1,256,256]{2,1,0:T(8,128)(2,1)S(1)}, bf16[1,256,256]{2,1,0:T(8,128)(2,1)S(1)}, u32[]{:S(2)}, u32[]{:S(2)}) %collective-permute-start.17) | collective-permute-done | bytes 131104 | tf_op jit(solution)/shard_map/ppermute | solution.py:348
  72.2 1.2 %shard_map.94 = bf16[512,256]{1,0:T(8,128)(2,1)} custom-call(s32[1]{0:T(128)} %bitcast.me_ref, s32[1,512]{1,0:T(1,128)S(1)} %get-tuple-element.44.slots_ref, bf16[512,256]{1,0:T(8,128)(2,1)S(1)} %get-tuple-element.49.mid_ref, bf16[192,256]{1,0:T(8,128)(2,1)S(1)} %get-tuple-element.78.rest_0_, bf16[192,256]{1,0:T(8,128)(2,1)S(1)} %collective-permute-done.13.rest_1_, ...), custom_call_target="tpu_custom_call" | custom-call | flops 1000000000 | bytes 1048576 | tf_op jit(solution)/shard_map/pallas_call | solution.py:32
  73.4 1.5 %shard_map.95 = (f32[2,256,768]{2,1,0:T(8,128)}, f32[2,256,256]{2,1,0:T(8,128)}) custom-call(s32[1]{0:T(128)} %bitcast.2.me_ref, bf16[1,256,256]{2,1,0:T(8,128)(2,1)S(1)} %shard_map.92.rest_0_, bf16[1,256,256]{2,1,0:T(8,128)(2,1)S(1)} %collective-permute-done.16.rest_1_, bf16[1,256,256]{2,1,0:T(8,128)(2,1)S(1)} %collective-permute-done.17.rest_2_, ...), custom_call_target="tpu_custom_call" | custom-call | flops 1000000000 | bytes 1048576 | tf_op jit(solution)/shard_map/pallas_call | solution.py:32
  (33 shorter events, 3.7 us)
Async XLA Ops:
  2.4 17.5 %collective-permute-start = (bf16[208,256]{1,0:T(8,128)(2,1)S(1)}, bf16[208,256]{1,0:T(8,128)(2,1)S(1)}, u32[]{:S(2)}, u32[]{:S(2)}) collective-permute-start(bf16[208,256]{1,0:T(8,128)(2,1)S(1)} %get-tuple-element.51), channel_id=1, source_target_pairs={{0,1},{1,0},{2,3},{3,2},{4,5},{5,4},{6,7},{7,6},{8,9},{9,8},{10,11... | collective-permute-start | bytes 319496 | tf_op jit(solution)/shard_map/ppermute | solution.py:348
  2.9 17.0 %collective-permute-start.1 = (bf16[208,256]{1,0:T(8,128)(2,1)S(1)}, bf16[208,256]{1,0:T(8,128)(2,1)S(1)}, u32[]{:S(2)}, u32[]{:S(2)}) collective-permute-start(bf16[208,256]{1,0:T(8,128)(2,1)S(1)} %get-tuple-element.52), channel_id=1, source_target_pairs={{0,2},{1,3},{2,0},{3,1},{4,6},{5,7},{6,4},{7,5},{8,10},{9,11},{10,... | collective-permute-start | bytes 319496 | tf_op jit(solution)/shard_map/ppermute | solution.py:348
  5.5 14.7 %collective-permute-start.2 = (bf16[208,256]{1,0:T(8,128)(2,1)S(1)}, bf16[208,256]{1,0:T(8,128)(2,1)S(1)}, u32[]{:S(2)}, u32[]{:S(2)}) collective-permute-start(bf16[208,256]{1,0:T(8,128)(2,1)S(1)} %get-tuple-element.53), channel_id=1, source_target_pairs={{0,3},{1,2},{2,1},{3,0},{4,7},{5,6},{6,5},{7,4},{8,11},{9,10},{10,... | collective-permute-start | bytes 319496 | tf_op jit(solution)/shard_map/ppermute | solution.py:348
  17.8 9.1 %collective-permute-start.3 = (bf16[192,256]{1,0:T(8,128)(2,1)S(1)}, bf16[192,256]{1,0:T(8,128)(2,1)S(1)}, u32[]{:S(2)}, u32[]{:S(2)}) collective-permute-start(bf16[192,256]{1,0:T(8,128)(2,1)S(1)} %get-tuple-element.62), channel_id=1, source_target_pairs={{0,1},{1,0},{2,3},{3,2},{4,5},{5,4},{6,7},{7,6},{8,9},{9,8},{10,11... | collective-permute-start | bytes 294920 | tf_op jit(solution)/shard_map/ppermute | solution.py:348
  18.0 8.9 %collective-permute-start.4 = (bf16[192,256]{1,0:T(8,128)(2,1)S(1)}, bf16[192,256]{1,0:T(8,128)(2,1)S(1)}, u32[]{:S(2)}, u32[]{:S(2)}) collective-permute-start(bf16[192,256]{1,0:T(8,128)(2,1)S(1)} %get-tuple-element.63), channel_id=1, source_target_pairs={{0,2},{1,3},{2,0},{3,1},{4,6},{5,7},{6,4},{7,5},{8,10},{9,11},{10,... | collective-permute-start | bytes 294920 | tf_op jit(solution)/shard_map/ppermute | solution.py:348
  19.9 7.0 %collective-permute-start.5 = (bf16[192,256]{1,0:T(8,128)(2,1)S(1)}, bf16[192,256]{1,0:T(8,128)(2,1)S(1)}, u32[]{:S(2)}, u32[]{:S(2)}) collective-permute-start(bf16[192,256]{1,0:T(8,128)(2,1)S(1)} %get-tuple-element.64), channel_id=1, source_target_pairs={{0,3},{1,2},{2,1},{3,0},{4,7},{5,6},{6,5},{7,4},{8,11},{9,10},{10,... | collective-permute-start | bytes 294920 | tf_op jit(solution)/shard_map/ppermute | solution.py:348
  19.9 14.3 %collective-permute-start.7 = (bf16[4,128,256]{2,1,0:T(8,128)(2,1)S(1)}, bf16[4,128,256]{2,1,0:T(8,128)(2,1)S(1)}, u32[]{:S(2)}, u32[]{:S(2)}) collective-permute-start(bf16[4,128,256]{2,1,0:T(8,128)(2,1)S(1)} %get-tuple-element.68), channel_id=1, source_target_pairs={{0,1},{1,0},{2,3},{3,2},{4,5},{5,4},{6,7},{7,6},{8,9},{9,8},{10,11... | collective-permute-start | bytes 786440 | tf_op jit(solution)/shard_map/ppermute | solution.py:348
  33.8 1.6 %collective-permute-start.6 = (bf16[4,128,256]{2,1,0:T(8,128)(2,1)S(1)}, bf16[4,128,256]{2,1,0:T(8,128)(2,1)S(1)}, u32[]{:S(2)}, u32[]{:S(2)}) collective-permute-start(bf16[4,128,256]{2,1,0:T(8,128)(2,1)S(1)} %get-tuple-element.66), channel_id=1, source_target_pairs={{0,1},{1,0},{2,3},{3,2},{4,5},{5,4},{6,7},{7,6},{8,9},{9,8},{10,11... | collective-permute-start | bytes 786440 | tf_op jit(solution)/shard_map/ppermute | solution.py:348
  35.5 5.9 %collective-permute-start.8 = (bf16[1,256,256]{2,1,0:T(8,128)(2,1)S(1)}, bf16[1,256,256]{2,1,0:T(8,128)(2,1)S(1)}, u32[]{:S(2)}, u32[]{:S(2)}) collective-permute-start(bf16[1,256,256]{2,1,0:T(8,128)(2,1)S(1)} %get-tuple-element.70), channel_id=1, source_target_pairs={{0,2},{1,3},{2,0},{3,1},{4,6},{5,7},{6,4},{7,5},{8,10},{9,11},{10,... | collective-permute-start | bytes 393224 | tf_op jit(solution)/shard_map/ppermute | solution.py:348
  37.5 8.1 %collective-permute-start.9 = (bf16[1,256,256]{2,1,0:T(8,128)(2,1)S(1)}, bf16[1,256,256]{2,1,0:T(8,128)(2,1)S(1)}, u32[]{:S(2)}, u32[]{:S(2)}) collective-permute-start(bf16[1,256,256]{2,1,0:T(8,128)(2,1)S(1)} %get-tuple-element.71), channel_id=1, source_target_pairs={{0,4},{1,5},{2,6},{3,7},{4,0},{5,1},{6,2},{7,3},{8,12},{9,13},{10,... | collective-permute-start | bytes 393224 | tf_op jit(solution)/shard_map/ppermute | solution.py:348
  39.0 6.5 %collective-permute-start.10 = (bf16[1,256,256]{2,1,0:T(8,128)(2,1)S(1)}, bf16[1,256,256]{2,1,0:T(8,128)(2,1)S(1)}, u32[]{:S(2)}, u32[]{:S(2)}) collective-permute-start(bf16[1,256,256]{2,1,0:T(8,128)(2,1)S(1)} %get-tuple-element.72), channel_id=1, source_target_pairs={{0,6},{1,7},{2,4},{3,5},{4,2},{5,3},{6,0},{7,1},{8,14},{9,15},{10,... | collective-permute-start | bytes 393224 | tf_op jit(solution)/shard_map/ppermute | solution.py:348
  45.7 8.0 %collective-permute-start.11 = (bf16[1,256,256]{2,1,0:T(8,128)(2,1)S(1)}, bf16[1,256,256]{2,1,0:T(8,128)(2,1)S(1)}, u32[]{:S(2)}, u32[]{:S(2)}) collective-permute-start(bf16[1,256,256]{2,1,0:T(8,128)(2,1)S(1)} %shard_map.90.rest_0_), channel_id=1, source_target_pairs={{0,16},{1,17},{2,18},{3,19},{4,20},{5,21},{6,22},{7,23},{8,24},{9,... | collective-permute-start | bytes 393224 | tf_op jit(solution)/shard_map/ppermute | solution.py:348
  53.7 5.0 %collective-permute-start.12 = (bf16[1,256,256]{2,1,0:T(8,128)(2,1)S(1)}, bf16[1,256,256]{2,1,0:T(8,128)(2,1)S(1)}, u32[]{:S(2)}, u32[]{:S(2)}) collective-permute-start(bf16[1,256,256]{2,1,0:T(8,128)(2,1)S(1)} %shard_map.91.rest_0_), channel_id=1, source_target_pairs={{0,8},{1,9},{2,10},{3,11},{4,12},{5,13},{6,14},{7,15},{8,0},{9,1},... | collective-permute-start | bytes 393224 | tf_op jit(solution)/shard_map/ppermute | solution.py:348
  55.3 3.5 %collective-permute-start.13 = (bf16[192,256]{1,0:T(8,128)(2,1)S(1)}, bf16[192,256]{1,0:T(8,128)(2,1)S(1)}, u32[]{:S(2)}, u32[]{:S(2)}) collective-permute-start(bf16[192,256]{1,0:T(8,128)(2,1)S(1)} %get-tuple-element.75), channel_id=1, source_target_pairs={{0,1},{1,0},{2,3},{3,2},{4,5},{5,4},{6,7},{7,6},{8,9},{9,8},{10,11... | collective-permute-start | bytes 294920 | tf_op jit(solution)/shard_map/ppermute | solution.py:348
  55.4 5.7 %collective-permute-start.14 = (bf16[192,256]{1,0:T(8,128)(2,1)S(1)}, bf16[192,256]{1,0:T(8,128)(2,1)S(1)}, u32[]{:S(2)}, u32[]{:S(2)}) collective-permute-start(bf16[192,256]{1,0:T(8,128)(2,1)S(1)} %get-tuple-element.76), channel_id=1, source_target_pairs={{0,2},{1,3},{2,0},{3,1},{4,6},{5,7},{6,4},{7,5},{8,10},{9,11},{10,... | collective-permute-start | bytes 294920 | tf_op jit(solution)/shard_map/ppermute | solution.py:348
  57.1 5.2 %collective-permute-start.15 = (bf16[192,256]{1,0:T(8,128)(2,1)S(1)}, bf16[192,256]{1,0:T(8,128)(2,1)S(1)}, u32[]{:S(2)}, u32[]{:S(2)}) collective-permute-start(bf16[192,256]{1,0:T(8,128)(2,1)S(1)} %get-tuple-element.77), channel_id=1, source_target_pairs={{0,3},{1,2},{2,1},{3,0},{4,7},{5,6},{6,5},{7,4},{8,11},{9,10},{10,... | collective-permute-start | bytes 294920 | tf_op jit(solution)/shard_map/ppermute | solution.py:348
  62.3 7.2 %collective-permute-start.18 = (bf16[1,256,256]{2,1,0:T(8,128)(2,1)S(1)}, bf16[1,256,256]{2,1,0:T(8,128)(2,1)S(1)}, u32[]{:S(2)}, u32[]{:S(2)}) collective-permute-start(bf16[1,256,256]{2,1,0:T(8,128)(2,1)S(1)} %shard_map.92.rest_0_), channel_id=1, source_target_pairs={{0,6},{1,7},{2,4},{3,5},{4,2},{5,3},{6,0},{7,1},{8,14},{9,15},{10,... | collective-permute-start | bytes 393224 | tf_op jit(solution)/shard_map/ppermute | solution.py:348
  63.9 7.7 %collective-permute-start.17 = (bf16[1,256,256]{2,1,0:T(8,128)(2,1)S(1)}, bf16[1,256,256]{2,1,0:T(8,128)(2,1)S(1)}, u32[]{:S(2)}, u32[]{:S(2)}) collective-permute-start(bf16[1,256,256]{2,1,0:T(8,128)(2,1)S(1)} %shard_map.92.rest_0_), channel_id=1, source_target_pairs={{0,4},{1,5},{2,6},{3,7},{4,0},{5,1},{6,2},{7,3},{8,12},{9,13},{10,... | collective-permute-start | bytes 393224 | tf_op jit(solution)/shard_map/ppermute | solution.py:348
  65.4 6.5 %collective-permute-start.16 = (bf16[1,256,256]{2,1,0:T(8,128)(2,1)S(1)}, bf16[1,256,256]{2,1,0:T(8,128)(2,1)S(1)}, u32[]{:S(2)}, u32[]{:S(2)}) collective-permute-start(bf16[1,256,256]{2,1,0:T(8,128)(2,1)S(1)} %shard_map.92.rest_0_), channel_id=1, source_target_pairs={{0,2},{1,3},{2,0},{3,1},{4,6},{5,7},{6,4},{7,5},{8,10},{9,11},{10,... | collective-permute-start | bytes 393224 | tf_op jit(solution)/shard_map/ppermute | solution.py:348
  65.8 7.6 %collective-permute-start.19 = (bf16[1,256,256]{2,1,0:T(8,128)(2,1)S(1)}, bf16[1,256,256]{2,1,0:T(8,128)(2,1)S(1)}, u32[]{:S(2)}, u32[]{:S(2)}) collective-permute-start(bf16[1,256,256]{2,1,0:T(8,128)(2,1)S(1)} %shard_map.92.rest_0_), channel_id=1, source_target_pairs={{0,1},{1,0},{2,3},{3,2},{4,5},{5,4},{6,7},{7,6},{8,9},{9,8},{10,11... | collective-permute-start | bytes 393224 | tf_op jit(solution)/shard_map/ppermute | solution.py:348
  69.5 3.9 %collective-permute-start.22 = (bf16[1,256,256]{2,1,0:T(8,128)(2,1)S(1)}, bf16[1,256,256]{2,1,0:T(8,128)(2,1)S(1)}, u32[]{:S(2)}, u32[]{:S(2)}) collective-permute-start(bf16[1,256,256]{2,1,0:T(8,128)(2,1)S(1)} %collective-permute-done.18.rest_3_), channel_id=1, source_target_pairs={{0,1},{1,0},{2,3},{3,2},{4,5},{5,4},{6,7},{7,6},{8,9},{9,8},{10,11... | collective-permute-start | bytes 393224 | tf_op jit(solution)/shard_map/ppermute | solution.py:348
  71.6 1.7 %collective-permute-start.21 = (bf16[1,256,256]{2,1,0:T(8,128)(2,1)S(1)}, bf16[1,256,256]{2,1,0:T(8,128)(2,1)S(1)}, u32[]{:S(2)}, u32[]{:S(2)}) collective-permute-start(bf16[1,256,256]{2,1,0:T(8,128)(2,1)S(1)} %collective-permute-done.17.rest_2_), channel_id=1, source_target_pairs={{0,1},{1,0},{2,3},{3,2},{4,5},{5,4},{6,7},{7,6},{8,9},{9,8},{10,11... | collective-permute-start | bytes 393224 | tf_op jit(solution)/shard_map/ppermute | solution.py:348
  71.8 1.6 %collective-permute-start.20 = (bf16[1,256,256]{2,1,0:T(8,128)(2,1)S(1)}, bf16[1,256,256]{2,1,0:T(8,128)(2,1)S(1)}, u32[]{:S(2)}, u32[]{:S(2)}) collective-permute-start(bf16[1,256,256]{2,1,0:T(8,128)(2,1)S(1)} %collective-permute-done.16.rest_1_), channel_id=1, source_target_pairs={{0,1},{1,0},{2,3},{3,2},{4,5},{5,4},{6,7},{7,6},{8,9},{9,8},{10,11... | collective-permute-start | bytes 393224 | tf_op jit(solution)/shard_map/ppermute | solution.py:348
